TPU v7x, 256 devices: a whole 4x4x8 slice. The times are simulated.
256 devices in a mesh: row: 8 (over z_lo, y), col: 32 (over z_hi, x, core).
Axes of the slice: x: 4, y: 4, z: 8 (z_hi: 4, z_lo: 2; z = z_hi * 2 + z_lo), core: 2. Of those that a mesh axis runs over, the one named last changes fastest.
Arguments:
- image: bfloat16 [128, 768, 768], P('row', 'col'), may hold values from -6 to 6
- conv_weight: float32 [7, 7, 768], replicated, may hold values from -0.875 to 0.875
- conv_bias: float32 [768], replicated, may hold values from -3 to 3
- layernorm_gain: float32 [768], replicated, may hold values from 0.5 to 1.5
- layernorm_bias: float32 [768], replicated, may hold values from -2 to 2
- w_expand: bfloat16 [3072, 768], replicated, may hold values from -0.21875 to 0.21875
- b_expand: float32 [3072], replicated, may hold values from -3 to 3
- w_reduce: bfloat16 [768, 3072], replicated, may hold values from -0.109375 to 0.109375
- b_reduce: float32 [768], replicated, may hold values from -3 to 3
- layer_scale: float32 [768], replicated, may hold values from 0.2 to 1.5
- cotangent: bfloat16 [128, 768, 768], P('row', 'col'), may hold values from -6 to 6
Outputs:
- grad_image: float32 [128, 768, 768], P('row', 'col')
- grad_expand: float32 [3072, 768], P(('row', 'col'))
- grad_reduce: float32 [768, 3072], P(None, ('row', 'col'))
- grad_conv_weight: float32 [7, 7, 768], replicated
- grad_conv_bias: float32 [768], replicated
- grad_ln_gain: float32 [768], replicated
- grad_ln_bias: float32 [768], replicated
- grad_b_expand: float32 [3072], replicated
- grad_b_reduce: float32 [768], replicated
- grad_layer_scale: float32 [768], replicated
All inputs are finite; a program needn't handle non-finite values.
Results may differ from a plain program's by a relative error of at most 0.0075.
Values may be sent and summed in bfloat16 or wider, within the bound.
No kernel may reach another device: no remote copies, remote signals or barrier semaphores. Data moves between devices by JAX's collectives and lax.ppermute only.
A program may use at most 128 MiB of HBM per device.

v0:
```python
import functools
import itertools
import math

import jax
import jax.numpy as jnp
from jax import lax
from jax.experimental import pallas as pl
from jax.experimental.pallas import tpu as pltpu
from jax.sharding import Mesh
from jax.sharding import PartitionSpec as P

KS = 7
AXES = ("zl", "y", "zh", "x", "c")
SIZES = (2, 4, 4, 4, 2)
ROW = ("zl", "y")
COL = ("zh", "x", "c")
BF = jnp.bfloat16
F32 = jnp.float32


def spot_z(z):
    return (z % 2) * 4 + z // 2


def core_pairs(k, lead):
    pairs = []
    for spot in itertools.product(*(range(n) for n in SIZES)):
        to = list(spot)
        at = AXES.index(lead[spot[-1]])
        to[at] = (to[at] + k) % SIZES[at]
        pairs.append((flat_index(spot), flat_index(to)))
    return pairs


def flat_index(spot):
    out = 0
    for i, n in zip(spot, SIZES):
        out = out * n + i
    return out


def split_send(v, small, lead, dims):
    core = lax.axis_index("c")
    me = [lax.axis_index(name) for name in lead]
    chans = v.shape[-1]

    def pick(k):
        parts = [
            lax.dynamic_index_in_dim(v, lax.rem(me[s] + k, 4), dims[s], keepdims=False).reshape(
                -1, chans
            )
            for s in range(2)
        ]
        return jnp.where(core == 0, parts[0], parts[1])

    low = small.astype(BF)
    return [jnp.concatenate([low, pick(k)], axis=0) for k in range(4)]


def split_move(moved, lead):
    return [lax.ppermute(moved[k], AXES, core_pairs(k, lead)) for k in range(1, 4)]


def split_add(moved, got, count):
    def add(part):
        out = part(moved[0]).astype(F32)
        for v in got:
            out = out + part(v).astype(F32)
        return out

    return add(lambda v: v[count:]), add(lambda v: v[:count])


def z_sum(v, small):
    count = small.shape[0]
    low = small.astype(BF)
    zl = lax.axis_index("zl")
    zh = lax.axis_index("zh")
    acc = lax.dynamic_index_in_dim(v, zl, 0, False)
    acc = lax.dynamic_index_in_dim(acc, zh, 0, False).astype(F32)
    sums = low.astype(F32)
    z = zh * 2 + zl
    for k in range(1, 8):
        to = lax.rem(z + k, 8)
        part = lax.dynamic_index_in_dim(v, lax.rem(to, 2), 0, False)
        part = lax.dynamic_index_in_dim(part, to // 2, 0, False)
        sent = jnp.concatenate([low, part], axis=0)
        pairs = [(spot_z(i), spot_z((i + k) % 8)) for i in range(8)]
        got = lax.ppermute(sent, ("zl", "zh"), pairs)
        sums = sums + got[:count].astype(F32)
        acc = acc + got[count:].astype(F32)
    return acc, sums


def core_swap(v):
    return lax.ppermute(v, "c", [(0, 1), (1, 0)])


def with_halo(x, w):
    rows, cols, _ = x.shape

    def shift(v, axes, d):
        n = lax.axis_size(axes)
        return lax.ppermute(v, axes, [(i, i + d) for i in range(n) if 0 <= i + d < n])

    west = shift(x[:, cols - w :], COL, 1)
    east = shift(x[:, :w], COL, -1)
    x = jnp.concatenate([west, x, east], axis=1)
    north = shift(x[rows - w :], ROW, 1)
    south = shift(x[:w], ROW, -1)
    return jnp.concatenate([north, x, south], axis=0)


def gelu_pair(pre):
    root = pre / math.sqrt(2.0)
    cdf = 0.5 * (1.0 + lax.erf(root))
    return (pre * cdf, cdf + pre * jnp.exp(-0.5 * pre * pre) / math.sqrt(2.0 * math.pi))


def tdot(a, b):
    return lax.dot_general(a, b, (((0,), (0,)), ((), ())), preferred_element_type=F32)


def backward_kernel(
    scale, pad_ref, conv_ref, dn_ref, br_ref, cot_ref, pre_ref, par_ref, small_ref, out_ref, im, dd, acc
):
    rows, cols, chans = conv_ref.shape
    lanes = 128
    blocks = chans // lanes
    high, wide, _ = pad_ref.shape
    gain = par_ref[0:1, :]
    bias = par_ref[1:2, :]
    layer = par_ref[2:3, :]
    acc[...] = jnp.zeros_like(acc)

    def spread(r, _):
        row = pad_ref[r].astype(F32)
        for b in range(blocks):
            im[b, r, 0:wide, :] = row[:, b * lanes : (b + 1) * lanes]
        return 0

    lax.fori_loop(0, high, spread, 0)

    def fold(v):
        out = v[0:8]
        for t in range(8, cols, 8):
            out = out + v[t : t + 8]
        return out

    def norm(r, _):
        v = conv_ref[r]
        v = v - jnp.mean(v, axis=-1, keepdims=True)
        rstd = lax.rsqrt(jnp.mean(v * v, axis=-1, keepdims=True) + 1e-06)
        xhat = v * rstd
        dn = dn_ref[r]
        dx = dn * gain
        d = (
            dx
            - jnp.mean(dx, axis=-1, keepdims=True)
            - xhat * jnp.mean(dx * xhat, axis=-1, keepdims=True)
        ) * rstd
        out_ref[r] = d.astype(BF)
        for b in range(blocks):
            dd[b, r] = d[:, b * lanes : (b + 1) * lanes]
        g = cot_ref[r].astype(F32)
        acc[0] += fold(d)
        acc[1] += fold(dn * xhat)
        acc[2] += fold(dn)
        acc[3] += fold((g * layer).astype(BF).astype(F32))
        acc[4] += fold(g * (br_ref[r] + bias))
        return 0

    lax.fori_loop(0, rows, norm, 0)
    kk = KS * KS
    for t in range(5):
        small_ref[kk + t : kk + t + 1, :] = jnp.sum(acc[t], axis=0, keepdims=True) * scale
    n_pre = pre_ref.shape[0]
    small_ref[kk + 5 : kk + 5 + n_pre, :] = pre_ref[...] * scale
    left = small_ref.shape[0] - (kk + 5 + n_pre)
    if left:
        small_ref[kk + 5 + n_pre :, :] = jnp.zeros((left, chans), F32)

    part = 8

    def taps(b, _):
        at = pl.ds(pl.multiple_of(b * lanes, lanes), lanes)
        for j in range(KS):
            total = [jnp.zeros((8, lanes), F32) for _ in range(KS)]
            for p0 in range(0, rows, part):
                size = min(part, rows - p0)
                held = [dd[b, p0 + p] for p in range(size)]
                for r in range(size + KS - 1):
                    s = im[b, p0 + r, j : j + cols, :]
                    for i in range(KS):
                        if 0 <= r - i < size:
                            total[i] = total[i] + fold(held[r - i] * s)
            for i in range(KS):
                t = KS * i + j
                small_ref[t : t + 1, at] = jnp.sum(total[i], axis=0, keepdims=True) * scale
        return 0

    lax.fori_loop(0, blocks, taps, 0)


def backward(scale, padded, conv_out, d_normed, branch, cotangent, sum_pre, params):
    rows, cols, chans = conv_out.shape
    used = KS * KS + 5 + sum_pre.shape[0]
    total = -(-used // 32) * 32
    blocks = chans // 128
    return pl.pallas_call(
        functools.partial(backward_kernel, scale),
        out_shape=(
            jax.ShapeDtypeStruct((total, chans), F32),
            jax.ShapeDtypeStruct((rows, cols, chans), BF),
        ),
        scratch_shapes=[
            pltpu.VMEM((blocks, rows + KS - 1, cols + 8, 128), F32),
            pltpu.VMEM((blocks, rows, cols, 128), F32),
            pltpu.VMEM((8, 8, chans), F32),
        ],
        compiler_params=pltpu.CompilerParams(vmem_limit_bytes=40 * 1024 * 1024),
        cost_estimate=pl.CostEstimate(
            flops=2 * KS * KS * rows * cols * chans, bytes_accessed=8 * 1024 * 1024, transcendentals=0
        ),
        name="backward",
    )(padded, conv_out, d_normed, branch, cotangent, sum_pre, params)


def on_device(
    image,
    conv_weight,
    conv_bias,
    layernorm_gain,
    layernorm_bias,
    w_expand,
    b_expand,
    w_reduce,
    b_reduce,
    layer_scale,
    cotangent,
):
    rows, cols, chans = image.shape
    hid = w_expand.shape[0]
    per = hid // 256
    scale = 1.0 / math.sqrt(rows * cols * 256)
    first = lax.axis_index("c") == 0
    padded = with_halo(image, 3)
    conv_out = jnp.zeros((rows, cols, chans), F32) + conv_bias
    for i in range(KS):
        for j in range(KS):
            conv_out = conv_out + conv_weight[i, j] * padded[i : i + rows, j : j + cols].astype(F32)
    flat = conv_out.reshape(rows * cols, chans)
    channel_mean = jnp.mean(flat, axis=-1, keepdims=True)
    centered = flat - channel_mean
    var = jnp.mean(centered * centered, axis=-1, keepdims=True)
    rstd = lax.rsqrt(var + 1e-06)
    xhat = centered * rstd
    normed = (xhat * layernorm_gain + layernorm_bias).astype(BF)
    pre = (
        lax.dot_general(normed, w_expand, (((1,), (1,)), ((), ())), preferred_element_type=F32)
        + b_expand
    )
    act, slope = gelu_pair(pre)
    hidden = act.astype(BF)
    grad_f = cotangent.reshape(rows * cols, chans).astype(F32)
    d_branch = (layer_scale * grad_f).astype(BF)
    d_hidden = jnp.dot(d_branch, w_reduce, preferred_element_type=F32)
    d_pre = (d_hidden * slope).astype(BF)

    far = tdot(jnp.where(first, hidden, d_pre), jnp.where(first, d_branch, normed)).astype(BF)
    come = core_swap(far)
    near = tdot(jnp.where(first, d_pre, hidden), jnp.where(first, normed, d_branch))
    near = lax.optimization_barrier(near)
    term = (near + come.astype(F32)).astype(BF).reshape(2, 4, 4, 4, 2 * per, chans)

    branch = lax.dot_general(
        hidden, w_reduce, (((1,), (1,)), ((), ())), preferred_element_type=F32
    )
    d_normed = jnp.dot(d_pre, w_expand, preferred_element_type=F32)
    sum_pre = jnp.sum(d_pre.astype(F32), axis=0).reshape(hid // chans, chans)
    params = jnp.stack([layernorm_gain, b_reduce, layer_scale] + [layer_scale] * 5)
    shape = (rows, cols, chans)
    small, d_conv = backward(
        scale,
        padded,
        conv_out,
        d_normed.reshape(shape),
        branch.reshape(shape),
        cotangent,
        sum_pre,
        params,
    )
    total = small.shape[0]
    lower, upper = small[: total // 2], small[total // 2 :]
    small = jnp.where(first, lower, upper) + core_swap(jnp.where(first, upper, lower))

    moved = split_send(term, small, ("x", "y"), (3, 1))
    d_pad = with_halo(d_conv, 3)
    grad_image = cotangent.astype(F32)
    for i in range(KS):
        for j in range(KS):
            grad_image = grad_image + conv_weight[i, j] * d_pad[
                6 - i : 6 - i + rows, 6 - j : 6 - j + cols
            ].astype(F32)
    got = split_move(moved, ("x", "y"))
    got, grad_image = lax.optimization_barrier((got, grad_image))
    term, small = split_add(moved, got, small.shape[0])
    term = term.astype(BF).reshape(2, 4, 4, 2 * per, chans)
    moved = split_send(term, small, ("y", "x"), (1, 2))
    term, small = split_add(moved, split_move(moved, ("y", "x")), small.shape[0])
    term = term.astype(BF).reshape(2, 4, 2 * per, chans)
    term, small = z_sum(term, small)
    term = term * scale
    top, low = term[:per], term[per:]
    got = core_swap(jnp.concatenate([small, jnp.where(first, low, top)], axis=0))
    keep = jnp.where(first, top, low)
    other, got = got[: total // 2], got[total // 2 :]
    small = jnp.concatenate(
        [jnp.where(first, small, other), jnp.where(first, other, small)], axis=0
    )
    grad_expand = jnp.where(first, keep, got)
    grad_reduce = jnp.where(first, got, keep).T

    kk = KS * KS
    return (
        grad_image,
        grad_expand,
        grad_reduce,
        small[:kk].reshape(KS, KS, chans),
        small[kk],
        small[kk + 1],
        small[kk + 2],
        small[kk + 5 : kk + 5 + hid // chans].reshape(hid),
        small[kk + 3],
        small[kk + 4],
    )


def solution(mesh):
    grid = Mesh(mesh.devices.reshape(SIZES), AXES)
    tile = P(ROW, COL, None)
    one = P()
    in_specs = (tile,) + (one,) * 9 + (tile,)
    out_specs = (tile, P(AXES, None), P(None, AXES)) + (one,) * 7
    return jax.shard_map(
        on_device, mesh=grid, in_specs=in_specs, out_specs=out_specs, check_vma=False
    )
```

profile of v0, /device:TPU:1, one launch (start us, length us, event | category | flops | bytes accessed | tf_op | source)
XLA Modules:
  0.0 199.0 jit_solution(4651616142282416556)
XLA Ops:
  1.9 5.1 %collective-permute-start.1 = (bf16[16,3,768]{2,1,0:T(4,128)(2,1)S(1)}, bf16[16,3,768]{2,1,0:T(4,128)(2,1)S(1)}, u32[]{:S(2)}, u32[]{:S(2)}) collective-permute-start(bf16[16,3,768]{2,1,0:T(4,128)(2,1)S(1)} %get-tuple-element.105), channel_id=1, source_target_pairs={{1,0},{2,1},{3,2},{4,3},{5,4},{6,5},{7,6},{8,7},{9,8},{10,9},{11,1... | collective-permute-start | bytes 221192 | tf_op jit(solution)/shard_map/ppermute | solution.py:105
  7.0 2.1 %collective-permute-start = (bf16[16,3,768]{2,1,0:T(4,128)(2,1)S(1)}, bf16[16,3,768]{2,1,0:T(4,128)(2,1)S(1)}, u32[]{:S(2)}, u32[]{:S(2)}) collective-permute-start(bf16[16,3,768]{2,1,0:T(4,128)(2,1)S(1)} %get-tuple-element.104), channel_id=1, source_target_pairs={{0,1},{1,2},{2,3},{3,4},{4,5},{5,6},{6,7},{7,8},{8,9},{9,10},{10,1... | collective-permute-start | bytes 221192 | tf_op jit(solution)/shard_map/ppermute | solution.py:105
  14.1 4.0 %collective-permute-start.2 = (bf16[3,30,768]{2,1,0:T(8,128)(2,1)S(1)}, bf16[3,30,768]{2,1,0:T(8,128)(2,1)S(1)}, u32[]{:S(2)}, u32[]{:S(2)}) collective-permute-start(bf16[3,30,768]{2,1,0:T(8,128)(2,1)S(1)} %get-tuple-element.100), channel_id=1, source_target_pairs={{0,32},{32,64},{64,96},{96,128},{128,160},{160,192},{192,224},{1,3... | collective-permute-start | bytes 414728 | tf_op jit(solution)/shard_map/ppermute | solution.py:105
  21.4 9.3 %fusion.31 = (f32[16,24]{1,0:T(8,128)S(1)}, f32[16,24,768]{2,1,0:T(8,128)S(1)}) fusion(bf16[19,30,768]{2,1,0:T(8,128)(2,1)S(1)} %get-tuple-element.99, f32[768]{0:T(1024)S(1)} %copy-done.74, f32[768]{0:T(1024)S(1)} %copy-done.76, f32[768]{0:T(1024)S(1)} %copy-done.20, f32[768]{0:T(1024)S(1)} %copy-done.22, f32[768]{0:T(1024)S(1)} %copy-done.24, ...), kind=kLoop, calls=%fused_computation.184 | loop fusion | flops 46300800 | bytes 28540416 | tf_op jit(solution)/shard_map/reduce_sum | solution.py:254
  31.8 4.8 %multiply_convert_fusion = (bf16[384,3072]{1,0:T(8,128)(2,1)S(1)}, f32[384,3072]{1,0:T(8,128)S(1)}) fusion(f32[3072]{0:T(1024)S(1)} %copy-done.84, bf16[384,768]{1,0:T(8,128)(2,1)S(1)} %fusion.14, bf16[3072,768]{1,0:T(8,128)(2,1)} %param.16), kind=kOutput, calls=%fused_computation.10 | convolution fusion | flops 1819017216 | bytes 12398592 | tf_op jit(solution)/shard_map/dot_general | solution.py:261
  36.6 3.6 %convert_reduce_fusion = (f32[3072]{0:T(1024)S(1)}, bf16[384,3072]{1,0:T(8,128)(2,1)S(1)}) fusion(f32[384,3072]{1,0:T(8,128)S(1)} %get-tuple-element.131, bf16[384,768]{1,0:T(8,128)(2,1)S(1)} %copy-done.7, bf16[768,3072]{1,0:T(8,128)(2,1)S(1)} %bitcast.123), kind=kOutput, calls=%fused_computation.9 | convolution fusion | flops 1826092032 | bytes 12398592 | tf_op jit(solution)/shard_map/dot_general | solution.py:268
  40.3 4.5 %convolution_convert_fusion = bf16[3072,768]{1,0:T(8,128)(2,1)} fusion(bf16[384,3072]{1,0:T(8,128)(2,1)S(1)} %get-tuple-element.130, bf16[384,3072]{1,0:T(8,128)(2,1)S(1)} %get-tuple-element.133, pred[]{:T(512)S(6)} %eq.2, bf16[384,768]{1,0:T(8,128)(2,1)S(1)} %copy-done.7, bf16[384,768]{1,0:T(8,128)(2,1)S(1)} %fusion.14), kind=kOutput, calls=%fused_computation.2 | convolution fusion | flops 1815773184 | bytes 10616833 | tf_op jit(solution)/shard_map/dot_general | solution.py:122
  47.1 5.2 %fusion.34 = f32[384,768]{1,0:T(8,128)S(1)} fusion(bf16[384,3072]{1,0:T(8,128)(2,1)} %copy-done.5, bf16[3072,768]{1,0:T(8,128)(2,1)} %param.16), kind=kOutput, calls=%fused_computation.187 | convolution fusion | flops 1811939328 | bytes 8257536 | tf_op jit(solution)/shard_map/dot_general | solution.py:280
  52.4 2.0 %fusion.35 = f32[384,768]{1,0:T(8,128)S(1)} fusion(bf16[384,3072]{1,0:T(8,128)(2,1)S(1)} %copy-done.4, bf16[768,3072]{1,0:T(8,128)(2,1)S(1)} %bitcast.125), kind=kOutput, calls=%fused_computation.188 | convolution fusion | flops 1811939328 | bytes 8257536 | tf_op jit(solution)/shard_map/dot_general | solution.py:277
  54.4 9.1 %backward.1 = (f32[64,768]{1,0:T(8,128)S(1)}, bf16[16,24,768]{2,1,0:T(8,128)(2,1)S(1)}) custom-call(bf16[22,30,768]{2,1,0:T(8,128)(2,1)S(1)} %pad_maximum_fusion.3.pad_ref, f32[16,24,768]{2,1,0:T(8,128)S(1)} %get-tuple-element.77.conv_ref, f32[16,24,768]{2,1,0:T(8,128)S(1)} %bitcast.114, f32[16,24,768]{2,1,0:T(8,128)S(1)} %bitcast.115, ...), custom_call_target="tpu_custom_call" | custom-call | flops 28901376 | bytes 8388608 | tf_op jit(solution)/shard_map/backward/pallas_call | solution.py:211
  63.7 5.1 %fusion.7 = f32[3072,768]{1,0:T(8,128)} fusion(bf16[384,3072]{1,0:T(8,128)(2,1)S(1)} %copy-done.6, bf16[384,3072]{1,0:T(8,128)(2,1)S(1)} %copy-done.4, pred[]{:T(512)S(6)} %eq.2, bf16[384,768]{1,0:T(8,128)(2,1)S(1)} %fusion.14, bf16[384,768]{1,0:T(8,128)(2,1)S(1)} %copy-done.8), kind=kOutput, calls=%fused_computation.15 | convolution fusion | flops 1813413888 | bytes 15335425 | tf_op jit(solution)/shard_map/dot_general | solution.py:122
  68.9 2.8 %collective-permute-start.9 = (bf16[16,3,768]{2,1,0:T(4,128)(2,1)S(1)}, bf16[16,3,768]{2,1,0:T(4,128)(2,1)S(1)}, u32[]{:S(2)}, u32[]{:S(2)}) collective-permute-start(bf16[16,3,768]{2,1,0:T(4,128)(2,1)S(1)} %get-tuple-element.103), channel_id=1, source_target_pairs={{0,1},{1,2},{2,3},{3,4},{4,5},{5,6},{6,7},{7,8},{8,9},{9,10},{10,1... | collective-permute-start | bytes 221192 | tf_op jit(solution)/shard_map/ppermute | solution.py:105
  71.7 1.9 collective-permute-start.10
  73.7 3.9 %collective-permute-done.10 = bf16[16,3,768]{2,1,0:T(4,128)(2,1)S(1)} collective-permute-done((bf16[16,3,768]{2,1,0:T(4,128)(2,1)S(1)}, bf16[16,3,768]{2,1,0:T(4,128)(2,1)S(1)}, u32[]{:S(2)}, u32[]{:S(2)}) %collective-permute-start.10) | collective-permute-done | bytes 73760 | tf_op jit(solution)/shard_map/ppermute | solution.py:105
  79.1 4.7 %collective-permute-start.12 = (bf16[3,30,768]{2,1,0:T(8,128)(2,1)S(1)}, bf16[3,30,768]{2,1,0:T(8,128)(2,1)S(1)}, u32[]{:S(2)}, u32[]{:S(2)}) collective-permute-start(bf16[3,30,768]{2,1,0:T(8,128)(2,1)S(1)} %get-tuple-element.97), channel_id=1, source_target_pairs={{0,32},{32,64},{64,96},{96,128},{128,160},{160,192},{192,224},{1,3... | collective-permute-start | bytes 414728 | tf_op jit(solution)/shard_map/ppermute | solution.py:105
  86.3 8.2 %add_convert_fusion = bf16[3072,768]{1,0:T(8,128)(2,1)} fusion(f32[3072,768]{1,0:T(8,128)} %fusion.7, bf16[3072,768]{1,0:T(8,128)(2,1)} %collective-permute-done.5), kind=kLoop, calls=%fused_computation | loop fusion | flops 7077888 | bytes 18874368 | tf_op jit(solution)/shard_map/convert_element_type | solution.py:275
  94.5 2.9 %constant_dynamic-slice_fusion.8 = (bf16[2,1,4,4,24,768]{5,4,3,2,1,0:T(8,128)(2,1)S(1)}, bf16[2,1,4,4,24,768]{5,4,3,2,1,0:T(8,128)(2,1)S(1)}, bf16[2,1,4,4,24,76...) fusion(bf16[2,4,4,4,24,768]{5,4,3,2,1,0:T(8,128)(2,1)} %bitcast.116, s32[]{:T(128)S(6)} %select_n.267, ...), kind=kLoop, calls=%fused_computation.121 | loop fusion | bytes 9437200 | tf_op jit(solution)/shard_map/jit(dynamic_index_in_dim)/dynamic_slice | solution.py:50
  100.3 2.0 collective-permute-start.6
  102.3 6.2 %collective-permute-start.7 = (bf16[800,768]{1,0:T(8,128)(2,1)S(1)}, bf16[800,768]{1,0:T(8,128)(2,1)S(1)}, u32[]{:S(2)}, u32[]{:S(2)}) collective-permute-start(bf16[800,768]{1,0:T(8,128)(2,1)S(1)} %get-tuple-element.128), channel_id=1, source_target_pairs={{0,4},{1,65},{2,6},{3,67},{4,0},{5,69},{6,2},{7,71},{8,12},{9,73},... | collective-permute-start | bytes 3686408 | tf_op jit(solution)/shard_map/ppermute | solution.py:62
  108.8 9.7 %multiply_add_fusion = f32[16,24,768]{2,1,0:T(8,128)} fusion(bf16[16,24,768]{2,1,0:T(8,128)(2,1)S(1)} %get-tuple-element.17, bf16[16,3,768]{2,1,0:T(4,128)(2,1)S(1)} %collective-permute-done.9, bf16[19,30,768]{2,1,0:T(8,128)(2,1)S(1)} %get-tuple-element.95, bf16[16,27,768]{2,1,0:T(8,128)(2,1)S(1)} %constant_dynamic-update-slice_fusion.2, ...), kind=kLoop, calls=%fused_computation.33 | loop fusion | flops 46301184 | bytes 29125632 | tf_op jit(solution)/shard_map/add | solution.py:303
  118.5 3.3 %collective-permute-done.6 = bf16[800,768]{1,0:T(8,128)(2,1)S(1)} collective-permute-done((bf16[800,768]{1,0:T(8,128)(2,1)S(1)}, bf16[800,768]{1,0:T(8,128)(2,1)S(1)}, u32[]{:S(2)}, u32[]{:S(2)}) %collective-permute-start.6) | collective-permute-done | bytes 1228832 | tf_op jit(solution)/shard_map/ppermute | solution.py:62
  121.8 14.0 %collective-permute-done.7 = bf16[800,768]{1,0:T(8,128)(2,1)S(1)} collective-permute-done((bf16[800,768]{1,0:T(8,128)(2,1)S(1)}, bf16[800,768]{1,0:T(8,128)(2,1)S(1)}, u32[]{:S(2)}, u32[]{:S(2)}) %collective-permute-start.7) | collective-permute-done | bytes 1228832 | tf_op jit(solution)/shard_map/ppermute | solution.py:62
  137.4 17.2 %collective-permute-start.15 = (bf16[224,768]{1,0:T(8,128)(2,1)S(1)}, bf16[224,768]{1,0:T(8,128)(2,1)S(1)}, u32[]{:S(2)}, u32[]{:S(2)}) collective-permute-start(bf16[224,768]{1,0:T(8,128)(2,1)S(1)} %get-tuple-element.126), channel_id=1, source_target_pairs={{0,96},{1,7},{2,98},{3,1},{4,100},{5,3},{6,102},{7,5},{8,104},{9,1... | collective-permute-start | bytes 1032200 | tf_op jit(solution)/shard_map/ppermute | solution.py:62
  155.3 7.2 %collective-permute-done.15 = bf16[224,768]{1,0:T(8,128)(2,1)S(1)} collective-permute-done((bf16[224,768]{1,0:T(8,128)(2,1)S(1)}, bf16[224,768]{1,0:T(8,128)(2,1)S(1)}, u32[]{:S(2)}, u32[]{:S(2)}) %collective-permute-start.15) | collective-permute-done | bytes 344096 | tf_op jit(solution)/shard_map/ppermute | solution.py:62
  162.5 3.1 %collective-permute-done.13 = bf16[224,768]{1,0:T(8,128)(2,1)S(1)} collective-permute-done((bf16[224,768]{1,0:T(8,128)(2,1)S(1)}, bf16[224,768]{1,0:T(8,128)(2,1)S(1)}, u32[]{:S(2)}, u32[]{:S(2)}) %collective-permute-start.13) | collective-permute-done | bytes 344096 | tf_op jit(solution)/shard_map/ppermute | solution.py:62
  166.1 3.6 %collective-permute-start.21 = (bf16[56,768]{1,0:T(8,128)(2,1)S(1)}, bf16[56,768]{1,0:T(8,128)(2,1)S(1)}, u32[]{:S(2)}, u32[]{:S(2)}) collective-permute-start(bf16[56,768]{1,0:T(8,128)(2,1)S(1)} %get-tuple-element.122), channel_id=1, source_target_pairs={{0,24},{128,152},{8,0},{136,128},{16,8},{144,136},{24,16},{152,144... | collective-permute-start | bytes 258056 | tf_op jit(solution)/shard_map/ppermute | solution.py:90
  169.7 5.5 %collective-permute-start.20 = (bf16[56,768]{1,0:T(8,128)(2,1)S(1)}, bf16[56,768]{1,0:T(8,128)(2,1)S(1)}, u32[]{:S(2)}, u32[]{:S(2)}) collective-permute-start(bf16[56,768]{1,0:T(8,128)(2,1)S(1)} %get-tuple-element.121), channel_id=1, source_target_pairs={{0,144},{128,24},{8,152},{136,0},{16,128},{144,8},{24,136},{152,16... | collective-permute-start | bytes 258056 | tf_op jit(solution)/shard_map/ppermute | solution.py:90
  175.2 3.1 %collective-permute-start.18 = (bf16[56,768]{1,0:T(8,128)(2,1)S(1)}, bf16[56,768]{1,0:T(8,128)(2,1)S(1)}, u32[]{:S(2)}, u32[]{:S(2)}) collective-permute-start(bf16[56,768]{1,0:T(8,128)(2,1)S(1)} %get-tuple-element.119), channel_id=1, source_target_pairs={{0,136},{128,16},{8,144},{136,24},{16,152},{144,0},{24,128},{152,8... | collective-permute-start | bytes 258056 | tf_op jit(solution)/shard_map/ppermute | solution.py:90
  180.9 3.3 %collective-permute-done.19 = bf16[56,768]{1,0:T(8,128)(2,1)S(1)} collective-permute-done((bf16[56,768]{1,0:T(8,128)(2,1)S(1)}, bf16[56,768]{1,0:T(8,128)(2,1)S(1)}, u32[]{:S(2)}, u32[]{:S(2)}) %collective-permute-start.19) | collective-permute-done | bytes 86048 | tf_op jit(solution)/shard_map/ppermute | solution.py:90
  184.2 4.1 %collective-permute-done.18 = bf16[56,768]{1,0:T(8,128)(2,1)S(1)} collective-permute-done((bf16[56,768]{1,0:T(8,128)(2,1)S(1)}, bf16[56,768]{1,0:T(8,128)(2,1)S(1)}, u32[]{:S(2)}, u32[]{:S(2)}) %collective-permute-start.18) | collective-permute-done | bytes 86048 | tf_op jit(solution)/shard_map/ppermute | solution.py:90
  188.3 2.2 %collective-permute-done.17 = bf16[56,768]{1,0:T(8,128)(2,1)S(1)} collective-permute-done((bf16[56,768]{1,0:T(8,128)(2,1)S(1)}, bf16[56,768]{1,0:T(8,128)(2,1)S(1)}, u32[]{:S(2)}, u32[]{:S(2)}) %collective-permute-start.17) | collective-permute-done | bytes 86048 | tf_op jit(solution)/shard_map/ppermute | solution.py:90
  190.5 4.2 %collective-permute-done.16 = bf16[56,768]{1,0:T(8,128)(2,1)S(1)} collective-permute-done((bf16[56,768]{1,0:T(8,128)(2,1)S(1)}, bf16[56,768]{1,0:T(8,128)(2,1)S(1)}, u32[]{:S(2)}, u32[]{:S(2)}) %collective-permute-start.16) | collective-permute-done | bytes 86048 | tf_op jit(solution)/shard_map/ppermute | solution.py:90
  (262 shorter events, 28.6 us)
Async XLA Ops:
  0.6 9.6 %copy-start.11 = (f32[7,7,768]{2,1,0:T(8,128)S(1)}, f32[7,7,768]{2,1,0:T(8,128)}, u32[]{:S(2)}) copy-start(f32[7,7,768]{2,1,0:T(8,128)} %param.12) | copy-start | bytes 451588
  0.7 10.3 %copy-start.79 = (f32[768]{0:T(1024)S(1)}, f32[768]{0:T(1024)}, u32[]{:S(2)}) copy-start(f32[768]{0:T(1024)} %param.20) | copy-start | bytes 9220
  0.7 10.3 %copy-start = (bf16[16,24,768]{2,1,0:T(8,128)(2,1)S(1)}, bf16[16,24,768]{2,1,0:T(8,128)(2,1)}, u32[]{:S(2)}) copy-start(bf16[16,24,768]{2,1,0:T(8,128)(2,1)} %cot_ref.1) | copy-start | bytes 1769476
  1.9 10.8 %collective-permute-start.1 = (bf16[16,3,768]{2,1,0:T(4,128)(2,1)S(1)}, bf16[16,3,768]{2,1,0:T(4,128)(2,1)S(1)}, u32[]{:S(2)}, u32[]{:S(2)}) collective-permute-start(bf16[16,3,768]{2,1,0:T(4,128)(2,1)S(1)} %get-tuple-element.105), channel_id=1, source_target_pairs={{1,0},{2,1},{3,2},{4,3},{5,4},{6,5},{7,6},{8,7},{9,8},{10,9},{11,1... | collective-permute-start | bytes 221192 | tf_op jit(solution)/shard_map/ppermute | solution.py:105
  7.0 5.6 %collective-permute-start = (bf16[16,3,768]{2,1,0:T(4,128)(2,1)S(1)}, bf16[16,3,768]{2,1,0:T(4,128)(2,1)S(1)}, u32[]{:S(2)}, u32[]{:S(2)}) collective-permute-start(bf16[16,3,768]{2,1,0:T(4,128)(2,1)S(1)} %get-tuple-element.104), channel_id=1, source_target_pairs={{0,1},{1,2},{2,3},{3,4},{4,5},{5,6},{6,7},{7,8},{8,9},{9,10},{10,1... | collective-permute-start | bytes 221192 | tf_op jit(solution)/shard_map/ppermute | solution.py:105
  12.8 6.8 %collective-permute-start.3 = (bf16[3,30,768]{2,1,0:T(8,128)(2,1)S(1)}, bf16[3,30,768]{2,1,0:T(8,128)(2,1)S(1)}, u32[]{:S(2)}, u32[]{:S(2)}) collective-permute-start(bf16[3,30,768]{2,1,0:T(8,128)(2,1)S(1)} %get-tuple-element.101), channel_id=1, source_target_pairs={{32,0},{64,32},{96,64},{128,96},{160,128},{192,160},{224,192},{33,... | collective-permute-start | bytes 414728 | tf_op jit(solution)/shard_map/ppermute | solution.py:105
  14.1 6.4 %collective-permute-start.2 = (bf16[3,30,768]{2,1,0:T(8,128)(2,1)S(1)}, bf16[3,30,768]{2,1,0:T(8,128)(2,1)S(1)}, u32[]{:S(2)}, u32[]{:S(2)}) collective-permute-start(bf16[3,30,768]{2,1,0:T(8,128)(2,1)S(1)} %get-tuple-element.100), channel_id=1, source_target_pairs={{0,32},{32,64},{64,96},{96,128},{128,160},{160,192},{192,224},{1,3... | collective-permute-start | bytes 414728 | tf_op jit(solution)/shard_map/ppermute | solution.py:105
  44.8 41.5 %collective-permute-start.5 = (bf16[3072,768]{1,0:T(8,128)(2,1)}, bf16[3072,768]{1,0:T(8,128)(2,1)}, u32[]{:S(2)}, u32[]{:S(2)}) collective-permute-start(bf16[3072,768]{1,0:T(8,128)(2,1)} %convolution_convert_fusion), channel_id=1, source_target_pairs={{0,1},{1,0},{2,3},{3,2},{4,5},{5,4},{6,7},{7,6},{8,9},{9,8},{10,11... | collective-permute-start | bytes 14155784 | tf_op jit(solution)/shard_map/ppermute | solution.py:97
  54.4 9.2 %copy-start.6 = (bf16[384,3072]{1,0:T(8,128)(2,1)S(1)}, bf16[384,3072]{1,0:T(8,128)(2,1)}, u32[]{:S(2)}) copy-start(bf16[384,3072]{1,0:T(8,128)(2,1)} %copy-done.5) | copy-start | bytes 7077892
  54.4 9.2 %copy-start.8 = (bf16[384,768]{1,0:T(8,128)(2,1)S(1)}, bf16[384,768]{1,0:T(8,128)(2,1)}, u32[]{:S(2)}) copy-start(bf16[384,768]{1,0:T(8,128)(2,1)} %fusion.15) | copy-start | bytes 1769476
  63.5 20.4 %collective-permute-start.4 = (f32[32,768]{1,0:T(8,128)S(1)}, f32[32,768]{1,0:T(8,128)S(1)}, u32[]{:S(2)}, u32[]{:S(2)}) collective-permute-start(f32[32,768]{1,0:T(8,128)S(1)} %slice_select_fusion.2), channel_id=1, source_target_pairs={{0,1},{1,0},{2,3},{3,2},{4,5},{5,4},{6,7},{7,6},{8,9},{9,8},{10,11... | collective-permute-start | bytes 294920 | tf_op jit(solution)/shard_map/ppermute | solution.py:97
  68.9 4.8 %collective-permute-start.9 = (bf16[16,3,768]{2,1,0:T(4,128)(2,1)S(1)}, bf16[16,3,768]{2,1,0:T(4,128)(2,1)S(1)}, u32[]{:S(2)}, u32[]{:S(2)}) collective-permute-start(bf16[16,3,768]{2,1,0:T(4,128)(2,1)S(1)} %get-tuple-element.103), channel_id=1, source_target_pairs={{0,1},{1,2},{2,3},{3,4},{4,5},{5,6},{6,7},{7,8},{8,9},{9,10},{10,1... | collective-permute-start | bytes 221192 | tf_op jit(solution)/shard_map/ppermute | solution.py:105
  71.7 5.9 %collective-permute-start.10 = (bf16[16,3,768]{2,1,0:T(4,128)(2,1)S(1)}, bf16[16,3,768]{2,1,0:T(4,128)(2,1)S(1)}, u32[]{:S(2)}, u32[]{:S(2)}) collective-permute-start(bf16[16,3,768]{2,1,0:T(4,128)(2,1)S(1)} %get-tuple-element.102), channel_id=1, source_target_pairs={{1,0},{2,1},{3,2},{4,3},{5,4},{6,5},{7,6},{8,7},{9,8},{10,9},{11,1... | collective-permute-start | bytes 221192 | tf_op jit(solution)/shard_map/ppermute | solution.py:105
  77.8 6.6 %collective-permute-start.11 = (bf16[3,30,768]{2,1,0:T(8,128)(2,1)S(1)}, bf16[3,30,768]{2,1,0:T(8,128)(2,1)S(1)}, u32[]{:S(2)}, u32[]{:S(2)}) collective-permute-start(bf16[3,30,768]{2,1,0:T(8,128)(2,1)S(1)} %get-tuple-element.96), channel_id=1, source_target_pairs={{32,0},{64,32},{96,64},{128,96},{160,128},{192,160},{224,192},{33,... | collective-permute-start | bytes 414728 | tf_op jit(solution)/shard_map/ppermute | solution.py:105
  79.1 6.8 %collective-permute-start.12 = (bf16[3,30,768]{2,1,0:T(8,128)(2,1)S(1)}, bf16[3,30,768]{2,1,0:T(8,128)(2,1)S(1)}, u32[]{:S(2)}, u32[]{:S(2)}) collective-permute-start(bf16[3,30,768]{2,1,0:T(8,128)(2,1)S(1)} %get-tuple-element.97), channel_id=1, source_target_pairs={{0,32},{32,64},{64,96},{96,128},{128,160},{160,192},{192,224},{1,3... | collective-permute-start | bytes 414728 | tf_op jit(solution)/shard_map/ppermute | solution.py:105
  99.7 8.8 %copy-start.13 = (f32[768]{0:T(1024)S(1)}, f32[768]{0:T(1024)}, u32[]{:S(2)}) copy-start(f32[768]{0:T(1024)} %get-tuple-element.57) | copy-start | bytes 9220
  99.7 8.8 %copy-start.15 = (f32[768]{0:T(1024)S(1)}, f32[768]{0:T(1024)}, u32[]{:S(2)}) copy-start(f32[768]{0:T(1024)} %get-tuple-element.58) | copy-start | bytes 9220
  99.7 8.8 %copy-start.17 = (f32[768]{0:T(1024)S(1)}, f32[768]{0:T(1024)}, u32[]{:S(2)}) copy-start(f32[768]{0:T(1024)} %get-tuple-element.59) | copy-start | bytes 9220
  100.3 21.4 %collective-permute-start.6 = (bf16[800,768]{1,0:T(8,128)(2,1)S(1)}, bf16[800,768]{1,0:T(8,128)(2,1)S(1)}, u32[]{:S(2)}, u32[]{:S(2)}) collective-permute-start(bf16[800,768]{1,0:T(8,128)(2,1)S(1)} %get-tuple-element.129), channel_id=1, source_target_pairs={{0,2},{1,33},{2,4},{3,35},{4,6},{5,37},{6,0},{7,39},{8,10},{9,41},... | collective-permute-start | bytes 3686408 | tf_op jit(solution)/shard_map/ppermute | solution.py:62
  102.3 33.5 %collective-permute-start.7 = (bf16[800,768]{1,0:T(8,128)(2,1)S(1)}, bf16[800,768]{1,0:T(8,128)(2,1)S(1)}, u32[]{:S(2)}, u32[]{:S(2)}) collective-permute-start(bf16[800,768]{1,0:T(8,128)(2,1)S(1)} %get-tuple-element.128), channel_id=1, source_target_pairs={{0,4},{1,65},{2,6},{3,67},{4,0},{5,69},{6,2},{7,71},{8,12},{9,73},... | collective-permute-start | bytes 3686408 | tf_op jit(solution)/shard_map/ppermute | solution.py:62
  108.5 27.3 %collective-permute-start.8 = (bf16[800,768]{1,0:T(8,128)(2,1)S(1)}, bf16[800,768]{1,0:T(8,128)(2,1)S(1)}, u32[]{:S(2)}, u32[]{:S(2)}) collective-permute-start(bf16[800,768]{1,0:T(8,128)(2,1)S(1)} %get-tuple-element.127), channel_id=1, source_target_pairs={{0,6},{1,97},{2,0},{3,99},{4,2},{5,101},{6,4},{7,103},{8,14},{9,10... | collective-permute-start | bytes 3686408 | tf_op jit(solution)/shard_map/ppermute | solution.py:62
  137.4 25.1 %collective-permute-start.15 = (bf16[224,768]{1,0:T(8,128)(2,1)S(1)}, bf16[224,768]{1,0:T(8,128)(2,1)S(1)}, u32[]{:S(2)}, u32[]{:S(2)}) collective-permute-start(bf16[224,768]{1,0:T(8,128)(2,1)S(1)} %get-tuple-element.126), channel_id=1, source_target_pairs={{0,96},{1,7},{2,98},{3,1},{4,100},{5,3},{6,102},{7,5},{8,104},{9,1... | collective-permute-start | bytes 1032200 | tf_op jit(solution)/shard_map/ppermute | solution.py:62
  154.6 7.9 %collective-permute-start.14 = (bf16[224,768]{1,0:T(8,128)(2,1)S(1)}, bf16[224,768]{1,0:T(8,128)(2,1)S(1)}, u32[]{:S(2)}, u32[]{:S(2)}) collective-permute-start(bf16[224,768]{1,0:T(8,128)(2,1)S(1)} %get-tuple-element.125), channel_id=1, source_target_pairs={{0,64},{1,5},{2,66},{3,7},{4,68},{5,1},{6,70},{7,3},{8,72},{9,13},... | collective-permute-start | bytes 1032200 | tf_op jit(solution)/shard_map/ppermute | solution.py:62
  154.6 11.0 %collective-permute-start.13 = (bf16[224,768]{1,0:T(8,128)(2,1)S(1)}, bf16[224,768]{1,0:T(8,128)(2,1)S(1)}, u32[]{:S(2)}, u32[]{:S(2)}) collective-permute-start(bf16[224,768]{1,0:T(8,128)(2,1)S(1)} %get-tuple-element.124), channel_id=1, source_target_pairs={{0,32},{1,3},{2,34},{3,5},{4,36},{5,7},{6,38},{7,1},{8,40},{9,11},... | collective-permute-start | bytes 1032200 | tf_op jit(solution)/shard_map/ppermute | solution.py:62
  166.0 12.3 %collective-permute-start.22 = (bf16[56,768]{1,0:T(8,128)(2,1)S(1)}, bf16[56,768]{1,0:T(8,128)(2,1)S(1)}, u32[]{:S(2)}, u32[]{:S(2)}) collective-permute-start(bf16[56,768]{1,0:T(8,128)(2,1)S(1)} %get-tuple-element.123), channel_id=1, source_target_pairs={{0,152},{128,0},{8,128},{136,8},{16,136},{144,16},{24,144},{152,24... | collective-permute-start | bytes 258056 | tf_op jit(solution)/shard_map/ppermute | solution.py:90
  166.1 13.2 %collective-permute-start.21 = (bf16[56,768]{1,0:T(8,128)(2,1)S(1)}, bf16[56,768]{1,0:T(8,128)(2,1)S(1)}, u32[]{:S(2)}, u32[]{:S(2)}) collective-permute-start(bf16[56,768]{1,0:T(8,128)(2,1)S(1)} %get-tuple-element.122), channel_id=1, source_target_pairs={{0,24},{128,152},{8,0},{136,128},{16,8},{144,136},{24,16},{152,144... | collective-permute-start | bytes 258056 | tf_op jit(solution)/shard_map/ppermute | solution.py:90
  169.7 11.2 %collective-permute-start.20 = (bf16[56,768]{1,0:T(8,128)(2,1)S(1)}, bf16[56,768]{1,0:T(8,128)(2,1)S(1)}, u32[]{:S(2)}, u32[]{:S(2)}) collective-permute-start(bf16[56,768]{1,0:T(8,128)(2,1)S(1)} %get-tuple-element.121), channel_id=1, source_target_pairs={{0,144},{128,24},{8,152},{136,0},{16,128},{144,8},{24,136},{152,16... | collective-permute-start | bytes 258056 | tf_op jit(solution)/shard_map/ppermute | solution.py:90
  175.2 9.0 %collective-permute-start.19 = (bf16[56,768]{1,0:T(8,128)(2,1)S(1)}, bf16[56,768]{1,0:T(8,128)(2,1)S(1)}, u32[]{:S(2)}, u32[]{:S(2)}) collective-permute-start(bf16[56,768]{1,0:T(8,128)(2,1)S(1)} %get-tuple-element.120), channel_id=1, source_target_pairs={{0,16},{128,144},{8,24},{136,152},{16,0},{144,128},{24,8},{152,136... | collective-permute-start | bytes 258056 | tf_op jit(solution)/shard_map/ppermute | solution.py:90
  175.2 13.1 %collective-permute-start.18 = (bf16[56,768]{1,0:T(8,128)(2,1)S(1)}, bf16[56,768]{1,0:T(8,128)(2,1)S(1)}, u32[]{:S(2)}, u32[]{:S(2)}) collective-permute-start(bf16[56,768]{1,0:T(8,128)(2,1)S(1)} %get-tuple-element.119), channel_id=1, source_target_pairs={{0,136},{128,16},{8,144},{136,24},{16,152},{144,0},{24,128},{152,8... | collective-permute-start | bytes 258056 | tf_op jit(solution)/shard_map/ppermute | solution.py:90
  178.3 12.2 %collective-permute-start.17 = (bf16[56,768]{1,0:T(8,128)(2,1)S(1)}, bf16[56,768]{1,0:T(8,128)(2,1)S(1)}, u32[]{:S(2)}, u32[]{:S(2)}) collective-permute-start(bf16[56,768]{1,0:T(8,128)(2,1)S(1)} %get-tuple-element.118), channel_id=1, source_target_pairs={{0,8},{128,136},{8,16},{136,144},{16,24},{144,152},{24,0},{152,128... | collective-permute-start | bytes 258056 | tf_op jit(solution)/shard_map/ppermute | solution.py:90
  179.3 15.4 %collective-permute-start.16 = (bf16[56,768]{1,0:T(8,128)(2,1)S(1)}, bf16[56,768]{1,0:T(8,128)(2,1)S(1)}, u32[]{:S(2)}, u32[]{:S(2)}) collective-permute-start(bf16[56,768]{1,0:T(8,128)(2,1)S(1)} %get-tuple-element.117), channel_id=1, source_target_pairs={{0,128},{128,8},{8,136},{136,16},{16,144},{144,24},{24,152},{152,0... | collective-permute-start | bytes 258056 | tf_op jit(solution)/shard_map/ppermute | solution.py:90
  194.8 1.6 collective-permute-start.23
  (81 other events, 410.6 us)
where the time goes:
time: 199 us
  starting transfers between devices  66.7 us (34%)
  waiting for transfers between devices  49.5 us (25%)
  other arithmetic  33.5 us (17%)
  matrix products  25.3 us (13%)
  local copies, waits for them, and re-layouts  12.5 us (6%)
  Pallas kernels  9.08 us (5%)
  between operations  2.39 us (1%)
    ppermute x6, waiting for transfers between devices, split_move(): lax.ppermute(moved[k], AXES, core_pairs(k, lead))  27.6 us
    ppermute x6, starting transfers between devices, split_move(): lax.ppermute(moved[k], AXES, core_pairs(k, lead))  26.1 us
    ppermute x8, starting transfers between devices, shift(): lax.ppermute(v, axes, [(i, i + d) for i in range(n) if 0 <= i + d < n])  23.3 us
    ppermute x7, starting transfers between devices, z_sum(): got = lax.ppermute(sent, ('zl', 'zh'), pairs)  14.9 us
    ppermute x7, waiting for transfers between devices, z_sum(): got = lax.ppermute(sent, ('zl', 'zh'), pairs)  13.7 us
    add x1, other arithmetic, on_device(): grad_image + conv_weight[i, j] * d_pad[6 - i:6 - i + rows, 6 - j:6 - j +...  9.66 us
    dot_general x2, matrix products, tdot(): lax.dot_general(a, b, (((0,), (0,)), ((), ())), preferred_element_type=F32)  9.58 us
    reduce_sum x1, other arithmetic, on_device(): channel_mean = jnp.mean(flat, axis=-1, keepdims=True)  9.29 us
  transfers between devices with their start and end apart: 24, of which 14 were waited for; matrix products, arithmetic and copies ran while one was open for 14% of the time, Pallas kernels for 5%

commit v1 on v0

--- a/solution.py
+++ b/solution.py
@@ -17,10 +17,6 @@
 COL = ("zh", "x", "c")
 BF = jnp.bfloat16
 F32 = jnp.float32
-
-
-def spot_z(z):
-    return (z % 2) * 4 + z // 2
 
 
 def core_pairs(k, lead):
@@ -73,21 +69,21 @@
 
 
 def z_sum(v, small):
-    count = small.shape[0]
+    count, chans = small.shape
     low = small.astype(BF)
     zl = lax.axis_index("zl")
     zh = lax.axis_index("zh")
-    acc = lax.dynamic_index_in_dim(v, zl, 0, False)
-    acc = lax.dynamic_index_in_dim(acc, zh, 0, False).astype(F32)
+    away = lax.dynamic_index_in_dim(v, 1 - zl, 0, False).reshape(-1, chans)
+    near = lax.dynamic_index_in_dim(v, zl, 0, False).reshape(-1, chans)
+    got = lax.ppermute(jnp.concatenate([low, away], axis=0), "zl", [(0, 1), (1, 0)])
+    low = (low.astype(F32) + got[:count].astype(F32)).astype(BF)
+    v = (near.astype(F32) + got[count:].astype(F32)).astype(BF).reshape(v.shape[1:])
+    acc = lax.dynamic_index_in_dim(v, zh, 0, False).astype(F32)
     sums = low.astype(F32)
-    z = zh * 2 + zl
-    for k in range(1, 8):
-        to = lax.rem(z + k, 8)
-        part = lax.dynamic_index_in_dim(v, lax.rem(to, 2), 0, False)
-        part = lax.dynamic_index_in_dim(part, to // 2, 0, False)
+    for k in range(1, 4):
+        part = lax.dynamic_index_in_dim(v, lax.rem(zh + k, 4), 0, False)
         sent = jnp.concatenate([low, part], axis=0)
-        pairs = [(spot_z(i), spot_z((i + k) % 8)) for i in range(8)]
-        got = lax.ppermute(sent, ("zl", "zh"), pairs)
+        got = lax.ppermute(sent, "zh", [(i, (i + k) % 4) for i in range(4)])
         sums = sums + got[:count].astype(F32)
         acc = acc + got[count:].astype(F32)
     return acc, sums
@@ -97,17 +93,19 @@
     return lax.ppermute(v, "c", [(0, 1), (1, 0)])
 
 
-def with_halo(x, w):
-    rows, cols, _ = x.shape
-
-    def shift(v, axes, d):
-        n = lax.axis_size(axes)
-        return lax.ppermute(v, axes, [(i, i + d) for i in range(n) if 0 <= i + d < n])
-
-    west = shift(x[:, cols - w :], COL, 1)
+def shift(v, axes, d):
+    n = lax.axis_size(axes)
+    return lax.ppermute(v, axes, [(i, i + d) for i in range(n) if 0 <= i + d < n])
+
+
+def halo_columns(x, w):
+    west = shift(x[:, x.shape[1] - w :], COL, 1)
     east = shift(x[:, :w], COL, -1)
-    x = jnp.concatenate([west, x, east], axis=1)
-    north = shift(x[rows - w :], ROW, 1)
+    return jnp.concatenate([west, x, east], axis=1)
+
+
+def halo_rows(x, w):
+    north = shift(x[x.shape[0] - w :], ROW, 1)
     south = shift(x[:w], ROW, -1)
     return jnp.concatenate([north, x, south], axis=0)
 
@@ -227,6 +225,86 @@
     )(padded, conv_out, d_normed, branch, cotangent, sum_pre, params)
 
 
+def chunk_kernel(at_ref, pre_ref, hid_ref, normed_ref, db_ref, come_ref, low_ref, *outs):
+    unit = hid_ref.shape[1] // 16
+    core = at_ref[0]
+    me = (at_ref[1], at_ref[2])
+    group = pl.program_id(0)
+    count = low_ref.shape[0]
+    first = core == 0
+    lhs = jnp.where(first, pre_ref[...], hid_ref[...])
+    rhs = jnp.where(first, normed_ref[...], db_ref[...])
+    v = lax.dot_general(lhs, rhs, (((0,), (0,)), ((), ())), preferred_element_type=F32)
+    v = v + come_ref[...].astype(F32)
+
+    @pl.when(group == 0)
+    def _():
+        for out in outs:
+            out[0:count, :] = low_ref[...]
+
+    def store(k, row, value):
+        value = value.astype(BF)
+        rows = pl.ds(pl.multiple_of(count + row, 16), 2 * unit)
+        for n in range(4):
+
+            @pl.when(k == n)
+            def _(n=n):
+                outs[n][rows, :] = value
+
+    def part(zh, x):
+        t = zh * 4 + x
+        return v[t * unit : (t + 1) * unit]
+
+    @pl.when(first)
+    def _():
+        for x in range(4):
+            k = lax.rem(x + 4 - me[0], 4)
+            for zh in (0, 2):
+                value = jnp.concatenate([part(zh, x), part(zh + 1, x)], axis=0)
+                store(k, (group * 4 + zh) * unit, value)
+
+    @pl.when(core == 1)
+    def _():
+        k = lax.rem(lax.rem(group, 4) + 4 - me[1], 4)
+        for zh in range(4):
+            for x in (0, 2):
+                t = zh * 4 + x
+                store(k, ((group // 4) * 16 + t) * unit, v[t * unit : (t + 2) * unit])
+
+
+def chunks(d_pre, hidden, normed, d_branch, come, low):
+    pixels, hid = hidden.shape
+    chans = normed.shape[1]
+    count = low.shape[0]
+    wide = hid // 8
+    at = jnp.stack([lax.axis_index("c"), lax.axis_index("x"), lax.axis_index("y")]).astype(
+        jnp.int32
+    )
+    whole = pl.BlockSpec((pixels, chans), lambda g: (0, 0))
+    columns = pl.BlockSpec((pixels, wide), lambda g: (0, g))
+    rows = count + hid // 4
+    return pl.pallas_call(
+        chunk_kernel,
+        grid=(8,),
+        in_specs=[
+            pl.BlockSpec(memory_space=pltpu.SMEM),
+            columns,
+            columns,
+            whole,
+            whole,
+            pl.BlockSpec((wide, chans), lambda g: (g, 0)),
+            pl.BlockSpec((count, chans), lambda g: (0, 0)),
+        ],
+        out_specs=[pl.BlockSpec((rows, chans), lambda g: (0, 0))] * 4,
+        out_shape=[jax.ShapeDtypeStruct((rows, chans), BF)] * 4,
+        compiler_params=pltpu.CompilerParams(vmem_limit_bytes=40 * 1024 * 1024),
+        cost_estimate=pl.CostEstimate(
+            flops=2 * pixels * hid * chans, bytes_accessed=18 * 1024 * 1024, transcendentals=0
+        ),
+        name="chunks",
+    )(at, d_pre, hidden, normed, d_branch, come, low)
+
+
 def on_device(
     image,
     conv_weight,
@@ -245,7 +323,7 @@
     per = hid // 256
     scale = 1.0 / math.sqrt(rows * cols * 256)
     first = lax.axis_index("c") == 0
-    padded = with_halo(image, 3)
+    padded = halo_rows(halo_columns(image, 3), 3)
     conv_out = jnp.zeros((rows, cols, chans), F32) + conv_bias
     for i in range(KS):
         for j in range(KS):
@@ -270,10 +348,6 @@
 
     far = tdot(jnp.where(first, hidden, d_pre), jnp.where(first, d_branch, normed)).astype(BF)
     come = core_swap(far)
-    near = tdot(jnp.where(first, d_pre, hidden), jnp.where(first, normed, d_branch))
-    near = lax.optimization_barrier(near)
-    term = (near + come.astype(F32)).astype(BF).reshape(2, 4, 4, 4, 2 * per, chans)
-
     branch = lax.dot_general(
         hidden, w_reduce, (((1,), (1,)), ((), ())), preferred_element_type=F32
     )
@@ -295,8 +369,10 @@
     lower, upper = small[: total // 2], small[total // 2 :]
     small = jnp.where(first, lower, upper) + core_swap(jnp.where(first, upper, lower))
 
-    moved = split_send(term, small, ("x", "y"), (3, 1))
-    d_pad = with_halo(d_conv, 3)
+    moved = list(chunks(d_pre, hidden, normed, d_branch, come, small.astype(BF)))
+    wide = halo_columns(d_conv, 3)
+    wide, moved[0] = lax.optimization_barrier((wide, moved[0]))
+    d_pad = halo_rows(wide, 3)
     grad_image = cotangent.astype(F32)
     for i in range(KS):
         for j in range(KS):

time: 199 us -> 186 us (0.935)
  Pallas kernels: 9.08 us -> 17.3 us
  other arithmetic: 33.5 us -> 25.4 us
  waiting for transfers between devices: 49.5 us -> 43.8 us
  matrix products: 25.3 us -> 20.7 us
  starting transfers between devices: 66.7 us -> 63.5 us
    ppermute x3, starting transfers between devices: 2.36 us -> 12.2 us  [core_swap(): return lax.ppermute(v, 'c', [(0, 1), (1, 0)])]
    ppermute x6, starting transfers between devices: 26.1 us -> 17.6 us  [split_move(): lax.ppermute(moved[k], AXES, core_pairs(k, lead))]
    pallas_call x0 -> x1, Pallas kernels: none -> 8.26 us  [chunks(): pl.pallas_call(chunk_kernel, grid=(8,), in_specs=[pl.BlockSpec(memory_spa...]
    convert_element_type x1 -> x3, other arithmetic: 8.2 us -> 0.08 us  [the longest x1 0.05 us: z_sum(): (near.astype(F32) + got[count:].astype(F32)).astype(BF).reshape(v.shape[1:])]
    dot_general x2 -> x1, matrix products: 9.58 us -> 4.49 us  [tdot(): lax.dot_general(a, b, (((0,), (0,)), ((), ())), preferred_element_type=F32)]
    ppermute x7 -> x4, waiting for transfers between devices: 13.7 us -> 9.22 us  [the longest x1 5.1 us: z_sum(): lax.ppermute(jnp.concatenate([low, away], axis=0), 'zl', [(0, 1), (1, 0)])]
    ppermute x7 -> x4, starting transfers between devices: 14.9 us -> 11.3 us  [the longest x3 10.8 us: z_sum(): got = lax.ppermute(sent, 'zh', [(i, (i + k) % 4) for i in range(4)])]
    unnamed x180 -> x175, local copies, waits for them, and re-layouts: 3.02 us -> 6.6 us
  transfers between devices with their start and end apart: 24 -> 21, of which waited for: 14 -> 12; matrix products, arithmetic and copies ran while one was open for 14% -> 12% of each run, Pallas kernels for 5% -> 5%
where the time goes in v1:
time: 186 us
  starting transfers between devices  63.5 us (34%)
  waiting for transfers between devices  43.8 us (24%)
  other arithmetic  25.4 us (14%)
  matrix products  20.7 us (11%)
  Pallas kernels  17.3 us (9%)
  local copies, waits for them, and re-layouts  12.7 us (7%)
  between operations  2.09 us (1%)
    ppermute x6, waiting for transfers between devices, split_move(): lax.ppermute(moved[k], AXES, core_pairs(k, lead))  26.8 us
    ppermute x8, starting transfers between devices, shift(): lax.ppermute(v, axes, [(i, i + d) for i in range(n) if 0 <= i + d < n])  22.4 us
    ppermute x6, starting transfers between devices, split_move(): lax.ppermute(moved[k], AXES, core_pairs(k, lead))  17.6 us
    ppermute x3, starting transfers between devices, core_swap(): return lax.ppermute(v, 'c', [(0, 1), (1, 0)])  12.2 us
    ppermute x3, starting transfers between devices, z_sum(): got = lax.ppermute(sent, 'zh', [(i, (i + k) % 4) for i in range(4)])  10.8 us
    reduce_sum x1, other arithmetic, on_device(): channel_mean = jnp.mean(flat, axis=-1, keepdims=True)  10.8 us
    add x1, other arithmetic, on_device(): grad_image + conv_weight[i, j] * d_pad[6 - i:6 - i + rows, 6 - j:6 - j +...  9.4 us
    pallas_call x1, Pallas kernels, backward(): pl.pallas_call(functools.partial(backward_kernel, scale), out_shape=(jax....  9.08 us
  transfers between devices with their start and end apart: 21, of which 12 were waited for; matrix products, arithmetic and copies ran while one was open for 12% of the time, Pallas kernels for 5%

profile of v1, /device:TPU:1, one launch (start us, length us, event | category | flops | bytes accessed | tf_op | source)
XLA Modules:
  0.0 185.5 jit_solution(8374486040502899808)
XLA Ops:
  1.9 4.5 %collective-permute-start = (bf16[16,3,768]{2,1,0:T(4,128)(2,1)S(1)}, bf16[16,3,768]{2,1,0:T(4,128)(2,1)S(1)}, u32[]{:S(2)}, u32[]{:S(2)}) collective-permute-start(bf16[16,3,768]{2,1,0:T(4,128)(2,1)S(1)} %get-tuple-element.108), channel_id=1, source_target_pairs={{0,1},{1,2},{2,3},{3,4},{4,5},{5,6},{6,7},{7,8},{8,9},{9,10},{10,1... | collective-permute-start | bytes 221192 | tf_op jit(solution)/shard_map/ppermute | solution.py:98
  6.4 2.1 %collective-permute-start.1 = (bf16[16,3,768]{2,1,0:T(4,128)(2,1)S(1)}, bf16[16,3,768]{2,1,0:T(4,128)(2,1)S(1)}, u32[]{:S(2)}, u32[]{:S(2)}) collective-permute-start(bf16[16,3,768]{2,1,0:T(4,128)(2,1)S(1)} %get-tuple-element.109), channel_id=1, source_target_pairs={{1,0},{2,1},{3,2},{4,3},{5,4},{6,5},{7,6},{8,7},{9,8},{10,9},{11,1... | collective-permute-start | bytes 221192 | tf_op jit(solution)/shard_map/ppermute | solution.py:98
  10.7 1.7 collective-permute-done.1
  12.6 3.2 %collective-permute-start.2 = (bf16[3,30,768]{2,1,0:T(8,128)(2,1)S(1)}, bf16[3,30,768]{2,1,0:T(8,128)(2,1)S(1)}, u32[]{:S(2)}, u32[]{:S(2)}) collective-permute-start(bf16[3,30,768]{2,1,0:T(8,128)(2,1)S(1)} %get-tuple-element.104), channel_id=1, source_target_pairs={{0,32},{32,64},{64,96},{96,128},{128,160},{160,192},{192,224},{1,3... | collective-permute-start | bytes 414728 | tf_op jit(solution)/shard_map/ppermute | solution.py:98
  18.1 3.6 %collective-permute-done.3 = bf16[3,30,768]{2,1,0:T(8,128)(2,1)S(1)} collective-permute-done((bf16[3,30,768]{2,1,0:T(8,128)(2,1)S(1)}, bf16[3,30,768]{2,1,0:T(8,128)(2,1)S(1)}, u32[]{:S(2)}, u32[]{:S(2)}) %collective-permute-start.3) | collective-permute-done | bytes 138272 | tf_op jit(solution)/shard_map/ppermute | solution.py:98
  22.4 10.8 %fusion.21 = (f32[16,24]{1,0:T(8,128)S(1)}, f32[16,24,768]{2,1,0:T(8,128)S(1)}) fusion(bf16[19,30,768]{2,1,0:T(8,128)(2,1)S(1)} %get-tuple-element.103, f32[768]{0:T(1024)S(1)} %copy-done.71, f32[768]{0:T(1024)S(1)} %copy-done.73, f32[768]{0:T(1024)S(1)} %get-tuple-element.35, f32[768]{0:T(1024)S(1)} %get-tuple-element.36, f32[768]{0:T(1024)S(1)} %get-tuple-element.37, ...), kind=kLoop, calls=%fused_computation.149 | loop fusion | flops 46300800 | bytes 28540416 | tf_op jit(solution)/shard_map/reduce_sum | solution.py:332
  34.3 4.8 %multiply_convert_fusion = (bf16[384,3072]{1,0:T(8,128)(2,1)S(1)}, f32[384,3072]{1,0:T(8,128)S(1)}) fusion(f32[3072]{0:T(1024)S(1)} %copy-done.81, bf16[384,768]{1,0:T(8,128)(2,1)S(1)} %fusion.11.normed_ref, bf16[3072,768]{1,0:T(8,128)(2,1)} %param.16), kind=kOutput, calls=%fused_computation.9 | convolution fusion | flops 1819017216 | bytes 12398592 | tf_op jit(solution)/shard_map/dot_general | solution.py:339
  39.1 4.2 %convert_reduce_fusion = (f32[3072]{0:T(1024)}, bf16[384,3072]{1,0:T(8,128)(2,1)S(1)}) fusion(f32[384,3072]{1,0:T(8,128)S(1)} %get-tuple-element.126, bf16[384,768]{1,0:T(8,128)(2,1)S(1)} %fusion.12.db_ref, bf16[768,3072]{1,0:T(8,128)(2,1)S(1)} %bitcast.76), kind=kOutput, calls=%fused_computation.8 | convolution fusion | flops 1826092032 | bytes 12398592 | tf_op jit(solution)/shard_map/dot_general | solution.py:346
  43.4 4.5 %convolution_convert_fusion = bf16[3072,768]{1,0:T(8,128)(2,1)} fusion(bf16[384,3072]{1,0:T(8,128)(2,1)S(1)} %get-tuple-element.125.hid_ref, bf16[384,3072]{1,0:T(8,128)(2,1)S(1)} %get-tuple-element.128.pre_ref, pred[]{:T(512)S(6)} %eq.2, bf16[384,768]{1,0:T(8,128)(2,1)S(1)} %fusion.12.db_ref, bf16[384,768]{1,0:T(8,128)(2,1)S(1)} %fusion.11.normed_ref), kind=kOutput, calls=%fused_computation.1 | convolution fusion | flops 1815773184 | bytes 10616833 | tf_op jit(solution)/shard_map/dot_general | solution.py:120
  48.8 1.6 pad_maximum_fusion.pad_ref
  50.4 5.2 %fusion.25 = f32[384,768]{1,0:T(8,128)S(1)} fusion(bf16[384,3072]{1,0:T(8,128)(2,1)} %copy-done.3, bf16[3072,768]{1,0:T(8,128)(2,1)} %param.16), kind=kOutput, calls=%fused_computation.153 | convolution fusion | flops 1811939328 | bytes 8257536 | tf_op jit(solution)/shard_map/dot_general | solution.py:354
  55.7 2.0 %fusion.26 = f32[384,768]{1,0:T(8,128)S(1)} fusion(bf16[384,3072]{1,0:T(8,128)(2,1)S(1)} %copy-done.2, bf16[768,3072]{1,0:T(8,128)(2,1)S(1)} %bitcast.78), kind=kOutput, calls=%fused_computation.154 | convolution fusion | flops 1811939328 | bytes 8257536 | tf_op jit(solution)/shard_map/dot_general | solution.py:351
  57.7 9.1 %backward.1 = (f32[64,768]{1,0:T(8,128)S(1)}, bf16[16,24,768]{2,1,0:T(8,128)(2,1)S(1)}) custom-call(bf16[22,30,768]{2,1,0:T(8,128)(2,1)S(1)} %pad_maximum_fusion.pad_ref, f32[16,24,768]{2,1,0:T(8,128)S(1)} %get-tuple-element.89.conv_ref, f32[16,24,768]{2,1,0:T(8,128)S(1)} %bitcast.67, f32[16,24,768]{2,1,0:T(8,128)S(1)} %bitcast.68, ...), custom_call_target="tpu_custom_call" | custom-call | flops 28901376 | bytes 8388608 | tf_op jit(solution)/shard_map/backward/pallas_call | solution.py:209
  66.9 2.5 %collective-permute-start.10 = (bf16[16,3,768]{2,1,0:T(4,128)(2,1)S(1)}, bf16[16,3,768]{2,1,0:T(4,128)(2,1)S(1)}, u32[]{:S(2)}, u32[]{:S(2)}) collective-permute-start(bf16[16,3,768]{2,1,0:T(4,128)(2,1)S(1)} %get-tuple-element.107), channel_id=1, source_target_pairs={{1,0},{2,1},{3,2},{4,3},{5,4},{6,5},{7,6},{8,7},{9,8},{10,9},{11,1... | collective-permute-start | bytes 221192 | tf_op jit(solution)/shard_map/ppermute | solution.py:98
  69.4 4.3 %collective-permute-start.9 = (bf16[16,3,768]{2,1,0:T(4,128)(2,1)S(1)}, bf16[16,3,768]{2,1,0:T(4,128)(2,1)S(1)}, u32[]{:S(2)}, u32[]{:S(2)}) collective-permute-start(bf16[16,3,768]{2,1,0:T(4,128)(2,1)S(1)} %get-tuple-element.106), channel_id=1, source_target_pairs={{0,1},{1,2},{2,3},{3,4},{4,5},{5,6},{6,7},{7,8},{8,9},{9,10},{10,1... | collective-permute-start | bytes 221192 | tf_op jit(solution)/shard_map/ppermute | solution.py:98
  75.7 8.3 %chunks.1 = (bf16[800,768]{1,0:T(8,128)(2,1)S(1)}, bf16[800,768]{1,0:T(8,128)(2,1)S(1)}, bf16[800,768]{1,0:T(8,128)(2,1)S(1)}, bf16[800,768]{1,0:T(8,128)(2,1)S(1)}) custom-call(s32[3]{0:T(128)S(1)} %pad_add_fusion.at_ref, bf16[384,3072]{1,0:T(8,128)(2,1)S(1)} %copy-done.4, bf16[384,3072]{1,0:T(8,128)(2,1)S(1)} %copy-done.2, ...), custom_call_target="tpu_custom_call" | custom-call | flops 1811939328 | bytes 18874368 | tf_op jit(solution)/shard_map/chunks/pallas_call | solution.py:286
  88.2 3.2 %collective-permute-start.12 = (bf16[3,30,768]{2,1,0:T(8,128)(2,1)S(1)}, bf16[3,30,768]{2,1,0:T(8,128)(2,1)S(1)}, u32[]{:S(2)}, u32[]{:S(2)}) collective-permute-start(bf16[3,30,768]{2,1,0:T(8,128)(2,1)S(1)} %get-tuple-element.99), channel_id=1, source_target_pairs={{0,32},{32,64},{64,96},{96,128},{128,160},{160,192},{192,224},{1,3... | collective-permute-start | bytes 414728 | tf_op jit(solution)/shard_map/ppermute | solution.py:98
  92.8 2.2 %collective-permute-start.6 = (bf16[800,768]{1,0:T(8,128)(2,1)}, bf16[800,768]{1,0:T(8,128)(2,1)S(1)}, u32[]{:S(2)}, u32[]{:S(2)}) collective-permute-start(bf16[800,768]{1,0:T(8,128)(2,1)} %copy-done.9), channel_id=1, source_target_pairs={{0,2},{1,33},{2,4},{3,35},{4,6},{5,37},{6,0},{7,39},{8,10},{9,41},... | collective-permute-start | bytes 3686408 | tf_op jit(solution)/shard_map/ppermute | solution.py:58
  94.9 4.7 %collective-permute-start.7 = (bf16[800,768]{1,0:T(8,128)(2,1)}, bf16[800,768]{1,0:T(8,128)(2,1)S(1)}, u32[]{:S(2)}, u32[]{:S(2)}) collective-permute-start(bf16[800,768]{1,0:T(8,128)(2,1)} %copy-done.8), channel_id=1, source_target_pairs={{0,4},{1,65},{2,6},{3,67},{4,0},{5,69},{6,2},{7,71},{8,12},{9,73},... | collective-permute-start | bytes 3686408 | tf_op jit(solution)/shard_map/ppermute | solution.py:58
  101.3 9.4 %multiply_add_fusion = f32[16,24,768]{2,1,0:T(8,128)} fusion(bf16[19,30,768]{2,1,0:T(8,128)(2,1)S(1)} %get-tuple-element.101, bf16[19,30,768]{2,1,0:T(8,128)(2,1)S(1)} %constant_dynamic-update-slice_fusion.2, bf16[16,30,768]{2,1,0:T(8,128)(2,1)S(1)} %pad_maximum_fusion.2, f32[768]{0:T(1024)S(1)} %copy-done.72, f32[768]{0:T(1024)S(1)} %copy-done.74, ...), kind=kLoop, calls=%fused_computation.22 | loop fusion | flops 43646976 | bytes 30821376 | tf_op jit(solution)/shard_map/add | solution.py:379
  110.7 2.4 %collective-permute-done.6 = bf16[800,768]{1,0:T(8,128)(2,1)S(1)} collective-permute-done((bf16[800,768]{1,0:T(8,128)(2,1)}, bf16[800,768]{1,0:T(8,128)(2,1)S(1)}, u32[]{:S(2)}, u32[]{:S(2)}) %collective-permute-start.6) | collective-permute-done | bytes 1228832 | tf_op jit(solution)/shard_map/ppermute | solution.py:58
  113.1 14.3 %collective-permute-done.7 = bf16[800,768]{1,0:T(8,128)(2,1)S(1)} collective-permute-done((bf16[800,768]{1,0:T(8,128)(2,1)}, bf16[800,768]{1,0:T(8,128)(2,1)S(1)}, u32[]{:S(2)}, u32[]{:S(2)}) %collective-permute-start.7) | collective-permute-done | bytes 1228832 | tf_op jit(solution)/shard_map/ppermute | solution.py:58
  127.4 1.4 collective-permute-done.8
  130.0 1.7 collective-permute-start.13
  131.8 8.3 %collective-permute-start.14 = (bf16[224,768]{1,0:T(8,128)(2,1)S(1)}, bf16[224,768]{1,0:T(8,128)(2,1)S(1)}, u32[]{:S(2)}, u32[]{:S(2)}) collective-permute-start(bf16[224,768]{1,0:T(8,128)(2,1)S(1)} %get-tuple-element.123), channel_id=1, source_target_pairs={{0,64},{1,5},{2,66},{3,7},{4,68},{5,1},{6,70},{7,3},{8,72},{9,13},... | collective-permute-start | bytes 1032200 | tf_op jit(solution)/shard_map/ppermute | solution.py:58
  140.1 3.7 %collective-permute-done.13 = bf16[224,768]{1,0:T(8,128)(2,1)S(1)} collective-permute-done((bf16[224,768]{1,0:T(8,128)(2,1)S(1)}, bf16[224,768]{1,0:T(8,128)(2,1)S(1)}, u32[]{:S(2)}, u32[]{:S(2)}) %collective-permute-start.13) | collective-permute-done | bytes 344096 | tf_op jit(solution)/shard_map/ppermute | solution.py:58
  143.8 4.9 %collective-permute-done.14 = bf16[224,768]{1,0:T(8,128)(2,1)S(1)} collective-permute-done((bf16[224,768]{1,0:T(8,128)(2,1)S(1)}, bf16[224,768]{1,0:T(8,128)(2,1)S(1)}, u32[]{:S(2)}, u32[]{:S(2)}) %collective-permute-start.14) | collective-permute-done | bytes 344096 | tf_op jit(solution)/shard_map/ppermute | solution.py:58
  149.5 5.1 %collective-permute-done.16 = bf16[128,768]{1,0:T(8,128)(2,1)S(1)} collective-permute-done((bf16[128,768]{1,0:T(8,128)(2,1)S(1)}, bf16[128,768]{1,0:T(8,128)(2,1)S(1)}, u32[]{:S(2)}, u32[]{:S(2)}) %collective-permute-start.16) | collective-permute-done | bytes 196640 | tf_op jit(solution)/shard_map/ppermute | solution.py:78
  154.7 6.8 %collective-permute-start.17 = (bf16[56,768]{1,0:T(8,128)(2,1)S(1)}, bf16[56,768]{1,0:T(8,128)(2,1)S(1)}, u32[]{:S(2)}, u32[]{:S(2)}) collective-permute-start(bf16[56,768]{1,0:T(8,128)(2,1)S(1)} %get-tuple-element.119), channel_id=1, source_target_pairs={{0,8},{8,16},{16,24},{24,0},{1,9},{9,17},{17,25},{25,1},{2,10},{10... | collective-permute-start | bytes 258056 | tf_op jit(solution)/shard_map/ppermute | solution.py:86
  162.1 3.5 %collective-permute-start.19 = (bf16[56,768]{1,0:T(8,128)(2,1)S(1)}, bf16[56,768]{1,0:T(8,128)(2,1)S(1)}, u32[]{:S(2)}, u32[]{:S(2)}) collective-permute-start(bf16[56,768]{1,0:T(8,128)(2,1)S(1)} %get-tuple-element.121), channel_id=1, source_target_pairs={{0,24},{8,0},{16,8},{24,16},{1,25},{9,1},{17,9},{25,17},{2,26},{10... | collective-permute-start | bytes 258056 | tf_op jit(solution)/shard_map/ppermute | solution.py:86
  165.5 4.1 %collective-permute-done.18 = bf16[56,768]{1,0:T(8,128)(2,1)S(1)} collective-permute-done((bf16[56,768]{1,0:T(8,128)(2,1)S(1)}, bf16[56,768]{1,0:T(8,128)(2,1)S(1)}, u32[]{:S(2)}, u32[]{:S(2)}) %collective-permute-start.18) | collective-permute-done | bytes 86048 | tf_op jit(solution)/shard_map/ppermute | solution.py:86
  169.8 12.1 %collective-permute-start.20 = (f32[44,768]{1,0:T(8,128)S(1)}, f32[44,768]{1,0:T(8,128)S(1)}, u32[]{:S(2)}, u32[]{:S(2)}) collective-permute-start(f32[44,768]{1,0:T(8,128)S(1)} %pad_maximum_fusion.12), channel_id=1, source_target_pairs={{0,1},{1,0},{2,3},{3,2},{4,5},{5,4},{6,7},{7,6},{8,9},{9,8},{10,11... | collective-permute-start | bytes 405512 | tf_op jit(solution)/shard_map/ppermute | solution.py:93
  (249 shorter events, 23.2 us)
Async XLA Ops:
  1.9 8.9 %collective-permute-start = (bf16[16,3,768]{2,1,0:T(4,128)(2,1)S(1)}, bf16[16,3,768]{2,1,0:T(4,128)(2,1)S(1)}, u32[]{:S(2)}, u32[]{:S(2)}) collective-permute-start(bf16[16,3,768]{2,1,0:T(4,128)(2,1)S(1)} %get-tuple-element.108), channel_id=1, source_target_pairs={{0,1},{1,2},{2,3},{3,4},{4,5},{5,6},{6,7},{7,8},{8,9},{9,10},{10,1... | collective-permute-start | bytes 221192 | tf_op jit(solution)/shard_map/ppermute | solution.py:98
  6.4 6.1 %collective-permute-start.1 = (bf16[16,3,768]{2,1,0:T(4,128)(2,1)S(1)}, bf16[16,3,768]{2,1,0:T(4,128)(2,1)S(1)}, u32[]{:S(2)}, u32[]{:S(2)}) collective-permute-start(bf16[16,3,768]{2,1,0:T(4,128)(2,1)S(1)} %get-tuple-element.109), channel_id=1, source_target_pairs={{1,0},{2,1},{3,2},{4,3},{5,4},{6,5},{7,6},{8,7},{9,8},{10,9},{11,1... | collective-permute-start | bytes 221192 | tf_op jit(solution)/shard_map/ppermute | solution.py:98
  9.8 12.3 %copy-start.13 = (f32[768]{0:T(1024)}, f32[768]{0:T(1024)S(1)}, u32[]{:S(2)}) copy-start(f32[768]{0:T(1024)S(1)} %get-tuple-element.71) | copy-start | bytes 9220
  10.6 11.5 %copy-start.15 = (f32[768]{0:T(1024)}, f32[768]{0:T(1024)S(1)}, u32[]{:S(2)}) copy-start(f32[768]{0:T(1024)S(1)} %get-tuple-element.34) | copy-start | bytes 9220
  10.7 11.5 %copy-start.17 = (f32[768]{0:T(1024)}, f32[768]{0:T(1024)S(1)}, u32[]{:S(2)}) copy-start(f32[768]{0:T(1024)S(1)} %get-tuple-element.35) | copy-start | bytes 9220
  10.7 11.5 %copy-start.19 = (f32[768]{0:T(1024)}, f32[768]{0:T(1024)S(1)}, u32[]{:S(2)}) copy-start(f32[768]{0:T(1024)S(1)} %get-tuple-element.36) | copy-start | bytes 9220
  10.7 11.5 %copy-start.21 = (f32[768]{0:T(1024)}, f32[768]{0:T(1024)S(1)}, u32[]{:S(2)}) copy-start(f32[768]{0:T(1024)S(1)} %get-tuple-element.37) | copy-start | bytes 9220
  10.7 11.5 %copy-start.23 = (f32[768]{0:T(1024)}, f32[768]{0:T(1024)S(1)}, u32[]{:S(2)}) copy-start(f32[768]{0:T(1024)S(1)} %get-tuple-element.38) | copy-start | bytes 9220
  10.7 11.5 %copy-start.25 = (f32[768]{0:T(1024)}, f32[768]{0:T(1024)S(1)}, u32[]{:S(2)}) copy-start(f32[768]{0:T(1024)S(1)} %get-tuple-element.39) | copy-start | bytes 9220
  10.7 11.5 %copy-start.27 = (f32[768]{0:T(1024)}, f32[768]{0:T(1024)S(1)}, u32[]{:S(2)}) copy-start(f32[768]{0:T(1024)S(1)} %get-tuple-element.40) | copy-start | bytes 9220
  10.7 11.5 %copy-start.29 = (f32[768]{0:T(1024)}, f32[768]{0:T(1024)S(1)}, u32[]{:S(2)}) copy-start(f32[768]{0:T(1024)S(1)} %get-tuple-element.41) | copy-start | bytes 9220
  10.7 11.5 %copy-start.31 = (f32[768]{0:T(1024)}, f32[768]{0:T(1024)S(1)}, u32[]{:S(2)}) copy-start(f32[768]{0:T(1024)S(1)} %get-tuple-element.42) | copy-start | bytes 9220
  12.6 5.5 %collective-permute-start.2 = (bf16[3,30,768]{2,1,0:T(8,128)(2,1)S(1)}, bf16[3,30,768]{2,1,0:T(8,128)(2,1)S(1)}, u32[]{:S(2)}, u32[]{:S(2)}) collective-permute-start(bf16[3,30,768]{2,1,0:T(8,128)(2,1)S(1)} %get-tuple-element.104), channel_id=1, source_target_pairs={{0,32},{32,64},{64,96},{96,128},{128,160},{160,192},{192,224},{1,3... | collective-permute-start | bytes 414728 | tf_op jit(solution)/shard_map/ppermute | solution.py:98
  15.8 5.9 %collective-permute-start.3 = (bf16[3,30,768]{2,1,0:T(8,128)(2,1)S(1)}, bf16[3,30,768]{2,1,0:T(8,128)(2,1)S(1)}, u32[]{:S(2)}, u32[]{:S(2)}) collective-permute-start(bf16[3,30,768]{2,1,0:T(8,128)(2,1)S(1)} %get-tuple-element.105), channel_id=1, source_target_pairs={{32,0},{64,32},{96,64},{128,96},{160,128},{192,160},{224,192},{33,... | collective-permute-start | bytes 414728 | tf_op jit(solution)/shard_map/ppermute | solution.py:98
  47.9 27.8 %collective-permute-start.4 = (bf16[3072,768]{1,0:T(8,128)(2,1)}, bf16[3072,768]{1,0:T(8,128)(2,1)}, u32[]{:S(2)}, u32[]{:S(2)}) collective-permute-start(bf16[3072,768]{1,0:T(8,128)(2,1)} %convolution_convert_fusion), channel_id=1, source_target_pairs={{0,1},{1,0},{2,3},{3,2},{4,5},{5,4},{6,7},{7,6},{8,9},{9,8},{10,11... | collective-permute-start | bytes 14155784 | tf_op jit(solution)/shard_map/ppermute | solution.py:93
  66.9 7.2 %collective-permute-start.10 = (bf16[16,3,768]{2,1,0:T(4,128)(2,1)S(1)}, bf16[16,3,768]{2,1,0:T(4,128)(2,1)S(1)}, u32[]{:S(2)}, u32[]{:S(2)}) collective-permute-start(bf16[16,3,768]{2,1,0:T(4,128)(2,1)S(1)} %get-tuple-element.107), channel_id=1, source_target_pairs={{1,0},{2,1},{3,2},{4,3},{5,4},{6,5},{7,6},{8,7},{9,8},{10,9},{11,1... | collective-permute-start | bytes 221192 | tf_op jit(solution)/shard_map/ppermute | solution.py:98
  69.4 5.9 %collective-permute-start.9 = (bf16[16,3,768]{2,1,0:T(4,128)(2,1)S(1)}, bf16[16,3,768]{2,1,0:T(4,128)(2,1)S(1)}, u32[]{:S(2)}, u32[]{:S(2)}) collective-permute-start(bf16[16,3,768]{2,1,0:T(4,128)(2,1)S(1)} %get-tuple-element.106), channel_id=1, source_target_pairs={{0,1},{1,2},{2,3},{3,4},{4,5},{5,6},{6,7},{7,8},{8,9},{9,10},{10,1... | collective-permute-start | bytes 221192 | tf_op jit(solution)/shard_map/ppermute | solution.py:98
  73.7 2.0 %collective-permute-start.5 = (f32[32,768]{1,0:T(8,128)S(1)}, f32[32,768]{1,0:T(8,128)S(1)}, u32[]{:S(2)}, u32[]{:S(2)}) collective-permute-start(f32[32,768]{1,0:T(8,128)S(1)} %slice_select_fusion.2), channel_id=1, source_target_pairs={{0,1},{1,0},{2,3},{3,2},{4,5},{5,4},{6,7},{7,6},{8,9},{9,8},{10,11... | collective-permute-start | bytes 294920 | tf_op jit(solution)/shard_map/ppermute | solution.py:93
  88.2 12.1 %collective-permute-start.12 = (bf16[3,30,768]{2,1,0:T(8,128)(2,1)S(1)}, bf16[3,30,768]{2,1,0:T(8,128)(2,1)S(1)}, u32[]{:S(2)}, u32[]{:S(2)}) collective-permute-start(bf16[3,30,768]{2,1,0:T(8,128)(2,1)S(1)} %get-tuple-element.99), channel_id=1, source_target_pairs={{0,32},{32,64},{64,96},{96,128},{128,160},{160,192},{192,224},{1,3... | collective-permute-start | bytes 414728 | tf_op jit(solution)/shard_map/ppermute | solution.py:98
  91.5 9.3 %collective-permute-start.11 = (bf16[3,30,768]{2,1,0:T(8,128)(2,1)S(1)}, bf16[3,30,768]{2,1,0:T(8,128)(2,1)S(1)}, u32[]{:S(2)}, u32[]{:S(2)}) collective-permute-start(bf16[3,30,768]{2,1,0:T(8,128)(2,1)S(1)} %get-tuple-element.98), channel_id=1, source_target_pairs={{32,0},{64,32},{96,64},{128,96},{160,128},{192,160},{224,192},{33,... | collective-permute-start | bytes 414728 | tf_op jit(solution)/shard_map/ppermute | solution.py:98
  92.8 20.3 %collective-permute-start.6 = (bf16[800,768]{1,0:T(8,128)(2,1)}, bf16[800,768]{1,0:T(8,128)(2,1)S(1)}, u32[]{:S(2)}, u32[]{:S(2)}) collective-permute-start(bf16[800,768]{1,0:T(8,128)(2,1)} %copy-done.9), channel_id=1, source_target_pairs={{0,2},{1,33},{2,4},{3,35},{4,6},{5,37},{6,0},{7,39},{8,10},{9,41},... | collective-permute-start | bytes 3686408 | tf_op jit(solution)/shard_map/ppermute | solution.py:58
  94.9 32.5 %collective-permute-start.7 = (bf16[800,768]{1,0:T(8,128)(2,1)}, bf16[800,768]{1,0:T(8,128)(2,1)S(1)}, u32[]{:S(2)}, u32[]{:S(2)}) collective-permute-start(bf16[800,768]{1,0:T(8,128)(2,1)} %copy-done.8), channel_id=1, source_target_pairs={{0,4},{1,65},{2,6},{3,67},{4,0},{5,69},{6,2},{7,71},{8,12},{9,73},... | collective-permute-start | bytes 3686408 | tf_op jit(solution)/shard_map/ppermute | solution.py:58
  99.7 29.2 %collective-permute-start.8 = (bf16[800,768]{1,0:T(8,128)(2,1)}, bf16[800,768]{1,0:T(8,128)(2,1)S(1)}, u32[]{:S(2)}, u32[]{:S(2)}) collective-permute-start(bf16[800,768]{1,0:T(8,128)(2,1)} %copy-done.7), channel_id=1, source_target_pairs={{0,6},{1,97},{2,0},{3,99},{4,2},{5,101},{6,4},{7,103},{8,14},{9,10... | collective-permute-start | bytes 3686408 | tf_op jit(solution)/shard_map/ppermute | solution.py:58
  101.3 27.6 %copy-start.6 = (bf16[800,768]{1,0:T(8,128)(2,1)S(1)}, bf16[800,768]{1,0:T(8,128)(2,1)}, u32[]{:S(2)}) copy-start(bf16[800,768]{1,0:T(8,128)(2,1)} %copy-done.5) | copy-start | bytes 3686404
  130.0 13.8 %collective-permute-start.13 = (bf16[224,768]{1,0:T(8,128)(2,1)S(1)}, bf16[224,768]{1,0:T(8,128)(2,1)S(1)}, u32[]{:S(2)}, u32[]{:S(2)}) collective-permute-start(bf16[224,768]{1,0:T(8,128)(2,1)S(1)} %get-tuple-element.122), channel_id=1, source_target_pairs={{0,32},{1,3},{2,34},{3,5},{4,36},{5,7},{6,38},{7,1},{8,40},{9,11},... | collective-permute-start | bytes 1032200 | tf_op jit(solution)/shard_map/ppermute | solution.py:58
  131.8 16.9 %collective-permute-start.14 = (bf16[224,768]{1,0:T(8,128)(2,1)S(1)}, bf16[224,768]{1,0:T(8,128)(2,1)S(1)}, u32[]{:S(2)}, u32[]{:S(2)}) collective-permute-start(bf16[224,768]{1,0:T(8,128)(2,1)S(1)} %get-tuple-element.123), channel_id=1, source_target_pairs={{0,64},{1,5},{2,66},{3,7},{4,68},{5,1},{6,70},{7,3},{8,72},{9,13},... | collective-permute-start | bytes 1032200 | tf_op jit(solution)/shard_map/ppermute | solution.py:58
  140.1 8.6 %collective-permute-start.15 = (bf16[224,768]{1,0:T(8,128)(2,1)S(1)}, bf16[224,768]{1,0:T(8,128)(2,1)S(1)}, u32[]{:S(2)}, u32[]{:S(2)}) collective-permute-start(bf16[224,768]{1,0:T(8,128)(2,1)S(1)} %get-tuple-element.124), channel_id=1, source_target_pairs={{0,96},{1,7},{2,98},{3,1},{4,100},{5,3},{6,102},{7,5},{8,104},{9,1... | collective-permute-start | bytes 1032200 | tf_op jit(solution)/shard_map/ppermute | solution.py:58
  149.0 5.6 %collective-permute-start.16 = (bf16[128,768]{1,0:T(8,128)(2,1)S(1)}, bf16[128,768]{1,0:T(8,128)(2,1)S(1)}, u32[]{:S(2)}, u32[]{:S(2)}) collective-permute-start(bf16[128,768]{1,0:T(8,128)(2,1)S(1)} %pad_maximum_fusion.7), channel_id=1, source_target_pairs={{0,128},{128,0},{1,129},{129,1},{2,130},{130,2},{3,131},{131,3},{4... | collective-permute-start | bytes 589832 | tf_op jit(solution)/shard_map/ppermute | solution.py:78
  154.7 10.8 %collective-permute-start.17 = (bf16[56,768]{1,0:T(8,128)(2,1)S(1)}, bf16[56,768]{1,0:T(8,128)(2,1)S(1)}, u32[]{:S(2)}, u32[]{:S(2)}) collective-permute-start(bf16[56,768]{1,0:T(8,128)(2,1)S(1)} %get-tuple-element.119), channel_id=1, source_target_pairs={{0,8},{8,16},{16,24},{24,0},{1,9},{9,17},{17,25},{25,1},{2,10},{10... | collective-permute-start | bytes 258056 | tf_op jit(solution)/shard_map/ppermute | solution.py:86
  161.5 8.1 %collective-permute-start.18 = (bf16[56,768]{1,0:T(8,128)(2,1)S(1)}, bf16[56,768]{1,0:T(8,128)(2,1)S(1)}, u32[]{:S(2)}, u32[]{:S(2)}) collective-permute-start(bf16[56,768]{1,0:T(8,128)(2,1)S(1)} %get-tuple-element.120), channel_id=1, source_target_pairs={{0,16},{8,24},{16,0},{24,8},{1,17},{9,25},{17,1},{25,9},{2,18},{10... | collective-permute-start | bytes 258056 | tf_op jit(solution)/shard_map/ppermute | solution.py:86
  162.1 7.6 %collective-permute-start.19 = (bf16[56,768]{1,0:T(8,128)(2,1)S(1)}, bf16[56,768]{1,0:T(8,128)(2,1)S(1)}, u32[]{:S(2)}, u32[]{:S(2)}) collective-permute-start(bf16[56,768]{1,0:T(8,128)(2,1)S(1)} %get-tuple-element.121), channel_id=1, source_target_pairs={{0,24},{8,0},{16,8},{24,16},{1,25},{9,1},{17,9},{25,17},{2,26},{10... | collective-permute-start | bytes 258056 | tf_op jit(solution)/shard_map/ppermute | solution.py:86
  169.8 13.2 %collective-permute-start.20 = (f32[44,768]{1,0:T(8,128)S(1)}, f32[44,768]{1,0:T(8,128)S(1)}, u32[]{:S(2)}, u32[]{:S(2)}) collective-permute-start(f32[44,768]{1,0:T(8,128)S(1)} %pad_maximum_fusion.12), channel_id=1, source_target_pairs={{0,1},{1,0},{2,3},{3,2},{4,5},{5,4},{6,7},{7,6},{8,9},{9,8},{10,11... | collective-permute-start | bytes 405512 | tf_op jit(solution)/shard_map/ppermute | solution.py:93
  (75 other events, 215.2 us)

commit v2 on v1

--- a/solution.py
+++ b/solution.py
@@ -68,16 +68,23 @@
     return add(lambda v: v[count:]), add(lambda v: v[:count])
 
 
+def add_all(parts):
+    out = parts[0].astype(F32)
+    for v in parts[1:]:
+        out = out + v.astype(F32)
+    return out
+
+
 def z_sum(v, small):
     count, chans = small.shape
-    low = small.astype(BF)
     zl = lax.axis_index("zl")
     zh = lax.axis_index("zh")
     away = lax.dynamic_index_in_dim(v, 1 - zl, 0, False).reshape(-1, chans)
     near = lax.dynamic_index_in_dim(v, zl, 0, False).reshape(-1, chans)
-    got = lax.ppermute(jnp.concatenate([low, away], axis=0), "zl", [(0, 1), (1, 0)])
-    low = (low.astype(F32) + got[:count].astype(F32)).astype(BF)
-    v = (near.astype(F32) + got[count:].astype(F32)).astype(BF).reshape(v.shape[1:])
+    low = small.astype(BF)
+    got = zl_swap(away)
+    low = add_all([low] + split_move([low] * 4, ("x", "y"))).astype(BF)
+    v = (near.astype(F32) + got.astype(F32)).astype(BF).reshape(v.shape[1:])
     acc = lax.dynamic_index_in_dim(v, zh, 0, False).astype(F32)
     sums = low.astype(F32)
     for k in range(1, 4):
@@ -87,6 +94,10 @@
         sums = sums + got[:count].astype(F32)
         acc = acc + got[count:].astype(F32)
     return acc, sums
+
+
+def zl_swap(v):
+    return lax.ppermute(v, "zl", [(0, 1), (1, 0)])
 
 
 def core_swap(v):
@@ -225,26 +236,20 @@
     )(padded, conv_out, d_normed, branch, cotangent, sum_pre, params)
 
 
-def chunk_kernel(at_ref, pre_ref, hid_ref, normed_ref, db_ref, come_ref, low_ref, *outs):
+def chunk_kernel(at_ref, pre_ref, hid_ref, normed_ref, db_ref, come_ref, *outs):
     unit = hid_ref.shape[1] // 16
     core = at_ref[0]
     me = (at_ref[1], at_ref[2])
     group = pl.program_id(0)
-    count = low_ref.shape[0]
     first = core == 0
     lhs = jnp.where(first, pre_ref[...], hid_ref[...])
     rhs = jnp.where(first, normed_ref[...], db_ref[...])
     v = lax.dot_general(lhs, rhs, (((0,), (0,)), ((), ())), preferred_element_type=F32)
     v = v + come_ref[...].astype(F32)
 
-    @pl.when(group == 0)
-    def _():
-        for out in outs:
-            out[0:count, :] = low_ref[...]
-
     def store(k, row, value):
         value = value.astype(BF)
-        rows = pl.ds(pl.multiple_of(count + row, 16), 2 * unit)
+        rows = pl.ds(pl.multiple_of(row, 16), 2 * unit)
         for n in range(4):
 
             @pl.when(k == n)
@@ -272,17 +277,16 @@
                 store(k, ((group // 4) * 16 + t) * unit, v[t * unit : (t + 2) * unit])
 
 
-def chunks(d_pre, hidden, normed, d_branch, come, low):
+def chunks(d_pre, hidden, normed, d_branch, come):
     pixels, hid = hidden.shape
     chans = normed.shape[1]
-    count = low.shape[0]
     wide = hid // 8
     at = jnp.stack([lax.axis_index("c"), lax.axis_index("x"), lax.axis_index("y")]).astype(
         jnp.int32
     )
     whole = pl.BlockSpec((pixels, chans), lambda g: (0, 0))
     columns = pl.BlockSpec((pixels, wide), lambda g: (0, g))
-    rows = count + hid // 4
+    rows = hid // 4
     return pl.pallas_call(
         chunk_kernel,
         grid=(8,),
@@ -293,16 +297,15 @@
             whole,
             whole,
             pl.BlockSpec((wide, chans), lambda g: (g, 0)),
-            pl.BlockSpec((count, chans), lambda g: (0, 0)),
         ],
         out_specs=[pl.BlockSpec((rows, chans), lambda g: (0, 0))] * 4,
-        out_shape=[jax.ShapeDtypeStruct((rows, chans), BF)] * 4,
+        out_shape=[pltpu.HBM((rows, chans), BF)] * 4,
         compiler_params=pltpu.CompilerParams(vmem_limit_bytes=40 * 1024 * 1024),
         cost_estimate=pl.CostEstimate(
             flops=2 * pixels * hid * chans, bytes_accessed=18 * 1024 * 1024, transcendentals=0
         ),
         name="chunks",
-    )(at, d_pre, hidden, normed, d_branch, come, low)
+    )(at, d_pre, hidden, normed, d_branch, come)
 
 
 def on_device(
@@ -355,6 +358,10 @@
     sum_pre = jnp.sum(d_pre.astype(F32), axis=0).reshape(hid // chans, chans)
     params = jnp.stack([layernorm_gain, b_reduce, layer_scale] + [layer_scale] * 5)
     shape = (rows, cols, chans)
+
+    moved = list(chunks(d_pre, hidden, normed, d_branch, come))
+    got = split_move(moved, ("x", "y"))
+    d_normed, moved[0] = lax.optimization_barrier((d_normed, moved[0]))
     small, d_conv = backward(
         scale,
         padded,
@@ -368,23 +375,22 @@
     total = small.shape[0]
     lower, upper = small[: total // 2], small[total // 2 :]
     small = jnp.where(first, lower, upper) + core_swap(jnp.where(first, upper, lower))
-
-    moved = list(chunks(d_pre, hidden, normed, d_branch, come, small.astype(BF)))
-    wide = halo_columns(d_conv, 3)
-    wide, moved[0] = lax.optimization_barrier((wide, moved[0]))
-    d_pad = halo_rows(wide, 3)
+    low = small.astype(BF)
+    small = low.astype(F32) + zl_swap(low).astype(F32)
+    d_pad = halo_rows(halo_columns(d_conv, 3), 3)
+    got, small, d_pad = lax.optimization_barrier((got, small, d_pad))
+    term = add_all([moved[0]] + got).astype(BF).reshape(2, 4, 4, 2 * per, chans)
+
+    moved = split_send(term, small, ("y", "x"), (1, 2))
+    got = split_move(moved, ("y", "x"))
     grad_image = cotangent.astype(F32)
     for i in range(KS):
         for j in range(KS):
             grad_image = grad_image + conv_weight[i, j] * d_pad[
                 6 - i : 6 - i + rows, 6 - j : 6 - j + cols
             ].astype(F32)
-    got = split_move(moved, ("x", "y"))
     got, grad_image = lax.optimization_barrier((got, grad_image))
     term, small = split_add(moved, got, small.shape[0])
-    term = term.astype(BF).reshape(2, 4, 4, 2 * per, chans)
-    moved = split_send(term, small, ("y", "x"), (1, 2))
-    term, small = split_add(moved, split_move(moved, ("y", "x")), small.shape[0])
     term = term.astype(BF).reshape(2, 4, 2 * per, chans)
     term, small = z_sum(term, small)
     term = term * scale

time: 186 us -> 164 us (0.88)
  starting transfers between devices: 63.5 us -> 52.3 us
  waiting for transfers between devices: 43.8 us -> 34.9 us
  local copies, waits for them, and re-layouts: 12.7 us -> 7.9 us
  Pallas kernels: 17.3 us -> 19.5 us
    ppermute x6 -> x9, waiting for transfers between devices: 26.8 us -> 1.57 us  [split_move(): lax.ppermute(moved[k], AXES, core_pairs(k, lead))]
    ppermute x8, waiting for transfers between devices: 6.81 us -> 20.5 us  [shift(): lax.ppermute(v, axes, [(i, i + d) for i in range(n) if 0 <= i + d < n])]
    ppermute x3, starting transfers between devices: 12.2 us -> 4.27 us  [core_swap(): return lax.ppermute(v, 'c', [(0, 1), (1, 0)])]
    ppermute x3, starting transfers between devices: 10.8 us -> 5.27 us  [z_sum(): got = lax.ppermute(sent, 'zh', [(i, (i + k) % 4) for i in range(4)])]
    unnamed x175 -> x165, local copies, waits for them, and re-layouts: 6.6 us -> 1.84 us
    ppermute x3, waiting for transfers between devices: 4.13 us -> 7.67 us  [z_sum(): got = lax.ppermute(sent, 'zh', [(i, (i + k) % 4) for i in range(4)])]
    pallas_call x1, Pallas kernels: 8.26 us -> 10.4 us  [chunks(): pl.pallas_call(chunk_kernel, grid=(8,), in_specs=[pl.BlockSpec(memory_spa...]
    ppermute x6 -> x9, starting transfers between devices: 17.6 us -> 19.5 us  [split_move(): lax.ppermute(moved[k], AXES, core_pairs(k, lead))]
  transfers between devices with their start and end apart: 21 -> 25, of which waited for: 12 -> 12; matrix products, arithmetic and copies ran while one was open for 12% -> 14% of each run, Pallas kernels for 5% -> 6%
where the time goes in v2:
time: 164 us; the launch traced here: 163 us
  starting transfers between devices  52.3 us (32%)
  waiting for transfers between devices  34.9 us (21%)
  other arithmetic  25.6 us (16%)
  matrix products  20.7 us (13%)
  Pallas kernels  19.5 us (12%)
  local copies, waits for them, and re-layouts  7.9 us (5%)
  between operations  2.37 us (1%)
    ppermute x8, starting transfers between devices, shift(): lax.ppermute(v, axes, [(i, i + d) for i in range(n) if 0 <= i + d < n])  21.2 us
    ppermute x8, waiting for transfers between devices, shift(): lax.ppermute(v, axes, [(i, i + d) for i in range(n) if 0 <= i + d < n])  20.5 us
    ppermute x9, starting transfers between devices, split_move(): lax.ppermute(moved[k], AXES, core_pairs(k, lead))  19.5 us
    reduce_sum x1, other arithmetic, on_device(): channel_mean = jnp.mean(flat, axis=-1, keepdims=True)  10.8 us
    pallas_call x1, Pallas kernels, chunks(): pl.pallas_call(chunk_kernel, grid=(8,), in_specs=[pl.BlockSpec(memory_spa...  10.4 us
    add x1, other arithmetic, on_device(): grad_image + conv_weight[i, j] * d_pad[6 - i:6 - i + rows, 6 - j:6 - j +...  9.41 us
    pallas_call x1, Pallas kernels, backward(): pl.pallas_call(functools.partial(backward_kernel, scale), out_shape=(jax....  9.07 us
    ppermute x3, waiting for transfers between devices, z_sum(): got = lax.ppermute(sent, 'zh', [(i, (i + k) % 4) for i in range(4)])  7.67 us
  transfers between devices with their start and end apart: 25, of which 12 were waited for; matrix products, arithmetic and copies ran while one was open for 14% of the time, Pallas kernels for 6%

profile of v2, /device:TPU:1, one launch (start us, length us, event | category | flops | bytes accessed | tf_op | source)
XLA Modules:
  0.0 163.3 jit_solution(1532970431768448897)
XLA Ops:
  1.9 4.5 %collective-permute-start = (bf16[16,3,768]{2,1,0:T(4,128)(2,1)S(1)}, bf16[16,3,768]{2,1,0:T(4,128)(2,1)S(1)}, u32[]{:S(2)}, u32[]{:S(2)}) collective-permute-start(bf16[16,3,768]{2,1,0:T(4,128)(2,1)S(1)} %get-tuple-element.116), channel_id=1, source_target_pairs={{0,1},{1,2},{2,3},{3,4},{4,5},{5,6},{6,7},{7,8},{8,9},{9,10},{10,1... | collective-permute-start | bytes 221192 | tf_op jit(solution)/shard_map/ppermute | solution.py:109
  6.4 2.1 %collective-permute-start.1 = (bf16[16,3,768]{2,1,0:T(4,128)(2,1)S(1)}, bf16[16,3,768]{2,1,0:T(4,128)(2,1)S(1)}, u32[]{:S(2)}, u32[]{:S(2)}) collective-permute-start(bf16[16,3,768]{2,1,0:T(4,128)(2,1)S(1)} %get-tuple-element.117), channel_id=1, source_target_pairs={{1,0},{2,1},{3,2},{4,3},{5,4},{6,5},{7,6},{8,7},{9,8},{10,9},{11,1... | collective-permute-start | bytes 221192 | tf_op jit(solution)/shard_map/ppermute | solution.py:109
  10.7 1.7 %collective-permute-done.1 = bf16[16,3,768]{2,1,0:T(4,128)(2,1)S(1)} collective-permute-done((bf16[16,3,768]{2,1,0:T(4,128)(2,1)S(1)}, bf16[16,3,768]{2,1,0:T(4,128)(2,1)S(1)}, u32[]{:S(2)}, u32[]{:S(2)}) %collective-permute-start.1) | collective-permute-done | bytes 73760 | tf_op jit(solution)/shard_map/ppermute | solution.py:109
  12.6 3.2 %collective-permute-start.2 = (bf16[3,30,768]{2,1,0:T(8,128)(2,1)S(1)}, bf16[3,30,768]{2,1,0:T(8,128)(2,1)S(1)}, u32[]{:S(2)}, u32[]{:S(2)}) collective-permute-start(bf16[3,30,768]{2,1,0:T(8,128)(2,1)S(1)} %get-tuple-element.112), channel_id=1, source_target_pairs={{0,32},{32,64},{64,96},{96,128},{128,160},{160,192},{192,224},{1,3... | collective-permute-start | bytes 414728 | tf_op jit(solution)/shard_map/ppermute | solution.py:109
  18.1 3.6 %collective-permute-done.3 = bf16[3,30,768]{2,1,0:T(8,128)(2,1)S(1)} collective-permute-done((bf16[3,30,768]{2,1,0:T(8,128)(2,1)S(1)}, bf16[3,30,768]{2,1,0:T(8,128)(2,1)S(1)}, u32[]{:S(2)}, u32[]{:S(2)}) %collective-permute-start.3) | collective-permute-done | bytes 138272 | tf_op jit(solution)/shard_map/ppermute | solution.py:109
  22.4 10.8 %fusion.21 = (f32[16,24]{1,0:T(8,128)S(1)}, f32[16,24,768]{2,1,0:T(8,128)S(1)}) fusion(bf16[19,30,768]{2,1,0:T(8,128)(2,1)S(1)} %get-tuple-element.111, f32[768]{0:T(1024)S(1)} %copy-done.67, f32[768]{0:T(1024)S(1)} %copy-done.69, f32[768]{0:T(1024)S(1)} %get-tuple-element.45, f32[768]{0:T(1024)S(1)} %get-tuple-element.46, f32[768]{0:T(1024)S(1)} %get-tuple-element.47, ...), kind=kLoop, calls=%fused_computation.147 | loop fusion | flops 46300800 | bytes 28540416 | tf_op jit(solution)/shard_map/reduce_sum | solution.py:335
  34.3 4.8 %multiply_convert_fusion = (bf16[384,3072]{1,0:T(8,128)(2,1)S(1)}, f32[384,3072]{1,0:T(8,128)S(1)}) fusion(f32[3072]{0:T(1024)S(1)} %copy-done.77, bf16[384,768]{1,0:T(8,128)(2,1)S(1)} %fusion.11.normed_ref, bf16[3072,768]{1,0:T(8,128)(2,1)} %param.16), kind=kOutput, calls=%fused_computation.9 | convolution fusion | flops 1819017216 | bytes 12398592 | tf_op jit(solution)/shard_map/dot_general | solution.py:342
  39.1 4.2 %convert_reduce_fusion = (f32[3072]{0:T(1024)}, bf16[384,3072]{1,0:T(8,128)(2,1)S(1)}) fusion(f32[384,3072]{1,0:T(8,128)S(1)} %get-tuple-element.134, bf16[384,768]{1,0:T(8,128)(2,1)S(1)} %fusion.12.db_ref, bf16[768,3072]{1,0:T(8,128)(2,1)S(1)} %bitcast.88), kind=kOutput, calls=%fused_computation.8 | convolution fusion | flops 1826092032 | bytes 12398592 | tf_op jit(solution)/shard_map/dot_general | solution.py:349
  43.4 4.5 %convolution_convert_fusion = bf16[3072,768]{1,0:T(8,128)(2,1)} fusion(bf16[384,3072]{1,0:T(8,128)(2,1)S(1)} %get-tuple-element.133.hid_ref, bf16[384,3072]{1,0:T(8,128)(2,1)S(1)} %get-tuple-element.136.pre_ref, pred[]{:T(512)S(6)} %eq.2, bf16[384,768]{1,0:T(8,128)(2,1)S(1)} %fusion.12.db_ref, bf16[384,768]{1,0:T(8,128)(2,1)S(1)} %fusion.11.normed_ref), kind=kOutput, calls=%fused_computation.1 | convolution fusion | flops 1815773184 | bytes 10616833 | tf_op jit(solution)/shard_map/dot_general | solution.py:131
  48.9 1.6 pad_maximum_fusion.pad_ref
  50.6 5.2 %fusion.24 = f32[384,768]{1,0:T(8,128)S(1)} fusion(bf16[384,3072]{1,0:T(8,128)(2,1)} %copy-done.3, bf16[3072,768]{1,0:T(8,128)(2,1)} %param.16), kind=kOutput, calls=%fused_computation.150 | convolution fusion | flops 1811939328 | bytes 8257536 | tf_op jit(solution)/shard_map/dot_general | solution.py:357
  55.8 2.0 %fusion.25 = f32[384,768]{1,0:T(8,128)S(1)} fusion(bf16[384,3072]{1,0:T(8,128)(2,1)S(1)} %copy-done.2, bf16[768,3072]{1,0:T(8,128)(2,1)S(1)} %bitcast.90), kind=kOutput, calls=%fused_computation.151 | convolution fusion | flops 1811939328 | bytes 8257536 | tf_op jit(solution)/shard_map/dot_general | solution.py:354
  57.8 10.4 %chunks.1 = (bf16[768,768]{1,0:T(8,128)(2,1)}, bf16[768,768]{1,0:T(8,128)(2,1)}, bf16[768,768]{1,0:T(8,128)(2,1)}, bf16[768,768]{1,0:T(8,128)(2,1)}) custom-call(s32[3]{0:T(128)S(1)} %pad_add_fusion.at_ref, bf16[384,3072]{1,0:T(8,128)(2,1)S(1)} %copy-done.4, bf16[384,3072]{1,0:T(8,128)(2,1)S(1)} %copy-done.2, bf16[384,768]{1,0:T(8,128)(2,1)S(1)} %fusion.11.normed_ref, ...), custom_call_target="tpu_custom_call" | custom-call | flops 1811939328 | bytes 18874368 | tf_op jit(solution)/shard_map/chunks/pallas_call | solution.py:290
  69.5 4.7 %collective-permute-start.6 = (bf16[768,768]{1,0:T(8,128)(2,1)}, bf16[768,768]{1,0:T(8,128)(2,1)S(1)}, u32[]{:S(2)}, u32[]{:S(2)}) collective-permute-start(bf16[768,768]{1,0:T(8,128)(2,1)} %get-tuple-element.28), channel_id=1, source_target_pairs={{0,4},{1,65},{2,6},{3,67},{4,0},{5,69},{6,2},{7,71},{8,12},{9,73},... | collective-permute-start | bytes 3538952 | tf_op jit(solution)/shard_map/ppermute | solution.py:58
  74.3 9.1 %backward.1 = (f32[64,768]{1,0:T(8,128)S(1)}, bf16[16,24,768]{2,1,0:T(8,128)(2,1)S(1)}) custom-call(bf16[22,30,768]{2,1,0:T(8,128)(2,1)S(1)} %pad_maximum_fusion.pad_ref, f32[16,24,768]{2,1,0:T(8,128)S(1)} %get-tuple-element.99.conv_ref, f32[16,24,768]{2,1,0:T(8,128)S(1)} %bitcast.79, f32[16,24,768]{2,1,0:T(8,128)S(1)} %bitcast.80, ...), custom_call_target="tpu_custom_call" | custom-call | flops 28901376 | bytes 8388608 | tf_op jit(solution)/shard_map/backward/pallas_call | solution.py:220
  83.4 3.6 %collective-permute-start.8 = (f32[32,768]{1,0:T(8,128)S(1)}, f32[32,768]{1,0:T(8,128)S(1)}, u32[]{:S(2)}, u32[]{:S(2)}) collective-permute-start(f32[32,768]{1,0:T(8,128)S(1)} %slice_select_fusion.2), channel_id=1, source_target_pairs={{0,1},{1,0},{2,3},{3,2},{4,5},{5,4},{6,7},{7,6},{8,9},{9,8},{10,11... | collective-permute-start | bytes 294920 | tf_op jit(solution)/shard_map/ppermute | solution.py:104
  87.0 3.6 %collective-permute-start.10 = (bf16[16,3,768]{2,1,0:T(4,128)(2,1)S(1)}, bf16[16,3,768]{2,1,0:T(4,128)(2,1)S(1)}, u32[]{:S(2)}, u32[]{:S(2)}) collective-permute-start(bf16[16,3,768]{2,1,0:T(4,128)(2,1)S(1)} %get-tuple-element.114), channel_id=1, source_target_pairs={{0,1},{1,2},{2,3},{3,4},{4,5},{5,6},{6,7},{7,8},{8,9},{9,10},{10,1... | collective-permute-start | bytes 221192 | tf_op jit(solution)/shard_map/ppermute | solution.py:109
  90.6 1.9 %collective-permute-start.11 = (bf16[16,3,768]{2,1,0:T(4,128)(2,1)S(1)}, bf16[16,3,768]{2,1,0:T(4,128)(2,1)S(1)}, u32[]{:S(2)}, u32[]{:S(2)}) collective-permute-start(bf16[16,3,768]{2,1,0:T(4,128)(2,1)S(1)} %get-tuple-element.115), channel_id=1, source_target_pairs={{1,0},{2,1},{3,2},{4,3},{5,4},{6,5},{7,6},{8,7},{9,8},{10,9},{11,1... | collective-permute-start | bytes 221192 | tf_op jit(solution)/shard_map/ppermute | solution.py:109
  93.3 2.0 %collective-permute-start.9 = (bf16[32,768]{1,0:T(8,128)(2,1)S(1)}, bf16[32,768]{1,0:T(8,128)(2,1)S(1)}, u32[]{:S(2)}, u32[]{:S(2)}) collective-permute-start(bf16[32,768]{1,0:T(8,128)(2,1)S(1)} %add_convert_fusion.4), channel_id=1, source_target_pairs={{0,128},{128,0},{1,129},{129,1},{2,130},{130,2},{3,131},{131,3},{4... | collective-permute-start | bytes 147464 | tf_op jit(solution)/shard_map/ppermute | solution.py:100
  95.3 9.6 %collective-permute-done.11 = bf16[16,3,768]{2,1,0:T(4,128)(2,1)S(1)} collective-permute-done((bf16[16,3,768]{2,1,0:T(4,128)(2,1)S(1)}, bf16[16,3,768]{2,1,0:T(4,128)(2,1)S(1)}, u32[]{:S(2)}, u32[]{:S(2)}) %collective-permute-start.11) | collective-permute-done | bytes 73760 | tf_op jit(solution)/shard_map/ppermute | solution.py:109
  105.0 3.4 %collective-permute-start.12 = (bf16[3,30,768]{2,1,0:T(8,128)(2,1)S(1)}, bf16[3,30,768]{2,1,0:T(8,128)(2,1)S(1)}, u32[]{:S(2)}, u32[]{:S(2)}) collective-permute-start(bf16[3,30,768]{2,1,0:T(8,128)(2,1)S(1)} %get-tuple-element.108), channel_id=1, source_target_pairs={{0,32},{32,64},{64,96},{96,128},{128,160},{160,192},{192,224},{1,3... | collective-permute-start | bytes 414728 | tf_op jit(solution)/shard_map/ppermute | solution.py:109
  110.5 4.1 %collective-permute-done.13 = bf16[3,30,768]{2,1,0:T(8,128)(2,1)S(1)} collective-permute-done((bf16[3,30,768]{2,1,0:T(8,128)(2,1)S(1)}, bf16[3,30,768]{2,1,0:T(8,128)(2,1)S(1)}, u32[]{:S(2)}, u32[]{:S(2)}) %collective-permute-start.13) | collective-permute-done | bytes 138272 | tf_op jit(solution)/shard_map/ppermute | solution.py:109
  116.8 3.6 %collective-permute-start.15 = (bf16[224,768]{1,0:T(8,128)(2,1)S(1)}, bf16[224,768]{1,0:T(8,128)(2,1)S(1)}, u32[]{:S(2)}, u32[]{:S(2)}) collective-permute-start(bf16[224,768]{1,0:T(8,128)(2,1)S(1)} %get-tuple-element.132), channel_id=1, source_target_pairs={{0,64},{1,5},{2,66},{3,7},{4,68},{5,1},{6,70},{7,3},{8,72},{9,13},... | collective-permute-start | bytes 1032200 | tf_op jit(solution)/shard_map/ppermute | solution.py:58
  120.7 9.4 %multiply_add_fusion = f32[16,24,768]{2,1,0:T(8,128)} fusion(bf16[22,30,768]{2,1,0:T(8,128)(2,1)S(1)} %pad_maximum_fusion.1, f32[768]{0:T(1024)S(1)} %copy-done.68, f32[768]{0:T(1024)S(1)} %copy-done.70, f32[768]{0:T(1024)S(1)} %copy-done.14, f32[768]{0:T(1024)S(1)} %copy-done.16, f32[768]{0:T(1024)S(1)} %copy-done.18, f32[768]{0:T(1024)S(1)} %copy-done.20, ...), kind=kLoop, calls=%fused_computation.22 | loop fusion | flops 43646976 | bytes 30821376 | tf_op jit(solution)/shard_map/add | solution.py:389
  130.2 7.0 %collective-permute-start.18 = (bf16[32,768]{1,0:T(8,128)(2,1)S(1)}, bf16[32,768]{1,0:T(8,128)(2,1)S(1)}, u32[]{:S(2)}, u32[]{:S(2)}) collective-permute-start(bf16[32,768]{1,0:T(8,128)(2,1)S(1)} %add_convert_fusion.3), channel_id=1, source_target_pairs={{0,2},{1,33},{2,4},{3,35},{4,6},{5,37},{6,0},{7,39},{8,10},{9,41},... | collective-permute-start | bytes 147464 | tf_op jit(solution)/shard_map/ppermute | solution.py:58
  137.5 2.2 %collective-permute-start.20 = (bf16[32,768]{1,0:T(8,128)(2,1)S(1)}, bf16[32,768]{1,0:T(8,128)(2,1)S(1)}, u32[]{:S(2)}, u32[]{:S(2)}) collective-permute-start(bf16[32,768]{1,0:T(8,128)(2,1)S(1)} %add_convert_fusion.3), channel_id=1, source_target_pairs={{0,6},{1,97},{2,0},{3,99},{4,2},{5,101},{6,4},{7,103},{8,14},{9,10... | collective-permute-start | bytes 147464 | tf_op jit(solution)/shard_map/ppermute | solution.py:58
  140.1 1.5 collective-permute-done.19
  141.7 4.1 %collective-permute-done.17 = bf16[96,768]{1,0:T(8,128)(2,1)S(1)} collective-permute-done((bf16[96,768]{1,0:T(8,128)(2,1)S(1)}, bf16[96,768]{1,0:T(8,128)(2,1)S(1)}, u32[]{:S(2)}, u32[]{:S(2)}) %collective-permute-start.17) | collective-permute-done | bytes 147488 | tf_op jit(solution)/shard_map/ppermute | solution.py:100
  146.8 1.7 %collective-permute-start.22 = (bf16[56,768]{1,0:T(8,128)(2,1)S(1)}, bf16[56,768]{1,0:T(8,128)(2,1)S(1)}, u32[]{:S(2)}, u32[]{:S(2)}) collective-permute-start(bf16[56,768]{1,0:T(8,128)(2,1)S(1)} %get-tuple-element.128), channel_id=1, source_target_pairs={{0,16},{8,24},{16,0},{24,8},{1,17},{9,25},{17,1},{25,9},{2,18},{10... | collective-permute-start | bytes 258056 | tf_op jit(solution)/shard_map/ppermute | solution.py:93
  148.5 2.7 %collective-permute-start.23 = (bf16[56,768]{1,0:T(8,128)(2,1)S(1)}, bf16[56,768]{1,0:T(8,128)(2,1)S(1)}, u32[]{:S(2)}, u32[]{:S(2)}) collective-permute-start(bf16[56,768]{1,0:T(8,128)(2,1)S(1)} %get-tuple-element.129), channel_id=1, source_target_pairs={{0,24},{8,0},{16,8},{24,16},{1,25},{9,1},{17,9},{25,17},{2,26},{10... | collective-permute-start | bytes 258056 | tf_op jit(solution)/shard_map/ppermute | solution.py:93
  151.9 4.0 %collective-permute-done.22 = bf16[56,768]{1,0:T(8,128)(2,1)S(1)} collective-permute-done((bf16[56,768]{1,0:T(8,128)(2,1)S(1)}, bf16[56,768]{1,0:T(8,128)(2,1)S(1)}, u32[]{:S(2)}, u32[]{:S(2)}) %collective-permute-start.22) | collective-permute-done | bytes 86048 | tf_op jit(solution)/shard_map/ppermute | solution.py:93
  155.9 3.0 %collective-permute-done.23 = bf16[56,768]{1,0:T(8,128)(2,1)S(1)} collective-permute-done((bf16[56,768]{1,0:T(8,128)(2,1)S(1)}, bf16[56,768]{1,0:T(8,128)(2,1)S(1)}, u32[]{:S(2)}, u32[]{:S(2)}) %collective-permute-start.23) | collective-permute-done | bytes 86048 | tf_op jit(solution)/shard_map/ppermute | solution.py:93
  (245 shorter events, 21.1 us)
Async XLA Ops:
  1.9 8.9 %collective-permute-start = (bf16[16,3,768]{2,1,0:T(4,128)(2,1)S(1)}, bf16[16,3,768]{2,1,0:T(4,128)(2,1)S(1)}, u32[]{:S(2)}, u32[]{:S(2)}) collective-permute-start(bf16[16,3,768]{2,1,0:T(4,128)(2,1)S(1)} %get-tuple-element.116), channel_id=1, source_target_pairs={{0,1},{1,2},{2,3},{3,4},{4,5},{5,6},{6,7},{7,8},{8,9},{9,10},{10,1... | collective-permute-start | bytes 221192 | tf_op jit(solution)/shard_map/ppermute | solution.py:109
  6.4 6.1 %collective-permute-start.1 = (bf16[16,3,768]{2,1,0:T(4,128)(2,1)S(1)}, bf16[16,3,768]{2,1,0:T(4,128)(2,1)S(1)}, u32[]{:S(2)}, u32[]{:S(2)}) collective-permute-start(bf16[16,3,768]{2,1,0:T(4,128)(2,1)S(1)} %get-tuple-element.117), channel_id=1, source_target_pairs={{1,0},{2,1},{3,2},{4,3},{5,4},{6,5},{7,6},{8,7},{9,8},{10,9},{11,1... | collective-permute-start | bytes 221192 | tf_op jit(solution)/shard_map/ppermute | solution.py:109
  9.8 12.3 %copy-start.9 = (f32[768]{0:T(1024)}, f32[768]{0:T(1024)S(1)}, u32[]{:S(2)}) copy-start(f32[768]{0:T(1024)S(1)} %get-tuple-element.81) | copy-start | bytes 9220
  10.7 11.5 %copy-start.17 = (f32[768]{0:T(1024)}, f32[768]{0:T(1024)S(1)}, u32[]{:S(2)}) copy-start(f32[768]{0:T(1024)S(1)} %get-tuple-element.47) | copy-start | bytes 9220
  10.7 11.5 %copy-start.19 = (f32[768]{0:T(1024)}, f32[768]{0:T(1024)S(1)}, u32[]{:S(2)}) copy-start(f32[768]{0:T(1024)S(1)} %get-tuple-element.48) | copy-start | bytes 9220
  10.7 11.5 %copy-start.21 = (f32[768]{0:T(1024)}, f32[768]{0:T(1024)S(1)}, u32[]{:S(2)}) copy-start(f32[768]{0:T(1024)S(1)} %get-tuple-element.49) | copy-start | bytes 9220
  10.7 11.5 %copy-start.23 = (f32[768]{0:T(1024)}, f32[768]{0:T(1024)S(1)}, u32[]{:S(2)}) copy-start(f32[768]{0:T(1024)S(1)} %get-tuple-element.50) | copy-start | bytes 9220
  10.7 11.5 %copy-start.25 = (f32[768]{0:T(1024)}, f32[768]{0:T(1024)S(1)}, u32[]{:S(2)}) copy-start(f32[768]{0:T(1024)S(1)} %get-tuple-element.51) | copy-start | bytes 9220
  10.7 11.5 %copy-start.27 = (f32[768]{0:T(1024)}, f32[768]{0:T(1024)S(1)}, u32[]{:S(2)}) copy-start(f32[768]{0:T(1024)S(1)} %get-tuple-element.52) | copy-start | bytes 9220
  12.6 5.5 %collective-permute-start.2 = (bf16[3,30,768]{2,1,0:T(8,128)(2,1)S(1)}, bf16[3,30,768]{2,1,0:T(8,128)(2,1)S(1)}, u32[]{:S(2)}, u32[]{:S(2)}) collective-permute-start(bf16[3,30,768]{2,1,0:T(8,128)(2,1)S(1)} %get-tuple-element.112), channel_id=1, source_target_pairs={{0,32},{32,64},{64,96},{96,128},{128,160},{160,192},{192,224},{1,3... | collective-permute-start | bytes 414728 | tf_op jit(solution)/shard_map/ppermute | solution.py:109
  15.8 5.9 %collective-permute-start.3 = (bf16[3,30,768]{2,1,0:T(8,128)(2,1)S(1)}, bf16[3,30,768]{2,1,0:T(8,128)(2,1)S(1)}, u32[]{:S(2)}, u32[]{:S(2)}) collective-permute-start(bf16[3,30,768]{2,1,0:T(8,128)(2,1)S(1)} %get-tuple-element.113), channel_id=1, source_target_pairs={{32,0},{64,32},{96,64},{128,96},{160,128},{192,160},{224,192},{33,... | collective-permute-start | bytes 414728 | tf_op jit(solution)/shard_map/ppermute | solution.py:109
  47.9 10.0 %collective-permute-start.4 = (bf16[3072,768]{1,0:T(8,128)(2,1)}, bf16[3072,768]{1,0:T(8,128)(2,1)}, u32[]{:S(2)}, u32[]{:S(2)}) collective-permute-start(bf16[3072,768]{1,0:T(8,128)(2,1)} %convolution_convert_fusion), channel_id=1, source_target_pairs={{0,1},{1,0},{2,3},{3,2},{4,5},{5,4},{6,7},{7,6},{8,9},{9,8},{10,11... | collective-permute-start | bytes 14155784 | tf_op jit(solution)/shard_map/ppermute | solution.py:104
  68.2 46.7 %collective-permute-start.5 = (bf16[768,768]{1,0:T(8,128)(2,1)}, bf16[768,768]{1,0:T(8,128)(2,1)S(1)}, u32[]{:S(2)}, u32[]{:S(2)}) collective-permute-start(bf16[768,768]{1,0:T(8,128)(2,1)} %get-tuple-element.27), channel_id=1, source_target_pairs={{0,2},{1,33},{2,4},{3,35},{4,6},{5,37},{6,0},{7,39},{8,10},{9,41},... | collective-permute-start | bytes 3538952 | tf_op jit(solution)/shard_map/ppermute | solution.py:58
  69.5 45.5 %collective-permute-start.6 = (bf16[768,768]{1,0:T(8,128)(2,1)}, bf16[768,768]{1,0:T(8,128)(2,1)S(1)}, u32[]{:S(2)}, u32[]{:S(2)}) collective-permute-start(bf16[768,768]{1,0:T(8,128)(2,1)} %get-tuple-element.28), channel_id=1, source_target_pairs={{0,4},{1,65},{2,6},{3,67},{4,0},{5,69},{6,2},{7,71},{8,12},{9,73},... | collective-permute-start | bytes 3538952 | tf_op jit(solution)/shard_map/ppermute | solution.py:58
  74.3 40.7 %collective-permute-start.7 = (bf16[768,768]{1,0:T(8,128)(2,1)}, bf16[768,768]{1,0:T(8,128)(2,1)S(1)}, u32[]{:S(2)}, u32[]{:S(2)}) collective-permute-start(bf16[768,768]{1,0:T(8,128)(2,1)} %get-tuple-element.29), channel_id=1, source_target_pairs={{0,6},{1,97},{2,0},{3,99},{4,2},{5,101},{6,4},{7,103},{8,14},{9,10... | collective-permute-start | bytes 3538952 | tf_op jit(solution)/shard_map/ppermute | solution.py:58
  83.4 7.2 %collective-permute-start.8 = (f32[32,768]{1,0:T(8,128)S(1)}, f32[32,768]{1,0:T(8,128)S(1)}, u32[]{:S(2)}, u32[]{:S(2)}) collective-permute-start(f32[32,768]{1,0:T(8,128)S(1)} %slice_select_fusion.2), channel_id=1, source_target_pairs={{0,1},{1,0},{2,3},{3,2},{4,5},{5,4},{6,7},{7,6},{8,9},{9,8},{10,11... | collective-permute-start | bytes 294920 | tf_op jit(solution)/shard_map/ppermute | solution.py:104
  87.0 6.2 %collective-permute-start.10 = (bf16[16,3,768]{2,1,0:T(4,128)(2,1)S(1)}, bf16[16,3,768]{2,1,0:T(4,128)(2,1)S(1)}, u32[]{:S(2)}, u32[]{:S(2)}) collective-permute-start(bf16[16,3,768]{2,1,0:T(4,128)(2,1)S(1)} %get-tuple-element.114), channel_id=1, source_target_pairs={{0,1},{1,2},{2,3},{3,4},{4,5},{5,6},{6,7},{7,8},{8,9},{9,10},{10,1... | collective-permute-start | bytes 221192 | tf_op jit(solution)/shard_map/ppermute | solution.py:109
  90.6 14.3 %collective-permute-start.11 = (bf16[16,3,768]{2,1,0:T(4,128)(2,1)S(1)}, bf16[16,3,768]{2,1,0:T(4,128)(2,1)S(1)}, u32[]{:S(2)}, u32[]{:S(2)}) collective-permute-start(bf16[16,3,768]{2,1,0:T(4,128)(2,1)S(1)} %get-tuple-element.115), channel_id=1, source_target_pairs={{1,0},{2,1},{3,2},{4,3},{5,4},{6,5},{7,6},{8,7},{9,8},{10,9},{11,1... | collective-permute-start | bytes 221192 | tf_op jit(solution)/shard_map/ppermute | solution.py:109
  93.3 15.1 %collective-permute-start.9 = (bf16[32,768]{1,0:T(8,128)(2,1)S(1)}, bf16[32,768]{1,0:T(8,128)(2,1)S(1)}, u32[]{:S(2)}, u32[]{:S(2)}) collective-permute-start(bf16[32,768]{1,0:T(8,128)(2,1)S(1)} %add_convert_fusion.4), channel_id=1, source_target_pairs={{0,128},{128,0},{1,129},{129,1},{2,130},{130,2},{3,131},{131,3},{4... | collective-permute-start | bytes 147464 | tf_op jit(solution)/shard_map/ppermute | solution.py:100
  105.0 5.4 %collective-permute-start.12 = (bf16[3,30,768]{2,1,0:T(8,128)(2,1)S(1)}, bf16[3,30,768]{2,1,0:T(8,128)(2,1)S(1)}, u32[]{:S(2)}, u32[]{:S(2)}) collective-permute-start(bf16[3,30,768]{2,1,0:T(8,128)(2,1)S(1)} %get-tuple-element.108), channel_id=1, source_target_pairs={{0,32},{32,64},{64,96},{96,128},{128,160},{160,192},{192,224},{1,3... | collective-permute-start | bytes 414728 | tf_op jit(solution)/shard_map/ppermute | solution.py:109
  108.4 6.2 %collective-permute-start.13 = (bf16[3,30,768]{2,1,0:T(8,128)(2,1)S(1)}, bf16[3,30,768]{2,1,0:T(8,128)(2,1)S(1)}, u32[]{:S(2)}, u32[]{:S(2)}) collective-permute-start(bf16[3,30,768]{2,1,0:T(8,128)(2,1)S(1)} %get-tuple-element.109), channel_id=1, source_target_pairs={{32,0},{64,32},{96,64},{128,96},{160,128},{192,160},{224,192},{33,... | collective-permute-start | bytes 414728 | tf_op jit(solution)/shard_map/ppermute | solution.py:109
  116.5 13.6 %collective-permute-start.14 = (bf16[224,768]{1,0:T(8,128)(2,1)S(1)}, bf16[224,768]{1,0:T(8,128)(2,1)S(1)}, u32[]{:S(2)}, u32[]{:S(2)}) collective-permute-start(bf16[224,768]{1,0:T(8,128)(2,1)S(1)} %get-tuple-element.131), channel_id=1, source_target_pairs={{0,32},{1,3},{2,34},{3,5},{4,36},{5,7},{6,38},{7,1},{8,40},{9,11},... | collective-permute-start | bytes 1032200 | tf_op jit(solution)/shard_map/ppermute | solution.py:58
  116.8 13.3 %collective-permute-start.15 = (bf16[224,768]{1,0:T(8,128)(2,1)S(1)}, bf16[224,768]{1,0:T(8,128)(2,1)S(1)}, u32[]{:S(2)}, u32[]{:S(2)}) collective-permute-start(bf16[224,768]{1,0:T(8,128)(2,1)S(1)} %get-tuple-element.132), channel_id=1, source_target_pairs={{0,64},{1,5},{2,66},{3,7},{4,68},{5,1},{6,70},{7,3},{8,72},{9,13},... | collective-permute-start | bytes 1032200 | tf_op jit(solution)/shard_map/ppermute | solution.py:58
  120.4 9.7 %collective-permute-start.16 = (bf16[224,768]{1,0:T(8,128)(2,1)S(1)}, bf16[224,768]{1,0:T(8,128)(2,1)S(1)}, u32[]{:S(2)}, u32[]{:S(2)}) collective-permute-start(bf16[224,768]{1,0:T(8,128)(2,1)S(1)} %get-tuple-element.130), channel_id=1, source_target_pairs={{0,96},{1,7},{2,98},{3,1},{4,100},{5,3},{6,102},{7,5},{8,104},{9,1... | collective-permute-start | bytes 1032200 | tf_op jit(solution)/shard_map/ppermute | solution.py:58
  130.2 9.9 %collective-permute-start.18 = (bf16[32,768]{1,0:T(8,128)(2,1)S(1)}, bf16[32,768]{1,0:T(8,128)(2,1)S(1)}, u32[]{:S(2)}, u32[]{:S(2)}) collective-permute-start(bf16[32,768]{1,0:T(8,128)(2,1)S(1)} %add_convert_fusion.3), channel_id=1, source_target_pairs={{0,2},{1,33},{2,4},{3,35},{4,6},{5,37},{6,0},{7,39},{8,10},{9,41},... | collective-permute-start | bytes 147464 | tf_op jit(solution)/shard_map/ppermute | solution.py:58
  137.2 4.4 %collective-permute-start.19 = (bf16[32,768]{1,0:T(8,128)(2,1)S(1)}, bf16[32,768]{1,0:T(8,128)(2,1)S(1)}, u32[]{:S(2)}, u32[]{:S(2)}) collective-permute-start(bf16[32,768]{1,0:T(8,128)(2,1)S(1)} %add_convert_fusion.3), channel_id=1, source_target_pairs={{0,4},{1,65},{2,6},{3,67},{4,0},{5,69},{6,2},{7,71},{8,12},{9,73},... | collective-permute-start | bytes 147464 | tf_op jit(solution)/shard_map/ppermute | solution.py:58
  137.5 4.1 %collective-permute-start.20 = (bf16[32,768]{1,0:T(8,128)(2,1)S(1)}, bf16[32,768]{1,0:T(8,128)(2,1)S(1)}, u32[]{:S(2)}, u32[]{:S(2)}) collective-permute-start(bf16[32,768]{1,0:T(8,128)(2,1)S(1)} %add_convert_fusion.3), channel_id=1, source_target_pairs={{0,6},{1,97},{2,0},{3,99},{4,2},{5,101},{6,4},{7,103},{8,14},{9,10... | collective-permute-start | bytes 147464 | tf_op jit(solution)/shard_map/ppermute | solution.py:58
  140.0 5.8 %collective-permute-start.17 = (bf16[96,768]{1,0:T(8,128)(2,1)S(1)}, bf16[96,768]{1,0:T(8,128)(2,1)S(1)}, u32[]{:S(2)}, u32[]{:S(2)}) collective-permute-start(bf16[96,768]{1,0:T(8,128)(2,1)S(1)} %bitcast.86), channel_id=1, source_target_pairs={{0,128},{128,0},{1,129},{129,1},{2,130},{130,2},{3,131},{131,3},{4... | collective-permute-start | bytes 442376 | tf_op jit(solution)/shard_map/ppermute | solution.py:100
  145.9 6.0 %collective-permute-start.21 = (bf16[56,768]{1,0:T(8,128)(2,1)S(1)}, bf16[56,768]{1,0:T(8,128)(2,1)S(1)}, u32[]{:S(2)}, u32[]{:S(2)}) collective-permute-start(bf16[56,768]{1,0:T(8,128)(2,1)S(1)} %get-tuple-element.127), channel_id=1, source_target_pairs={{0,8},{8,16},{16,24},{24,0},{1,9},{9,17},{17,25},{25,1},{2,10},{10... | collective-permute-start | bytes 258056 | tf_op jit(solution)/shard_map/ppermute | solution.py:93
  146.8 9.1 %collective-permute-start.22 = (bf16[56,768]{1,0:T(8,128)(2,1)S(1)}, bf16[56,768]{1,0:T(8,128)(2,1)S(1)}, u32[]{:S(2)}, u32[]{:S(2)}) collective-permute-start(bf16[56,768]{1,0:T(8,128)(2,1)S(1)} %get-tuple-element.128), channel_id=1, source_target_pairs={{0,16},{8,24},{16,0},{24,8},{1,17},{9,25},{17,1},{25,9},{2,18},{10... | collective-permute-start | bytes 258056 | tf_op jit(solution)/shard_map/ppermute | solution.py:93
  148.5 10.4 %collective-permute-start.23 = (bf16[56,768]{1,0:T(8,128)(2,1)S(1)}, bf16[56,768]{1,0:T(8,128)(2,1)S(1)}, u32[]{:S(2)}, u32[]{:S(2)}) collective-permute-start(bf16[56,768]{1,0:T(8,128)(2,1)S(1)} %get-tuple-element.129), channel_id=1, source_target_pairs={{0,24},{8,0},{16,8},{24,16},{1,25},{9,1},{17,9},{25,17},{2,26},{10... | collective-permute-start | bytes 258056 | tf_op jit(solution)/shard_map/ppermute | solution.py:93
  159.0 1.7 %collective-permute-start.24 = (f32[44,768]{1,0:T(8,128)S(1)}, f32[44,768]{1,0:T(8,128)S(1)}, u32[]{:S(2)}, u32[]{:S(2)}) collective-permute-start(f32[44,768]{1,0:T(8,128)S(1)} %pad_maximum_fusion.14), channel_id=1, source_target_pairs={{0,1},{1,0},{2,3},{3,2},{4,5},{5,4},{6,7},{7,6},{8,9},{9,8},{10,11... | collective-permute-start | bytes 405512 | tf_op jit(solution)/shard_map/ppermute | solution.py:104
  (75 other events, 360.6 us)

commit v3 on v2

--- a/solution.py
+++ b/solution.py
@@ -236,6 +236,78 @@
     )(padded, conv_out, d_normed, branch, cotangent, sum_pre, params)
 
 
+def conv_kernel(ahead, pad_ref, w_ref, *refs):
+    if ahead:
+        par_ref, out_ref, normed_ref, im = refs
+    else:
+        start_ref, out_ref, im = refs
+    rows, cols, chans = out_ref.shape
+    high, wide, _ = pad_ref.shape
+    lanes = 128
+    blocks = chans // lanes
+    kk = KS * KS
+
+    def spread(r, _):
+        row = pad_ref[r].astype(F32)
+        for b in range(blocks):
+            im[b, r, 0:wide, :] = row[:, b * lanes : (b + 1) * lanes]
+        return 0
+
+    lax.fori_loop(0, high, spread, 0)
+    part = 8
+
+    def block(b, _):
+        at = pl.ds(pl.multiple_of(b * lanes, lanes), lanes)
+        for p0 in range(0, rows, part):
+            size = min(part, rows - p0)
+            if ahead:
+                acc = [jnp.zeros((cols, lanes), F32) + par_ref[0:1, at] for _ in range(size)]
+            else:
+                acc = [start_ref[p0 + p, :, at].astype(F32) for p in range(size)]
+            for j in range(KS):
+                spots = [KS * i + j for i in range(KS)]
+                w = [
+                    w_ref[t : t + 1, at] if ahead else w_ref[kk - 1 - t : kk - t, at]
+                    for t in spots
+                ]
+                for r in range(size + KS - 1):
+                    v = im[b, p0 + r, j : j + cols, :]
+                    for i in range(KS):
+                        if 0 <= r - i < size:
+                            acc[r - i] = acc[r - i] + w[i] * v
+            for p in range(size):
+                out_ref[p0 + p, :, at] = acc[p]
+        return 0
+
+    lax.fori_loop(0, blocks, block, 0)
+    if ahead:
+
+        def norm(r, _):
+            v = out_ref[r]
+            v = v - jnp.mean(v, axis=-1, keepdims=True)
+            rstd = lax.rsqrt(jnp.mean(v * v, axis=-1, keepdims=True) + 1e-06)
+            normed_ref[r] = ((v * rstd) * par_ref[1:2, :] + par_ref[2:3, :]).astype(BF)
+            return 0
+
+        lax.fori_loop(0, rows, norm, 0)
+
+
+def conv(ahead, padded, weights, extra):
+    high, wide, chans = padded.shape
+    shape = (high - KS + 1, wide - KS + 1, chans)
+    out = jax.ShapeDtypeStruct(shape, F32)
+    return pl.pallas_call(
+        functools.partial(conv_kernel, ahead),
+        out_shape=(out, jax.ShapeDtypeStruct(shape, BF)) if ahead else out,
+        scratch_shapes=[pltpu.VMEM((chans // 128, high, shape[1] + 8, 128), F32)],
+        compiler_params=pltpu.CompilerParams(vmem_limit_bytes=32 * 1024 * 1024),
+        cost_estimate=pl.CostEstimate(
+            flops=2 * KS * KS * math.prod(shape), bytes_accessed=16 * 1024 * 1024, transcendentals=0
+        ),
+        name="conv_norm" if ahead else "conv_image",
+    )(padded, weights, extra)
+
+
 def chunk_kernel(at_ref, pre_ref, hid_ref, normed_ref, db_ref, come_ref, *outs):
     unit = hid_ref.shape[1] // 16
     core = at_ref[0]
@@ -327,17 +399,14 @@
     scale = 1.0 / math.sqrt(rows * cols * 256)
     first = lax.axis_index("c") == 0
     padded = halo_rows(halo_columns(image, 3), 3)
-    conv_out = jnp.zeros((rows, cols, chans), F32) + conv_bias
-    for i in range(KS):
-        for j in range(KS):
-            conv_out = conv_out + conv_weight[i, j] * padded[i : i + rows, j : j + cols].astype(F32)
-    flat = conv_out.reshape(rows * cols, chans)
-    channel_mean = jnp.mean(flat, axis=-1, keepdims=True)
-    centered = flat - channel_mean
-    var = jnp.mean(centered * centered, axis=-1, keepdims=True)
-    rstd = lax.rsqrt(var + 1e-06)
-    xhat = centered * rstd
-    normed = (xhat * layernorm_gain + layernorm_bias).astype(BF)
+    kernel = conv_weight.reshape(KS * KS, chans)
+    conv_out, normed = conv(
+        True,
+        padded,
+        kernel,
+        jnp.stack([conv_bias, layernorm_gain, layernorm_bias] + [layernorm_bias] * 5),
+    )
+    normed = normed.reshape(rows * cols, chans)
     pre = (
         lax.dot_general(normed, w_expand, (((1,), (1,)), ((), ())), preferred_element_type=F32)
         + b_expand
@@ -377,18 +446,14 @@
     small = jnp.where(first, lower, upper) + core_swap(jnp.where(first, upper, lower))
     low = small.astype(BF)
     small = low.astype(F32) + zl_swap(low).astype(F32)
-    d_pad = halo_rows(halo_columns(d_conv, 3), 3)
-    got, small, d_pad = lax.optimization_barrier((got, small, d_pad))
+    wide = halo_columns(d_conv, 3)
+    d_pad = halo_rows(wide, 3)
+    got, small, wide = lax.optimization_barrier((got, small, wide))
     term = add_all([moved[0]] + got).astype(BF).reshape(2, 4, 4, 2 * per, chans)
 
     moved = split_send(term, small, ("y", "x"), (1, 2))
     got = split_move(moved, ("y", "x"))
-    grad_image = cotangent.astype(F32)
-    for i in range(KS):
-        for j in range(KS):
-            grad_image = grad_image + conv_weight[i, j] * d_pad[
-                6 - i : 6 - i + rows, 6 - j : 6 - j + cols
-            ].astype(F32)
+    grad_image = conv(False, d_pad, kernel, cotangent)
     got, grad_image = lax.optimization_barrier((got, grad_image))
     term, small = split_add(moved, got, small.shape[0])
     term = term.astype(BF).reshape(2, 4, 2 * per, chans)

time: 164 us -> 164 us (level)
  other arithmetic: 25.6 us -> 10.4 us
  Pallas kernels: 19.5 us -> 33.8 us
  waiting for transfers between devices: 34.9 us -> 21.9 us
  starting transfers between devices: 52.3 us -> 61 us
  matrix products: 20.7 us -> 23.4 us
  local copies, waits for them, and re-layouts: 7.9 us -> 9.9 us
    pallas_call x0 -> x2, Pallas kernels: none -> 14.3 us  [conv(): pl.pallas_call(functools.partial(conv_kernel, ahead), out_shape=(out, jax...]
    reduce_sum x2 -> x0, other arithmetic: 11 us -> none  [the longest x1 10.8 us: on_device(): channel_mean = jnp.mean(flat, axis=-1, keepdims=True)]
    ppermute x8, waiting for transfers between devices: 20.5 us -> 10.7 us  [shift(): lax.ppermute(v, axes, [(i, i + d) for i in range(n) if 0 <= i + d < n])]
    add x1 -> x0, other arithmetic: 9.41 us -> none  [on_device(): grad_image + conv_weight[i, j] * d_pad[6 - i:6 - i + rows, 6 - j:6 - j +...]
    dot_general x1, matrix products: 2.02 us -> 6.25 us  [on_device(): lax.dot_general(hidden, w_reduce, (((1,), (1,)), ((), ())), preferred_ele...]
    ppermute x9, starting transfers between devices: 19.5 us -> 23.2 us  [split_move(): lax.ppermute(moved[k], AXES, core_pairs(k, lead))]
    ppermute x3, waiting for transfers between devices: 7.67 us -> 4.53 us  [z_sum(): got = lax.ppermute(sent, 'zh', [(i, (i + k) % 4) for i in range(4)])]
    ppermute x3, starting transfers between devices: 5.27 us -> 8.31 us  [z_sum(): got = lax.ppermute(sent, 'zh', [(i, (i + k) % 4) for i in range(4)])]
  transfers between devices with their start and end apart: 25 -> 25, of which waited for: 12 -> 11; matrix products, arithmetic and copies ran while one was open for 14% -> 12% of each run, Pallas kernels for 6% -> 9%
where the time goes in v3:
time: 164 us; the launch traced here: 162 us
  starting transfers between devices  61 us (37%)
  Pallas kernels  33.8 us (21%)
  matrix products  23.4 us (14%)
  waiting for transfers between devices  21.9 us (13%)
  other arithmetic  10.4 us (6%)
  local copies, waits for them, and re-layouts  9.9 us (6%)
    ppermute x9, starting transfers between devices, split_move(): lax.ppermute(moved[k], AXES, core_pairs(k, lead))  23.2 us
    ppermute x8, starting transfers between devices, shift(): lax.ppermute(v, axes, [(i, i + d) for i in range(n) if 0 <= i + d < n])  20.9 us
    pallas_call x2, Pallas kernels, conv(): pl.pallas_call(functools.partial(conv_kernel, ahead), out_shape=(out, jax...  14.3 us
    ppermute x8, waiting for transfers between devices, shift(): lax.ppermute(v, axes, [(i, i + d) for i in range(n) if 0 <= i + d < n])  10.7 us
    pallas_call x1, Pallas kernels, chunks(): pl.pallas_call(chunk_kernel, grid=(8,), in_specs=[pl.BlockSpec(memory_spa...  10.4 us
    pallas_call x1, Pallas kernels, backward(): pl.pallas_call(functools.partial(backward_kernel, scale), out_shape=(jax....  9.07 us
    ppermute x3, starting transfers between devices, z_sum(): got = lax.ppermute(sent, 'zh', [(i, (i + k) % 4) for i in range(4)])  8.31 us
    ppermute x3, starting transfers between devices, core_swap(): return lax.ppermute(v, 'c', [(0, 1), (1, 0)])  6.33 us
  transfers between devices with their start and end apart: 25, of which 11 were waited for; matrix products, arithmetic and copies ran while one was open for 12% of the time, Pallas kernels for 9%

profile of v3, /device:TPU:1, one launch (start us, length us, event | category | flops | bytes accessed | tf_op | source)
XLA Modules:
  0.0 161.9 jit_solution(16337126775605964966)
XLA Ops:
  1.8 4.5 %collective-permute-start = (bf16[16,3,768]{2,1,0:T(4,128)(2,1)S(1)}, bf16[16,3,768]{2,1,0:T(4,128)(2,1)S(1)}, u32[]{:S(2)}, u32[]{:S(2)}) collective-permute-start(bf16[16,3,768]{2,1,0:T(4,128)(2,1)S(1)} %get-tuple-element.65), channel_id=1, source_target_pairs={{0,1},{1,2},{2,3},{3,4},{4,5},{5,6},{6,7},{7,8},{8,9},{9,10},{10,1... | collective-permute-start | bytes 221192 | tf_op jit(solution)/shard_map/ppermute | solution.py:109
  6.3 1.9 %collective-permute-start.1 = (bf16[16,3,768]{2,1,0:T(4,128)(2,1)S(1)}, bf16[16,3,768]{2,1,0:T(4,128)(2,1)S(1)}, u32[]{:S(2)}, u32[]{:S(2)}) collective-permute-start(bf16[16,3,768]{2,1,0:T(4,128)(2,1)S(1)} %get-tuple-element.66), channel_id=1, source_target_pairs={{1,0},{2,1},{3,2},{4,3},{5,4},{6,5},{7,6},{8,7},{9,8},{10,9},{11,1... | collective-permute-start | bytes 221192 | tf_op jit(solution)/shard_map/ppermute | solution.py:109
  13.5 3.3 %collective-permute-start.2 = (bf16[3,30,768]{2,1,0:T(8,128)(2,1)S(1)}, bf16[3,30,768]{2,1,0:T(8,128)(2,1)S(1)}, u32[]{:S(2)}, u32[]{:S(2)}) collective-permute-start(bf16[3,30,768]{2,1,0:T(8,128)(2,1)S(1)} %get-tuple-element.61), channel_id=1, source_target_pairs={{0,32},{32,64},{64,96},{96,128},{128,160},{160,192},{192,224},{1,3... | collective-permute-start | bytes 414728 | tf_op jit(solution)/shard_map/ppermute | solution.py:109
  16.8 1.3 collective-permute-start.3
  19.3 3.4 %collective-permute-done.3 = bf16[3,30,768]{2,1,0:T(8,128)(2,1)S(1)} collective-permute-done((bf16[3,30,768]{2,1,0:T(8,128)(2,1)S(1)}, bf16[3,30,768]{2,1,0:T(8,128)(2,1)S(1)}, u32[]{:S(2)}, u32[]{:S(2)}) %collective-permute-start.3) | collective-permute-done | bytes 138272 | tf_op jit(solution)/shard_map/ppermute | solution.py:109
  23.1 8.0 %conv_norm.1 = (f32[16,24,768]{2,1,0:T(8,128)S(1)}, bf16[16,24,768]{2,1,0:T(8,128)(2,1)S(1)}) custom-call(bf16[22,30,768]{2,1,0:T(8,128)(2,1)S(1)} %pad_maximum_fusion.pad_ref, f32[49,768]{1,0:T(8,128)S(1)} %reshape.97.w_ref, f32[8,768]{1,0:T(8,128)S(1)} %stack.49.refs_0_), custom_call_target="tpu_custom_call" | custom-call | flops 28901376 | bytes 16777216 | tf_op jit(solution)/shard_map/conv_norm/pallas_call | solution.py:299
  31.3 2.8 %multiply_convert_fusion = (bf16[384,3072]{1,0:T(8,128)(2,1)S(1)}, f32[384,3072]{1,0:T(8,128)S(1)}) fusion(f32[3072]{0:T(1024)S(1)} %copy-done.19, bf16[384,768]{1,0:T(8,128)(2,1)S(1)} %bitcast.71, bf16[3072,768]{1,0:T(8,128)(2,1)S(1)} %copy-done.18), kind=kOutput, calls=%fused_computation.9 | convolution fusion | flops 1819017216 | bytes 12398592 | tf_op jit(solution)/shard_map/dot_general | solution.py:411
  34.1 3.6 %convert_reduce_fusion = (f32[3072]{0:T(1024)S(1)}, bf16[384,3072]{1,0:T(8,128)(2,1)S(1)}) fusion(f32[384,3072]{1,0:T(8,128)S(1)} %get-tuple-element.83, bf16[384,768]{1,0:T(8,128)(2,1)S(1)} %fusion.8.db_ref, bf16[768,3072]{1,0:T(8,128)(2,1)S(1)} %bitcast.81), kind=kOutput, calls=%fused_computation.8 | convolution fusion | flops 1826092032 | bytes 12398592 | tf_op jit(solution)/shard_map/dot_general | solution.py:418
  37.8 4.5 %convolution_convert_fusion = bf16[3072,768]{1,0:T(8,128)(2,1)} fusion(bf16[384,3072]{1,0:T(8,128)(2,1)S(1)} %get-tuple-element.82.hid_ref, bf16[384,3072]{1,0:T(8,128)(2,1)S(1)} %get-tuple-element.85.pre_ref, pred[]{:T(512)S(6)} %eq.2, bf16[384,768]{1,0:T(8,128)(2,1)S(1)} %fusion.8.db_ref, bf16[384,768]{1,0:T(8,128)(2,1)S(1)} %bitcast.72), kind=kOutput, calls=%fused_computation.1 | convolution fusion | flops 1815773184 | bytes 10616833 | tf_op jit(solution)/shard_map/dot_general | solution.py:131
  42.6 6.3 %fusion.18 = f32[384,768]{1,0:T(8,128)} fusion(bf16[384,3072]{1,0:T(8,128)(2,1)} %copy-done.2, bf16[3072,768]{1,0:T(8,128)(2,1)} %param.16), kind=kOutput, calls=%fused_computation.78 | convolution fusion | flops 1811939328 | bytes 8257536 | tf_op jit(solution)/shard_map/dot_general | solution.py:426
  48.8 1.7 %collective-permute-done.4.come_ref = bf16[3072,768]{1,0:T(8,128)(2,1)} collective-permute-done((bf16[3072,768]{1,0:T(8,128)(2,1)}, bf16[3072,768]{1,0:T(8,128)(2,1)}, u32[]{:S(2)}, u32[]{:S(2)}) %collective-permute-start.4) | collective-permute-done | bytes 4718624 | tf_op jit(solution)/shard_map/ppermute | solution.py:104
  50.6 10.4 %chunks.1 = (bf16[768,768]{1,0:T(8,128)(2,1)}, bf16[768,768]{1,0:T(8,128)(2,1)}, bf16[768,768]{1,0:T(8,128)(2,1)}, bf16[768,768]{1,0:T(8,128)(2,1)}) custom-call(s32[3]{0:T(128)S(1)} %pad_add_fusion.at_ref, bf16[384,3072]{1,0:T(8,128)(2,1)S(1)} %copy-done.3, bf16[384,3072]{1,0:T(8,128)(2,1)S(1)} %get-tuple-element.82.hid_ref, bf16[384,768]{1,0:T(8,128)(2,1)S(1)} %bitcast.73, ...), custom_call_target="tpu_custom_call" | custom-call | flops 1811939328 | bytes 18874368 | tf_op jit(solution)/shard_map/chunks/pallas_call | solution.py:362
  61.0 1.3 collective-permute-start.5
  62.3 4.7 %collective-permute-start.6 = (bf16[768,768]{1,0:T(8,128)(2,1)}, bf16[768,768]{1,0:T(8,128)(2,1)}, u32[]{:S(2)}, u32[]{:S(2)}) collective-permute-start(bf16[768,768]{1,0:T(8,128)(2,1)} %get-tuple-element.30), channel_id=1, source_target_pairs={{0,4},{1,65},{2,6},{3,67},{4,0},{5,69},{6,2},{7,71},{8,12},{9,73},... | collective-permute-start | bytes 3538952 | tf_op jit(solution)/shard_map/ppermute | solution.py:58
  67.0 6.3 %fusion.19 = f32[384,768]{1,0:T(8,128)} fusion(bf16[384,3072]{1,0:T(8,128)(2,1)} %copy-done.1, bf16[768,3072]{1,0:T(8,128)(2,1)} %param.18), kind=kOutput, calls=%fused_computation.79 | convolution fusion | flops 1811939328 | bytes 8257536 | tf_op jit(solution)/shard_map/dot_general | solution.py:423
  75.9 9.1 %backward.1 = (f32[64,768]{1,0:T(8,128)S(1)}, bf16[16,24,768]{2,1,0:T(8,128)(2,1)S(1)}) custom-call(bf16[22,30,768]{2,1,0:T(8,128)(2,1)S(1)} %pad_maximum_fusion.pad_ref, f32[16,24,768]{2,1,0:T(8,128)S(1)} %copy-done.9, f32[16,24,768]{2,1,0:T(8,128)S(1)} %bitcast.69, f32[16,24,768]{2,1,0:T(8,128)S(1)} %bitcast.70, bf16[16,24,768]{2,1,0:T(8,128)(2,1)S(1)} %copy-done, ...), custom_call_target="tpu_custom_call" | custom-call | flops 28901376 | bytes 8388608 | tf_op jit(solution)/shard_map/backward/pallas_call | solution.py:220
  85.0 3.2 %collective-permute-start.8 = (f32[32,768]{1,0:T(8,128)S(1)}, f32[32,768]{1,0:T(8,128)S(1)}, u32[]{:S(2)}, u32[]{:S(2)}) collective-permute-start(f32[32,768]{1,0:T(8,128)S(1)} %slice_select_fusion.2), channel_id=1, source_target_pairs={{0,1},{1,0},{2,3},{3,2},{4,5},{5,4},{6,7},{7,6},{8,9},{9,8},{10,11... | collective-permute-start | bytes 294920 | tf_op jit(solution)/shard_map/ppermute | solution.py:104
  88.3 3.6 %collective-permute-start.10 = (bf16[16,3,768]{2,1,0:T(4,128)(2,1)S(1)}, bf16[16,3,768]{2,1,0:T(4,128)(2,1)S(1)}, u32[]{:S(2)}, u32[]{:S(2)}) collective-permute-start(bf16[16,3,768]{2,1,0:T(4,128)(2,1)S(1)} %get-tuple-element.63), channel_id=1, source_target_pairs={{0,1},{1,2},{2,3},{3,4},{4,5},{5,6},{6,7},{7,8},{8,9},{9,10},{10,1... | collective-permute-start | bytes 221192 | tf_op jit(solution)/shard_map/ppermute | solution.py:109
  91.9 1.9 %collective-permute-start.11 = (bf16[16,3,768]{2,1,0:T(4,128)(2,1)S(1)}, bf16[16,3,768]{2,1,0:T(4,128)(2,1)S(1)}, u32[]{:S(2)}, u32[]{:S(2)}) collective-permute-start(bf16[16,3,768]{2,1,0:T(4,128)(2,1)S(1)} %get-tuple-element.64), channel_id=1, source_target_pairs={{1,0},{2,1},{3,2},{4,3},{5,4},{6,5},{7,6},{8,7},{9,8},{10,9},{11,1... | collective-permute-start | bytes 221192 | tf_op jit(solution)/shard_map/ppermute | solution.py:109
  93.8 2.1 %collective-permute-start.9 = (bf16[32,768]{1,0:T(8,128)(2,1)S(1)}, bf16[32,768]{1,0:T(8,128)(2,1)S(1)}, u32[]{:S(2)}, u32[]{:S(2)}) collective-permute-start(bf16[32,768]{1,0:T(8,128)(2,1)S(1)} %add_convert_fusion.4), channel_id=1, source_target_pairs={{0,128},{128,0},{1,129},{129,1},{2,130},{130,2},{3,131},{131,3},{4... | collective-permute-start | bytes 147464 | tf_op jit(solution)/shard_map/ppermute | solution.py:100
  95.9 1.9 %collective-permute-done.11 = bf16[16,3,768]{2,1,0:T(4,128)(2,1)S(1)} collective-permute-done((bf16[16,3,768]{2,1,0:T(4,128)(2,1)S(1)}, bf16[16,3,768]{2,1,0:T(4,128)(2,1)S(1)}, u32[]{:S(2)}, u32[]{:S(2)}) %collective-permute-start.11) | collective-permute-done | bytes 73760 | tf_op jit(solution)/shard_map/ppermute | solution.py:109
  98.2 2.6 %add_convert_fusion = bf16[768,768]{1,0:T(8,128)(2,1)S(1)} fusion(bf16[768,768]{1,0:T(8,128)(2,1)} %collective-permute-done.7, bf16[768,768]{1,0:T(8,128)(2,1)} %collective-permute-done.6, bf16[768,768]{1,0:T(8,128)(2,1)} %collective-permute-done.5, bf16[768,768]{1,0:T(8,128)(2,1)S(1)} %copy-done.15), kind=kLoop, calls=%fused_computation.12 | loop fusion | flops 4718592 | bytes 5898240 | tf_op jit(solution)/shard_map/convert_element_type | solution.py:452
  102.3 12.5 %collective-permute-start.13 = (bf16[224,768]{1,0:T(8,128)(2,1)}, bf16[224,768]{1,0:T(8,128)(2,1)}, u32[]{:S(2)}, u32[]{:S(2)}) collective-permute-start(bf16[224,768]{1,0:T(8,128)(2,1)} %get-tuple-element.81), channel_id=1, source_target_pairs={{0,64},{1,5},{2,66},{3,7},{4,68},{5,1},{6,70},{7,3},{8,72},{9,13},... | collective-permute-start | bytes 1032200 | tf_op jit(solution)/shard_map/ppermute | solution.py:58
  115.4 3.1 %collective-permute-start.15 = (bf16[3,30,768]{2,1,0:T(8,128)(2,1)}, bf16[3,30,768]{2,1,0:T(8,128)(2,1)S(1)}, u32[]{:S(2)}, u32[]{:S(2)}) collective-permute-start(bf16[3,30,768]{2,1,0:T(8,128)(2,1)} %get-tuple-element.59), channel_id=1, source_target_pairs={{0,32},{32,64},{64,96},{96,128},{128,160},{160,192},{192,224},{1,3... | collective-permute-start | bytes 414728 | tf_op jit(solution)/shard_map/ppermute | solution.py:109
  120.9 3.5 %collective-permute-done.16 = bf16[3,30,768]{2,1,0:T(8,128)(2,1)S(1)} collective-permute-done((bf16[3,30,768]{2,1,0:T(8,128)(2,1)S(1)}, bf16[3,30,768]{2,1,0:T(8,128)(2,1)S(1)}, u32[]{:S(2)}, u32[]{:S(2)}) %collective-permute-start.16) | collective-permute-done | bytes 138272 | tf_op jit(solution)/shard_map/ppermute | solution.py:109
  124.8 6.3 %conv_image.1 = f32[16,24,768]{2,1,0:T(8,128)} custom-call(bf16[22,30,768]{2,1,0:T(8,128)(2,1)S(1)} %pad_maximum_fusion.1.pad_ref, f32[49,768]{1,0:T(8,128)S(1)} %copy-done.7, bf16[16,24,768]{2,1,0:T(8,128)(2,1)S(1)} %copy-done), custom_call_target="tpu_custom_call" | custom-call | flops 28901376 | bytes 16777216 | tf_op jit(solution)/shard_map/conv_image/pallas_call | solution.py:299
  133.1 3.6 %collective-permute-start.19 = (bf16[32,768]{1,0:T(8,128)(2,1)S(1)}, bf16[32,768]{1,0:T(8,128)(2,1)S(1)}, u32[]{:S(2)}, u32[]{:S(2)}) collective-permute-start(bf16[32,768]{1,0:T(8,128)(2,1)S(1)} %add_convert_fusion.3), channel_id=1, source_target_pairs={{0,4},{1,65},{2,6},{3,67},{4,0},{5,69},{6,2},{7,71},{8,12},{9,73},... | collective-permute-start | bytes 147464 | tf_op jit(solution)/shard_map/ppermute | solution.py:58
  139.6 2.4 %collective-permute-done.17 = bf16[96,768]{1,0:T(8,128)(2,1)S(1)} collective-permute-done((bf16[96,768]{1,0:T(8,128)(2,1)S(1)}, bf16[96,768]{1,0:T(8,128)(2,1)S(1)}, u32[]{:S(2)}, u32[]{:S(2)}) %collective-permute-start.17) | collective-permute-done | bytes 147488 | tf_op jit(solution)/shard_map/ppermute | solution.py:100
  142.2 4.9 %collective-permute-start.21 = (bf16[56,768]{1,0:T(8,128)(2,1)S(1)}, bf16[56,768]{1,0:T(8,128)(2,1)S(1)}, u32[]{:S(2)}, u32[]{:S(2)}) collective-permute-start(bf16[56,768]{1,0:T(8,128)(2,1)S(1)} %get-tuple-element.76), channel_id=1, source_target_pairs={{0,8},{8,16},{16,24},{24,0},{1,9},{9,17},{17,25},{25,1},{2,10},{10... | collective-permute-start | bytes 258056 | tf_op jit(solution)/shard_map/ppermute | solution.py:93
  147.1 3.4 %collective-permute-start.23 = (bf16[56,768]{1,0:T(8,128)(2,1)S(1)}, bf16[56,768]{1,0:T(8,128)(2,1)S(1)}, u32[]{:S(2)}, u32[]{:S(2)}) collective-permute-start(bf16[56,768]{1,0:T(8,128)(2,1)S(1)} %get-tuple-element.78), channel_id=1, source_target_pairs={{0,24},{8,0},{16,8},{24,16},{1,25},{9,1},{17,9},{25,17},{2,26},{10... | collective-permute-start | bytes 258056 | tf_op jit(solution)/shard_map/ppermute | solution.py:93
  150.5 4.5 %collective-permute-done.22 = bf16[56,768]{1,0:T(8,128)(2,1)S(1)} collective-permute-done((bf16[56,768]{1,0:T(8,128)(2,1)S(1)}, bf16[56,768]{1,0:T(8,128)(2,1)S(1)}, u32[]{:S(2)}, u32[]{:S(2)}) %collective-permute-start.22) | collective-permute-done | bytes 86048 | tf_op jit(solution)/shard_map/ppermute | solution.py:93
  155.1 3.1 %collective-permute-start.24 = (f32[44,768]{1,0:T(8,128)S(1)}, f32[44,768]{1,0:T(8,128)S(1)}, u32[]{:S(2)}, u32[]{:S(2)}) collective-permute-start(f32[44,768]{1,0:T(8,128)S(1)} %pad_maximum_fusion.10), channel_id=1, source_target_pairs={{0,1},{1,0},{2,3},{3,2},{4,5},{5,4},{6,7},{7,6},{8,9},{9,8},{10,11... | collective-permute-start | bytes 405512 | tf_op jit(solution)/shard_map/ppermute | solution.py:104
  (117 shorter events, 24.7 us)
Async XLA Ops:
  0.6 22.1 %copy-start.14 = (bf16[16,24,768]{2,1,0:T(8,128)(2,1)S(1)}, bf16[16,24,768]{2,1,0:T(8,128)(2,1)}, u32[]{:S(2)}) copy-start(bf16[16,24,768]{2,1,0:T(8,128)(2,1)} %param.11) | copy-start | bytes 1769476
  1.8 9.6 %collective-permute-start = (bf16[16,3,768]{2,1,0:T(4,128)(2,1)S(1)}, bf16[16,3,768]{2,1,0:T(4,128)(2,1)S(1)}, u32[]{:S(2)}, u32[]{:S(2)}) collective-permute-start(bf16[16,3,768]{2,1,0:T(4,128)(2,1)S(1)} %get-tuple-element.65), channel_id=1, source_target_pairs={{0,1},{1,2},{2,3},{3,4},{4,5},{5,6},{6,7},{7,8},{8,9},{9,10},{10,1... | collective-permute-start | bytes 221192 | tf_op jit(solution)/shard_map/ppermute | solution.py:109
  6.3 5.9 %collective-permute-start.1 = (bf16[16,3,768]{2,1,0:T(4,128)(2,1)S(1)}, bf16[16,3,768]{2,1,0:T(4,128)(2,1)S(1)}, u32[]{:S(2)}, u32[]{:S(2)}) collective-permute-start(bf16[16,3,768]{2,1,0:T(4,128)(2,1)S(1)} %get-tuple-element.66), channel_id=1, source_target_pairs={{1,0},{2,1},{3,2},{4,3},{5,4},{6,5},{7,6},{8,7},{9,8},{10,9},{11,1... | collective-permute-start | bytes 221192 | tf_op jit(solution)/shard_map/ppermute | solution.py:109
  9.2 22.0 %copy-start.6 = (f32[49,768]{1,0:T(8,128)}, f32[49,768]{1,0:T(8,128)S(1)}, u32[]{:S(2)}) copy-start(f32[49,768]{1,0:T(8,128)S(1)} %reshape.97.w_ref) | copy-start | bytes 451588
  12.3 18.9 %copy-start.18 = (bf16[3072,768]{1,0:T(8,128)(2,1)S(1)}, bf16[3072,768]{1,0:T(8,128)(2,1)}, u32[]{:S(2)}) copy-start(bf16[3072,768]{1,0:T(8,128)(2,1)} %param.16) | copy-start | bytes 14155780
  13.5 17.7 %copy-start.19 = (f32[3072]{0:T(1024)S(1)}, f32[3072]{0:T(1024)}, u32[]{:S(2)}) copy-start(f32[3072]{0:T(1024)} %param.17) | copy-start | bytes 36868
  13.5 5.8 %collective-permute-start.2 = (bf16[3,30,768]{2,1,0:T(8,128)(2,1)S(1)}, bf16[3,30,768]{2,1,0:T(8,128)(2,1)S(1)}, u32[]{:S(2)}, u32[]{:S(2)}) collective-permute-start(bf16[3,30,768]{2,1,0:T(8,128)(2,1)S(1)} %get-tuple-element.61), channel_id=1, source_target_pairs={{0,32},{32,64},{64,96},{96,128},{128,160},{160,192},{192,224},{1,3... | collective-permute-start | bytes 414728 | tf_op jit(solution)/shard_map/ppermute | solution.py:109
  16.8 5.9 %collective-permute-start.3 = (bf16[3,30,768]{2,1,0:T(8,128)(2,1)S(1)}, bf16[3,30,768]{2,1,0:T(8,128)(2,1)S(1)}, u32[]{:S(2)}, u32[]{:S(2)}) collective-permute-start(bf16[3,30,768]{2,1,0:T(8,128)(2,1)S(1)} %get-tuple-element.62), channel_id=1, source_target_pairs={{32,0},{64,32},{96,64},{128,96},{160,128},{192,160},{224,192},{33,... | collective-permute-start | bytes 414728 | tf_op jit(solution)/shard_map/ppermute | solution.py:109
  19.3 18.4 %copy-start.4 = (bf16[384,768]{1,0:T(8,128)(2,1)}, bf16[384,768]{1,0:T(8,128)(2,1)S(1)}, u32[]{:S(2)}) copy-start(bf16[384,768]{1,0:T(8,128)(2,1)S(1)} %fusion.8.db_ref) | copy-start | bytes 1769476
  34.1 16.5 %copy-start.1 = (bf16[384,3072]{1,0:T(8,128)(2,1)}, bf16[384,3072]{1,0:T(8,128)(2,1)S(1)}, u32[]{:S(2)}) copy-start(bf16[384,3072]{1,0:T(8,128)(2,1)S(1)} %get-tuple-element.82.hid_ref) | copy-start | bytes 7077892
  42.3 8.3 %collective-permute-start.4 = (bf16[3072,768]{1,0:T(8,128)(2,1)}, bf16[3072,768]{1,0:T(8,128)(2,1)}, u32[]{:S(2)}, u32[]{:S(2)}) collective-permute-start(bf16[3072,768]{1,0:T(8,128)(2,1)} %convolution_convert_fusion), channel_id=1, source_target_pairs={{0,1},{1,0},{2,3},{3,2},{4,5},{5,4},{6,7},{7,6},{8,9},{9,8},{10,11... | collective-permute-start | bytes 14155784 | tf_op jit(solution)/shard_map/ppermute | solution.py:104
  61.0 37.2 %collective-permute-start.5 = (bf16[768,768]{1,0:T(8,128)(2,1)}, bf16[768,768]{1,0:T(8,128)(2,1)}, u32[]{:S(2)}, u32[]{:S(2)}) collective-permute-start(bf16[768,768]{1,0:T(8,128)(2,1)} %get-tuple-element.29), channel_id=1, source_target_pairs={{0,2},{1,33},{2,4},{3,35},{4,6},{5,37},{6,0},{7,39},{8,10},{9,41},... | collective-permute-start | bytes 3538952 | tf_op jit(solution)/shard_map/ppermute | solution.py:58
  62.3 35.9 %collective-permute-start.6 = (bf16[768,768]{1,0:T(8,128)(2,1)}, bf16[768,768]{1,0:T(8,128)(2,1)}, u32[]{:S(2)}, u32[]{:S(2)}) collective-permute-start(bf16[768,768]{1,0:T(8,128)(2,1)} %get-tuple-element.30), channel_id=1, source_target_pairs={{0,4},{1,65},{2,6},{3,67},{4,0},{5,69},{6,2},{7,71},{8,12},{9,73},... | collective-permute-start | bytes 3538952 | tf_op jit(solution)/shard_map/ppermute | solution.py:58
  67.0 31.2 %collective-permute-start.7 = (bf16[768,768]{1,0:T(8,128)(2,1)}, bf16[768,768]{1,0:T(8,128)(2,1)}, u32[]{:S(2)}, u32[]{:S(2)}) collective-permute-start(bf16[768,768]{1,0:T(8,128)(2,1)} %get-tuple-element.31), channel_id=1, source_target_pairs={{0,6},{1,97},{2,0},{3,99},{4,2},{5,101},{6,4},{7,103},{8,14},{9,10... | collective-permute-start | bytes 3538952 | tf_op jit(solution)/shard_map/ppermute | solution.py:58
  85.0 6.9 %collective-permute-start.8 = (f32[32,768]{1,0:T(8,128)S(1)}, f32[32,768]{1,0:T(8,128)S(1)}, u32[]{:S(2)}, u32[]{:S(2)}) collective-permute-start(f32[32,768]{1,0:T(8,128)S(1)} %slice_select_fusion.2), channel_id=1, source_target_pairs={{0,1},{1,0},{2,3},{3,2},{4,5},{5,4},{6,7},{7,6},{8,9},{9,8},{10,11... | collective-permute-start | bytes 294920 | tf_op jit(solution)/shard_map/ppermute | solution.py:104
  88.3 5.5 %collective-permute-start.10 = (bf16[16,3,768]{2,1,0:T(4,128)(2,1)S(1)}, bf16[16,3,768]{2,1,0:T(4,128)(2,1)S(1)}, u32[]{:S(2)}, u32[]{:S(2)}) collective-permute-start(bf16[16,3,768]{2,1,0:T(4,128)(2,1)S(1)} %get-tuple-element.63), channel_id=1, source_target_pairs={{0,1},{1,2},{2,3},{3,4},{4,5},{5,6},{6,7},{7,8},{8,9},{9,10},{10,1... | collective-permute-start | bytes 221192 | tf_op jit(solution)/shard_map/ppermute | solution.py:109
  91.9 5.9 %collective-permute-start.11 = (bf16[16,3,768]{2,1,0:T(4,128)(2,1)S(1)}, bf16[16,3,768]{2,1,0:T(4,128)(2,1)S(1)}, u32[]{:S(2)}, u32[]{:S(2)}) collective-permute-start(bf16[16,3,768]{2,1,0:T(4,128)(2,1)S(1)} %get-tuple-element.64), channel_id=1, source_target_pairs={{1,0},{2,1},{3,2},{4,3},{5,4},{6,5},{7,6},{8,7},{9,8},{10,9},{11,1... | collective-permute-start | bytes 221192 | tf_op jit(solution)/shard_map/ppermute | solution.py:109
  93.8 4.3 %collective-permute-start.9 = (bf16[32,768]{1,0:T(8,128)(2,1)S(1)}, bf16[32,768]{1,0:T(8,128)(2,1)S(1)}, u32[]{:S(2)}, u32[]{:S(2)}) collective-permute-start(bf16[32,768]{1,0:T(8,128)(2,1)S(1)} %add_convert_fusion.4), channel_id=1, source_target_pairs={{0,128},{128,0},{1,129},{129,1},{2,130},{130,2},{3,131},{131,3},{4... | collective-permute-start | bytes 147464 | tf_op jit(solution)/shard_map/ppermute | solution.py:100
  101.2 23.6 %copy-start.7 = (f32[49,768]{1,0:T(8,128)S(1)}, f32[49,768]{1,0:T(8,128)}, u32[]{:S(2)}) copy-start(f32[49,768]{1,0:T(8,128)} %copy-done.6) | copy-start | bytes 451588
  102.3 28.9 %collective-permute-start.12 = (bf16[224,768]{1,0:T(8,128)(2,1)}, bf16[224,768]{1,0:T(8,128)(2,1)S(1)}, u32[]{:S(2)}, u32[]{:S(2)}) collective-permute-start(bf16[224,768]{1,0:T(8,128)(2,1)} %get-tuple-element.80), channel_id=1, source_target_pairs={{0,32},{1,3},{2,34},{3,5},{4,36},{5,7},{6,38},{7,1},{8,40},{9,11},... | collective-permute-start | bytes 1032200 | tf_op jit(solution)/shard_map/ppermute | solution.py:58
  102.3 28.9 %collective-permute-start.13 = (bf16[224,768]{1,0:T(8,128)(2,1)}, bf16[224,768]{1,0:T(8,128)(2,1)}, u32[]{:S(2)}, u32[]{:S(2)}) collective-permute-start(bf16[224,768]{1,0:T(8,128)(2,1)} %get-tuple-element.81), channel_id=1, source_target_pairs={{0,64},{1,5},{2,66},{3,7},{4,68},{5,1},{6,70},{7,3},{8,72},{9,13},... | collective-permute-start | bytes 1032200 | tf_op jit(solution)/shard_map/ppermute | solution.py:58
  114.7 16.4 %collective-permute-start.14 = (bf16[224,768]{1,0:T(8,128)(2,1)}, bf16[224,768]{1,0:T(8,128)(2,1)}, u32[]{:S(2)}, u32[]{:S(2)}) collective-permute-start(bf16[224,768]{1,0:T(8,128)(2,1)} %get-tuple-element.79), channel_id=1, source_target_pairs={{0,96},{1,7},{2,98},{3,1},{4,100},{5,3},{6,102},{7,5},{8,104},{9,1... | collective-permute-start | bytes 1032200 | tf_op jit(solution)/shard_map/ppermute | solution.py:58
  115.4 5.5 %collective-permute-start.15 = (bf16[3,30,768]{2,1,0:T(8,128)(2,1)}, bf16[3,30,768]{2,1,0:T(8,128)(2,1)S(1)}, u32[]{:S(2)}, u32[]{:S(2)}) collective-permute-start(bf16[3,30,768]{2,1,0:T(8,128)(2,1)} %get-tuple-element.59), channel_id=1, source_target_pairs={{0,32},{32,64},{64,96},{96,128},{128,160},{160,192},{192,224},{1,3... | collective-permute-start | bytes 414728 | tf_op jit(solution)/shard_map/ppermute | solution.py:109
  118.5 5.9 %collective-permute-start.16 = (bf16[3,30,768]{2,1,0:T(8,128)(2,1)S(1)}, bf16[3,30,768]{2,1,0:T(8,128)(2,1)S(1)}, u32[]{:S(2)}, u32[]{:S(2)}) collective-permute-start(bf16[3,30,768]{2,1,0:T(8,128)(2,1)S(1)} %get-tuple-element.60), channel_id=1, source_target_pairs={{32,0},{64,32},{96,64},{128,96},{160,128},{192,160},{224,192},{33,... | collective-permute-start | bytes 414728 | tf_op jit(solution)/shard_map/ppermute | solution.py:109
  132.0 6.1 %collective-permute-start.18 = (bf16[32,768]{1,0:T(8,128)(2,1)S(1)}, bf16[32,768]{1,0:T(8,128)(2,1)S(1)}, u32[]{:S(2)}, u32[]{:S(2)}) collective-permute-start(bf16[32,768]{1,0:T(8,128)(2,1)S(1)} %add_convert_fusion.3), channel_id=1, source_target_pairs={{0,2},{1,33},{2,4},{3,35},{4,6},{5,37},{6,0},{7,39},{8,10},{9,41},... | collective-permute-start | bytes 147464 | tf_op jit(solution)/shard_map/ppermute | solution.py:58
  133.1 5.6 %collective-permute-start.19 = (bf16[32,768]{1,0:T(8,128)(2,1)S(1)}, bf16[32,768]{1,0:T(8,128)(2,1)S(1)}, u32[]{:S(2)}, u32[]{:S(2)}) collective-permute-start(bf16[32,768]{1,0:T(8,128)(2,1)S(1)} %add_convert_fusion.3), channel_id=1, source_target_pairs={{0,4},{1,65},{2,6},{3,67},{4,0},{5,69},{6,2},{7,71},{8,12},{9,73},... | collective-permute-start | bytes 147464 | tf_op jit(solution)/shard_map/ppermute | solution.py:58
  136.7 2.9 %collective-permute-start.20 = (bf16[32,768]{1,0:T(8,128)(2,1)S(1)}, bf16[32,768]{1,0:T(8,128)(2,1)S(1)}, u32[]{:S(2)}, u32[]{:S(2)}) collective-permute-start(bf16[32,768]{1,0:T(8,128)(2,1)S(1)} %add_convert_fusion.3), channel_id=1, source_target_pairs={{0,6},{1,97},{2,0},{3,99},{4,2},{5,101},{6,4},{7,103},{8,14},{9,10... | collective-permute-start | bytes 147464 | tf_op jit(solution)/shard_map/ppermute | solution.py:58
  138.0 4.1 %collective-permute-start.17 = (bf16[96,768]{1,0:T(8,128)(2,1)S(1)}, bf16[96,768]{1,0:T(8,128)(2,1)S(1)}, u32[]{:S(2)}, u32[]{:S(2)}) collective-permute-start(bf16[96,768]{1,0:T(8,128)(2,1)S(1)} %bitcast.79), channel_id=1, source_target_pairs={{0,128},{128,0},{1,129},{129,1},{2,130},{130,2},{3,131},{131,3},{4... | collective-permute-start | bytes 442376 | tf_op jit(solution)/shard_map/ppermute | solution.py:100
  142.2 8.3 %collective-permute-start.21 = (bf16[56,768]{1,0:T(8,128)(2,1)S(1)}, bf16[56,768]{1,0:T(8,128)(2,1)S(1)}, u32[]{:S(2)}, u32[]{:S(2)}) collective-permute-start(bf16[56,768]{1,0:T(8,128)(2,1)S(1)} %get-tuple-element.76), channel_id=1, source_target_pairs={{0,8},{8,16},{16,24},{24,0},{1,9},{9,17},{17,25},{25,1},{2,10},{10... | collective-permute-start | bytes 258056 | tf_op jit(solution)/shard_map/ppermute | solution.py:93
  147.1 7.9 %collective-permute-start.22 = (bf16[56,768]{1,0:T(8,128)(2,1)S(1)}, bf16[56,768]{1,0:T(8,128)(2,1)S(1)}, u32[]{:S(2)}, u32[]{:S(2)}) collective-permute-start(bf16[56,768]{1,0:T(8,128)(2,1)S(1)} %get-tuple-element.77), channel_id=1, source_target_pairs={{0,16},{8,24},{16,0},{24,8},{1,17},{9,25},{17,1},{25,9},{2,18},{10... | collective-permute-start | bytes 258056 | tf_op jit(solution)/shard_map/ppermute | solution.py:93
  147.1 7.9 %collective-permute-start.23 = (bf16[56,768]{1,0:T(8,128)(2,1)S(1)}, bf16[56,768]{1,0:T(8,128)(2,1)S(1)}, u32[]{:S(2)}, u32[]{:S(2)}) collective-permute-start(bf16[56,768]{1,0:T(8,128)(2,1)S(1)} %get-tuple-element.78), channel_id=1, source_target_pairs={{0,24},{8,0},{16,8},{24,16},{1,25},{9,1},{17,9},{25,17},{2,26},{10... | collective-permute-start | bytes 258056 | tf_op jit(solution)/shard_map/ppermute | solution.py:93
  155.1 4.1 %collective-permute-start.24 = (f32[44,768]{1,0:T(8,128)S(1)}, f32[44,768]{1,0:T(8,128)S(1)}, u32[]{:S(2)}, u32[]{:S(2)}) collective-permute-start(f32[44,768]{1,0:T(8,128)S(1)} %pad_maximum_fusion.10), channel_id=1, source_target_pairs={{0,1},{1,0},{2,3},{3,2},{4,5},{5,4},{6,7},{7,6},{8,9},{9,8},{10,11... | collective-permute-start | bytes 405512 | tf_op jit(solution)/shard_map/ppermute | solution.py:104
  (15 other events, 89.3 us)

commit v4 on v3

--- a/solution.py
+++ b/solution.py
@@ -75,7 +75,7 @@
     return out
 
 
-def z_sum(v, small):
+def z_sum(v, small, beside):
     count, chans = small.shape
     zl = lax.axis_index("zl")
     zh = lax.axis_index("zh")
@@ -83,7 +83,9 @@
     near = lax.dynamic_index_in_dim(v, zl, 0, False).reshape(-1, chans)
     low = small.astype(BF)
     got = zl_swap(away)
-    low = add_all([low] + split_move([low] * 4, ("x", "y"))).astype(BF)
+    others = split_move([low] * 4, ("x", "y"))
+    got, others, beside = lax.optimization_barrier((got, others, beside))
+    low = add_all([low] + others).astype(BF)
     v = (near.astype(F32) + got.astype(F32)).astype(BF).reshape(v.shape[1:])
     acc = lax.dynamic_index_in_dim(v, zh, 0, False).astype(F32)
     sums = low.astype(F32)
@@ -93,7 +95,7 @@
         got = lax.ppermute(sent, "zh", [(i, (i + k) % 4) for i in range(4)])
         sums = sums + got[:count].astype(F32)
         acc = acc + got[count:].astype(F32)
-    return acc, sums
+    return acc, sums, beside
 
 
 def zl_swap(v):
@@ -228,7 +230,7 @@
             pltpu.VMEM((blocks, rows, cols, 128), F32),
             pltpu.VMEM((8, 8, chans), F32),
         ],
-        compiler_params=pltpu.CompilerParams(vmem_limit_bytes=40 * 1024 * 1024),
+        compiler_params=pltpu.CompilerParams(vmem_limit_bytes=16 * 1024 * 1024),
         cost_estimate=pl.CostEstimate(
             flops=2 * KS * KS * rows * cols * chans, bytes_accessed=8 * 1024 * 1024, transcendentals=0
         ),
@@ -300,7 +302,7 @@
         functools.partial(conv_kernel, ahead),
         out_shape=(out, jax.ShapeDtypeStruct(shape, BF)) if ahead else out,
         scratch_shapes=[pltpu.VMEM((chans // 128, high, shape[1] + 8, 128), F32)],
-        compiler_params=pltpu.CompilerParams(vmem_limit_bytes=32 * 1024 * 1024),
+        compiler_params=pltpu.CompilerParams(vmem_limit_bytes=14 * 1024 * 1024),
         cost_estimate=pl.CostEstimate(
             flops=2 * KS * KS * math.prod(shape), bytes_accessed=16 * 1024 * 1024, transcendentals=0
         ),
@@ -372,7 +374,7 @@
         ],
         out_specs=[pl.BlockSpec((rows, chans), lambda g: (0, 0))] * 4,
         out_shape=[pltpu.HBM((rows, chans), BF)] * 4,
-        compiler_params=pltpu.CompilerParams(vmem_limit_bytes=40 * 1024 * 1024),
+        compiler_params=pltpu.CompilerParams(vmem_limit_bytes=22 * 1024 * 1024),
         cost_estimate=pl.CostEstimate(
             flops=2 * pixels * hid * chans, bytes_accessed=18 * 1024 * 1024, transcendentals=0
         ),
@@ -453,11 +455,11 @@
 
     moved = split_send(term, small, ("y", "x"), (1, 2))
     got = split_move(moved, ("y", "x"))
-    grad_image = conv(False, d_pad, kernel, cotangent)
-    got, grad_image = lax.optimization_barrier((got, grad_image))
     term, small = split_add(moved, got, small.shape[0])
     term = term.astype(BF).reshape(2, 4, 2 * per, chans)
-    term, small = z_sum(term, small)
+    d_pad, _ = lax.optimization_barrier((d_pad, term))
+    grad_image = conv(False, d_pad, kernel, cotangent)
+    term, small, grad_image = z_sum(term, small, grad_image)
     term = term * scale
     top, low = term[:per], term[per:]
     got = core_swap(jnp.concatenate([small, jnp.where(first, low, top)], axis=0))

time: 164 us -> 159 us (0.970); the launches traced: 162 us -> 159 us
  waiting for transfers between devices: 21.9 us -> 17.5 us
    ppermute x8, waiting for transfers between devices: 10.7 us -> 6.16 us  [shift(): lax.ppermute(v, axes, [(i, i + d) for i in range(n) if 0 <= i + d < n])]
    ppermute x3, starting transfers between devices: 6.33 us -> 9.72 us  [core_swap(): return lax.ppermute(v, 'c', [(0, 1), (1, 0)])]
    ppermute x9, waiting for transfers between devices: 1.53 us -> 4.18 us  [split_move(): lax.ppermute(moved[k], AXES, core_pairs(k, lead))]
    ppermute x3, starting transfers between devices: 8.31 us -> 5.77 us  [z_sum(): got = lax.ppermute(sent, 'zh', [(i, (i + k) % 4) for i in range(4)])]
    ppermute x2, waiting for transfers between devices: 2.43 us -> 0.01 us  [zl_swap(): return lax.ppermute(v, 'zl', [(0, 1), (1, 0)])]
  transfers between devices with their start and end apart: 25 -> 25, of which waited for: 11 -> 8; matrix products, arithmetic and copies ran while one was open for 12% -> 13% of each run, Pallas kernels for 9% -> 10%
where the time goes in v4:
time: 159 us
  starting transfers between devices  61.8 us (39%)
  Pallas kernels  33.8 us (21%)
  matrix products  23.4 us (15%)
  waiting for transfers between devices  17.5 us (11%)
  other arithmetic  10.5 us (7%)
  local copies, waits for them, and re-layouts  10.2 us (6%)
    ppermute x9, starting transfers between devices, split_move(): lax.ppermute(moved[k], AXES, core_pairs(k, lead))  23.2 us
    ppermute x8, starting transfers between devices, shift(): lax.ppermute(v, axes, [(i, i + d) for i in range(n) if 0 <= i + d < n])  21 us
    pallas_call x2, Pallas kernels, conv(): pl.pallas_call(functools.partial(conv_kernel, ahead), out_shape=(out, jax...  14.3 us
    pallas_call x1, Pallas kernels, chunks(): pl.pallas_call(chunk_kernel, grid=(8,), in_specs=[pl.BlockSpec(memory_spa...  10.4 us
    ppermute x3, starting transfers between devices, core_swap(): return lax.ppermute(v, 'c', [(0, 1), (1, 0)])  9.72 us
    pallas_call x1, Pallas kernels, backward(): pl.pallas_call(functools.partial(backward_kernel, scale), out_shape=(jax....  9.07 us
    dot_general x1, matrix products, on_device(): d_normed = jnp.dot(d_pre, w_expand, preferred_element_type=F32)  6.25 us
    dot_general x1, matrix products, on_device(): lax.dot_general(hidden, w_reduce, (((1,), (1,)), ((), ())), preferred_ele...  6.25 us
  transfers between devices with their start and end apart: 25, of which 8 were waited for; matrix products, arithmetic and copies ran while one was open for 13% of the time, Pallas kernels for 10%

profile of v4, /device:TPU:1, one launch (start us, length us, event | category | flops | bytes accessed | tf_op | source)
XLA Modules:
  0.0 158.5 jit_solution(14627932214568795825)
XLA Ops:
  1.8 4.5 %collective-permute-start = (bf16[16,3,768]{2,1,0:T(4,128)(2,1)S(1)}, bf16[16,3,768]{2,1,0:T(4,128)(2,1)S(1)}, u32[]{:S(2)}, u32[]{:S(2)}) collective-permute-start(bf16[16,3,768]{2,1,0:T(4,128)(2,1)S(1)} %get-tuple-element.69), channel_id=1, source_target_pairs={{0,1},{1,2},{2,3},{3,4},{4,5},{5,6},{6,7},{7,8},{8,9},{9,10},{10,1... | collective-permute-start | bytes 221192 | tf_op jit(solution)/shard_map/ppermute | solution.py:111
  6.3 1.9 %collective-permute-start.1 = (bf16[16,3,768]{2,1,0:T(4,128)(2,1)S(1)}, bf16[16,3,768]{2,1,0:T(4,128)(2,1)S(1)}, u32[]{:S(2)}, u32[]{:S(2)}) collective-permute-start(bf16[16,3,768]{2,1,0:T(4,128)(2,1)S(1)} %get-tuple-element.70), channel_id=1, source_target_pairs={{1,0},{2,1},{3,2},{4,3},{5,4},{6,5},{7,6},{8,7},{9,8},{10,9},{11,1... | collective-permute-start | bytes 221192 | tf_op jit(solution)/shard_map/ppermute | solution.py:111
  13.5 3.3 %collective-permute-start.2 = (bf16[3,30,768]{2,1,0:T(8,128)(2,1)S(1)}, bf16[3,30,768]{2,1,0:T(8,128)(2,1)S(1)}, u32[]{:S(2)}, u32[]{:S(2)}) collective-permute-start(bf16[3,30,768]{2,1,0:T(8,128)(2,1)S(1)} %get-tuple-element.65), channel_id=1, source_target_pairs={{0,32},{32,64},{64,96},{96,128},{128,160},{160,192},{192,224},{1,3... | collective-permute-start | bytes 414728 | tf_op jit(solution)/shard_map/ppermute | solution.py:111
  16.8 1.3 collective-permute-start.3
  19.3 3.4 %collective-permute-done.3 = bf16[3,30,768]{2,1,0:T(8,128)(2,1)S(1)} collective-permute-done((bf16[3,30,768]{2,1,0:T(8,128)(2,1)S(1)}, bf16[3,30,768]{2,1,0:T(8,128)(2,1)S(1)}, u32[]{:S(2)}, u32[]{:S(2)}) %collective-permute-start.3) | collective-permute-done | bytes 138272 | tf_op jit(solution)/shard_map/ppermute | solution.py:111
  23.1 8.0 %conv_norm.1 = (f32[16,24,768]{2,1,0:T(8,128)S(1)}, bf16[16,24,768]{2,1,0:T(8,128)(2,1)S(1)}) custom-call(bf16[22,30,768]{2,1,0:T(8,128)(2,1)S(1)} %pad_maximum_fusion.pad_ref, f32[49,768]{1,0:T(8,128)S(1)} %reshape.97.w_ref, f32[8,768]{1,0:T(8,128)S(1)} %stack.45.refs_0_), custom_call_target="tpu_custom_call" | custom-call | flops 28901376 | bytes 16777216 | tf_op jit(solution)/shard_map/conv_norm/pallas_call | solution.py:301
  32.2 2.8 %multiply_convert_fusion = (bf16[384,3072]{1,0:T(8,128)(2,1)S(1)}, f32[384,3072]{1,0:T(8,128)S(1)}) fusion(f32[3072]{0:T(1024)S(1)} %copy-done.19, bf16[384,768]{1,0:T(8,128)(2,1)S(1)} %bitcast.71, bf16[3072,768]{1,0:T(8,128)(2,1)S(1)} %copy-done.18), kind=kOutput, calls=%fused_computation.9 | convolution fusion | flops 1819017216 | bytes 12398592 | tf_op jit(solution)/shard_map/dot_general | solution.py:413
  35.0 3.6 %convert_reduce_fusion = (f32[3072]{0:T(1024)S(1)}, bf16[384,3072]{1,0:T(8,128)(2,1)S(1)}) fusion(f32[384,3072]{1,0:T(8,128)S(1)} %get-tuple-element.87, bf16[384,768]{1,0:T(8,128)(2,1)S(1)} %fusion.8.db_ref, bf16[768,3072]{1,0:T(8,128)(2,1)S(1)} %bitcast.81), kind=kOutput, calls=%fused_computation.8 | convolution fusion | flops 1826092032 | bytes 12398592 | tf_op jit(solution)/shard_map/dot_general | solution.py:420
  38.7 4.5 %convolution_convert_fusion = bf16[3072,768]{1,0:T(8,128)(2,1)} fusion(bf16[384,3072]{1,0:T(8,128)(2,1)S(1)} %get-tuple-element.86.hid_ref, bf16[384,3072]{1,0:T(8,128)(2,1)S(1)} %get-tuple-element.89.pre_ref, pred[]{:T(512)S(6)} %eq.2, bf16[384,768]{1,0:T(8,128)(2,1)S(1)} %fusion.8.db_ref, bf16[384,768]{1,0:T(8,128)(2,1)S(1)} %bitcast.72), kind=kOutput, calls=%fused_computation.1 | convolution fusion | flops 1815773184 | bytes 10616833 | tf_op jit(solution)/shard_map/dot_general | solution.py:133
  43.5 6.3 %fusion.18 = f32[384,768]{1,0:T(8,128)} fusion(bf16[384,3072]{1,0:T(8,128)(2,1)} %copy-done.2, bf16[3072,768]{1,0:T(8,128)(2,1)} %param.16), kind=kOutput, calls=%fused_computation.78 | convolution fusion | flops 1811939328 | bytes 8257536 | tf_op jit(solution)/shard_map/dot_general | solution.py:428
  49.8 1.7 %collective-permute-done.4.come_ref = bf16[3072,768]{1,0:T(8,128)(2,1)} collective-permute-done((bf16[3072,768]{1,0:T(8,128)(2,1)}, bf16[3072,768]{1,0:T(8,128)(2,1)}, u32[]{:S(2)}, u32[]{:S(2)}) %collective-permute-start.4) | collective-permute-done | bytes 4718624 | tf_op jit(solution)/shard_map/ppermute | solution.py:106
  51.5 10.4 %chunks.1 = (bf16[768,768]{1,0:T(8,128)(2,1)}, bf16[768,768]{1,0:T(8,128)(2,1)}, bf16[768,768]{1,0:T(8,128)(2,1)}, bf16[768,768]{1,0:T(8,128)(2,1)}) custom-call(s32[3]{0:T(128)S(1)} %pad_add_fusion.at_ref, bf16[384,3072]{1,0:T(8,128)(2,1)S(1)} %copy-done.3, bf16[384,3072]{1,0:T(8,128)(2,1)S(1)} %get-tuple-element.86.hid_ref, bf16[384,768]{1,0:T(8,128)(2,1)S(1)} %bitcast.73, ...), custom_call_target="tpu_custom_call" | custom-call | flops 1811939328 | bytes 18874368 | tf_op jit(solution)/shard_map/chunks/pallas_call | solution.py:364
  63.2 4.7 %collective-permute-start.6 = (bf16[768,768]{1,0:T(8,128)(2,1)}, bf16[768,768]{1,0:T(8,128)(2,1)}, u32[]{:S(2)}, u32[]{:S(2)}) collective-permute-start(bf16[768,768]{1,0:T(8,128)(2,1)} %get-tuple-element.34), channel_id=1, source_target_pairs={{0,4},{1,65},{2,6},{3,67},{4,0},{5,69},{6,2},{7,71},{8,12},{9,73},... | collective-permute-start | bytes 3538952 | tf_op jit(solution)/shard_map/ppermute | solution.py:58
  68.0 6.3 %fusion.19 = f32[384,768]{1,0:T(8,128)} fusion(bf16[384,3072]{1,0:T(8,128)(2,1)} %copy-done.1, bf16[768,3072]{1,0:T(8,128)(2,1)} %param.18), kind=kOutput, calls=%fused_computation.79 | convolution fusion | flops 1811939328 | bytes 8257536 | tf_op jit(solution)/shard_map/dot_general | solution.py:425
  76.8 9.1 %backward.1 = (f32[64,768]{1,0:T(8,128)S(1)}, bf16[16,24,768]{2,1,0:T(8,128)(2,1)S(1)}) custom-call(bf16[22,30,768]{2,1,0:T(8,128)(2,1)S(1)} %pad_maximum_fusion.pad_ref, f32[16,24,768]{2,1,0:T(8,128)S(1)} %copy-done.9, f32[16,24,768]{2,1,0:T(8,128)S(1)} %bitcast.69, f32[16,24,768]{2,1,0:T(8,128)S(1)} %bitcast.70, bf16[16,24,768]{2,1,0:T(8,128)(2,1)S(1)} %copy-done, ...), custom_call_target="tpu_custom_call" | custom-call | flops 28901376 | bytes 8388608 | tf_op jit(solution)/shard_map/backward/pallas_call | solution.py:222
  85.9 3.3 %collective-permute-start.8 = (f32[32,768]{1,0:T(8,128)S(1)}, f32[32,768]{1,0:T(8,128)S(1)}, u32[]{:S(2)}, u32[]{:S(2)}) collective-permute-start(f32[32,768]{1,0:T(8,128)S(1)} %slice_select_fusion.2), channel_id=1, source_target_pairs={{0,1},{1,0},{2,3},{3,2},{4,5},{5,4},{6,7},{7,6},{8,9},{9,8},{10,11... | collective-permute-start | bytes 294920 | tf_op jit(solution)/shard_map/ppermute | solution.py:106
  89.2 3.6 %collective-permute-start.10 = (bf16[16,3,768]{2,1,0:T(4,128)(2,1)S(1)}, bf16[16,3,768]{2,1,0:T(4,128)(2,1)S(1)}, u32[]{:S(2)}, u32[]{:S(2)}) collective-permute-start(bf16[16,3,768]{2,1,0:T(4,128)(2,1)S(1)} %get-tuple-element.67), channel_id=1, source_target_pairs={{0,1},{1,2},{2,3},{3,4},{4,5},{5,6},{6,7},{7,8},{8,9},{9,10},{10,1... | collective-permute-start | bytes 221192 | tf_op jit(solution)/shard_map/ppermute | solution.py:111
  92.8 1.9 %collective-permute-start.11 = (bf16[16,3,768]{2,1,0:T(4,128)(2,1)S(1)}, bf16[16,3,768]{2,1,0:T(4,128)(2,1)S(1)}, u32[]{:S(2)}, u32[]{:S(2)}) collective-permute-start(bf16[16,3,768]{2,1,0:T(4,128)(2,1)S(1)} %get-tuple-element.68), channel_id=1, source_target_pairs={{1,0},{2,1},{3,2},{4,3},{5,4},{6,5},{7,6},{8,7},{9,8},{10,9},{11,1... | collective-permute-start | bytes 221192 | tf_op jit(solution)/shard_map/ppermute | solution.py:111
  94.8 2.1 %collective-permute-start.9 = (bf16[32,768]{1,0:T(8,128)(2,1)S(1)}, bf16[32,768]{1,0:T(8,128)(2,1)S(1)}, u32[]{:S(2)}, u32[]{:S(2)}) collective-permute-start(bf16[32,768]{1,0:T(8,128)(2,1)S(1)} %add_convert_fusion.4), channel_id=1, source_target_pairs={{0,128},{128,0},{1,129},{129,1},{2,130},{130,2},{3,131},{131,3},{4... | collective-permute-start | bytes 147464 | tf_op jit(solution)/shard_map/ppermute | solution.py:102
  96.9 1.9 %collective-permute-done.11 = bf16[16,3,768]{2,1,0:T(4,128)(2,1)S(1)} collective-permute-done((bf16[16,3,768]{2,1,0:T(4,128)(2,1)S(1)}, bf16[16,3,768]{2,1,0:T(4,128)(2,1)S(1)}, u32[]{:S(2)}, u32[]{:S(2)}) %collective-permute-start.11) | collective-permute-done | bytes 73760 | tf_op jit(solution)/shard_map/ppermute | solution.py:111
  99.2 2.6 %add_convert_fusion = bf16[768,768]{1,0:T(8,128)(2,1)S(1)} fusion(bf16[768,768]{1,0:T(8,128)(2,1)} %collective-permute-done.7, bf16[768,768]{1,0:T(8,128)(2,1)} %collective-permute-done.6, bf16[768,768]{1,0:T(8,128)(2,1)} %collective-permute-done.5, bf16[768,768]{1,0:T(8,128)(2,1)S(1)} %copy-done.15), kind=kLoop, calls=%fused_computation.12 | loop fusion | flops 4718592 | bytes 5898240 | tf_op jit(solution)/shard_map/convert_element_type | solution.py:454
  103.2 12.5 %collective-permute-start.13 = (bf16[224,768]{1,0:T(8,128)(2,1)}, bf16[224,768]{1,0:T(8,128)(2,1)}, u32[]{:S(2)}, u32[]{:S(2)}) collective-permute-start(bf16[224,768]{1,0:T(8,128)(2,1)} %get-tuple-element.85), channel_id=1, source_target_pairs={{0,64},{1,5},{2,66},{3,7},{4,68},{5,1},{6,70},{7,3},{8,72},{9,13},... | collective-permute-start | bytes 1032200 | tf_op jit(solution)/shard_map/ppermute | solution.py:58
  115.7 3.1 %collective-permute-start.19 = (bf16[3,30,768]{2,1,0:T(8,128)(2,1)S(1)}, bf16[3,30,768]{2,1,0:T(8,128)(2,1)S(1)}, u32[]{:S(2)}, u32[]{:S(2)}) collective-permute-start(bf16[3,30,768]{2,1,0:T(8,128)(2,1)S(1)} %get-tuple-element.63), channel_id=1, source_target_pairs={{0,32},{32,64},{64,96},{96,128},{128,160},{160,192},{192,224},{1,3... | collective-permute-start | bytes 414728 | tf_op jit(solution)/shard_map/ppermute | solution.py:111
  118.9 1.3 collective-permute-start.20
  120.2 4.2 %collective-permute-done.13 = bf16[224,768]{1,0:T(8,128)(2,1)} collective-permute-done((bf16[224,768]{1,0:T(8,128)(2,1)}, bf16[224,768]{1,0:T(8,128)(2,1)}, u32[]{:S(2)}, u32[]{:S(2)}) %collective-permute-start.13) | collective-permute-done | bytes 344096 | tf_op jit(solution)/shard_map/ppermute | solution.py:58
  126.6 1.3 collective-permute-start.16
  127.9 2.5 %collective-permute-start.17 = (bf16[32,768]{1,0:T(8,128)(2,1)S(1)}, bf16[32,768]{1,0:T(8,128)(2,1)S(1)}, u32[]{:S(2)}, u32[]{:S(2)}) collective-permute-start(bf16[32,768]{1,0:T(8,128)(2,1)S(1)} %add_convert_fusion.3), channel_id=1, source_target_pairs={{0,4},{1,65},{2,6},{3,67},{4,0},{5,69},{6,2},{7,71},{8,12},{9,73},... | collective-permute-start | bytes 147464 | tf_op jit(solution)/shard_map/ppermute | solution.py:58
  131.7 6.3 %conv_image.1 = f32[16,24,768]{2,1,0:T(8,128)} custom-call(bf16[22,30,768]{2,1,0:T(8,128)(2,1)S(1)} %pad_maximum_fusion.1.pad_ref, f32[49,768]{1,0:T(8,128)S(1)} %copy-done.7, bf16[16,24,768]{2,1,0:T(8,128)(2,1)S(1)} %copy-done), custom_call_target="tpu_custom_call" | custom-call | flops 28901376 | bytes 16777216 | tf_op jit(solution)/shard_map/conv_image/pallas_call | solution.py:301
  138.2 2.4 %collective-permute-start.21 = (bf16[56,768]{1,0:T(8,128)(2,1)S(1)}, bf16[56,768]{1,0:T(8,128)(2,1)S(1)}, u32[]{:S(2)}, u32[]{:S(2)}) collective-permute-start(bf16[56,768]{1,0:T(8,128)(2,1)S(1)} %get-tuple-element.80), channel_id=1, source_target_pairs={{0,8},{8,16},{16,24},{24,0},{1,9},{9,17},{17,25},{25,1},{2,10},{10... | collective-permute-start | bytes 258056 | tf_op jit(solution)/shard_map/ppermute | solution.py:95
  140.6 3.4 %collective-permute-start.23 = (bf16[56,768]{1,0:T(8,128)(2,1)S(1)}, bf16[56,768]{1,0:T(8,128)(2,1)S(1)}, u32[]{:S(2)}, u32[]{:S(2)}) collective-permute-start(bf16[56,768]{1,0:T(8,128)(2,1)S(1)} %get-tuple-element.82), channel_id=1, source_target_pairs={{0,24},{8,0},{16,8},{24,16},{1,25},{9,1},{17,9},{25,17},{2,26},{10... | collective-permute-start | bytes 258056 | tf_op jit(solution)/shard_map/ppermute | solution.py:95
  144.5 3.8 %collective-permute-done.22 = bf16[56,768]{1,0:T(8,128)(2,1)S(1)} collective-permute-done((bf16[56,768]{1,0:T(8,128)(2,1)S(1)}, bf16[56,768]{1,0:T(8,128)(2,1)S(1)}, u32[]{:S(2)}, u32[]{:S(2)}) %collective-permute-start.22) | collective-permute-done | bytes 86048 | tf_op jit(solution)/shard_map/ppermute | solution.py:95
  148.4 6.5 %collective-permute-start.24 = (f32[44,768]{1,0:T(8,128)S(1)}, f32[44,768]{1,0:T(8,128)S(1)}, u32[]{:S(2)}, u32[]{:S(2)}) collective-permute-start(f32[44,768]{1,0:T(8,128)S(1)} %pad_maximum_fusion.10), channel_id=1, source_target_pairs={{0,1},{1,0},{2,3},{3,2},{4,5},{5,4},{6,7},{7,6},{8,9},{9,8},{10,11... | collective-permute-start | bytes 405512 | tf_op jit(solution)/shard_map/ppermute | solution.py:106
  (117 shorter events, 22.9 us)
Async XLA Ops:
  0.6 22.1 %copy-start.14 = (bf16[16,24,768]{2,1,0:T(8,128)(2,1)S(1)}, bf16[16,24,768]{2,1,0:T(8,128)(2,1)}, u32[]{:S(2)}) copy-start(bf16[16,24,768]{2,1,0:T(8,128)(2,1)} %param.11) | copy-start | bytes 1769476
  1.8 9.6 %collective-permute-start = (bf16[16,3,768]{2,1,0:T(4,128)(2,1)S(1)}, bf16[16,3,768]{2,1,0:T(4,128)(2,1)S(1)}, u32[]{:S(2)}, u32[]{:S(2)}) collective-permute-start(bf16[16,3,768]{2,1,0:T(4,128)(2,1)S(1)} %get-tuple-element.69), channel_id=1, source_target_pairs={{0,1},{1,2},{2,3},{3,4},{4,5},{5,6},{6,7},{7,8},{8,9},{9,10},{10,1... | collective-permute-start | bytes 221192 | tf_op jit(solution)/shard_map/ppermute | solution.py:111
  6.3 5.9 %collective-permute-start.1 = (bf16[16,3,768]{2,1,0:T(4,128)(2,1)S(1)}, bf16[16,3,768]{2,1,0:T(4,128)(2,1)S(1)}, u32[]{:S(2)}, u32[]{:S(2)}) collective-permute-start(bf16[16,3,768]{2,1,0:T(4,128)(2,1)S(1)} %get-tuple-element.70), channel_id=1, source_target_pairs={{1,0},{2,1},{3,2},{4,3},{5,4},{6,5},{7,6},{8,7},{9,8},{10,9},{11,1... | collective-permute-start | bytes 221192 | tf_op jit(solution)/shard_map/ppermute | solution.py:111
  9.2 22.0 %copy-start.6 = (f32[49,768]{1,0:T(8,128)}, f32[49,768]{1,0:T(8,128)S(1)}, u32[]{:S(2)}) copy-start(f32[49,768]{1,0:T(8,128)S(1)} %reshape.97.w_ref) | copy-start | bytes 451588
  12.3 19.9 %copy-start.18 = (bf16[3072,768]{1,0:T(8,128)(2,1)S(1)}, bf16[3072,768]{1,0:T(8,128)(2,1)}, u32[]{:S(2)}) copy-start(bf16[3072,768]{1,0:T(8,128)(2,1)} %param.16) | copy-start | bytes 14155780
  13.5 18.7 %copy-start.19 = (f32[3072]{0:T(1024)S(1)}, f32[3072]{0:T(1024)}, u32[]{:S(2)}) copy-start(f32[3072]{0:T(1024)} %param.17) | copy-start | bytes 36868
  13.5 5.8 %collective-permute-start.2 = (bf16[3,30,768]{2,1,0:T(8,128)(2,1)S(1)}, bf16[3,30,768]{2,1,0:T(8,128)(2,1)S(1)}, u32[]{:S(2)}, u32[]{:S(2)}) collective-permute-start(bf16[3,30,768]{2,1,0:T(8,128)(2,1)S(1)} %get-tuple-element.65), channel_id=1, source_target_pairs={{0,32},{32,64},{64,96},{96,128},{128,160},{160,192},{192,224},{1,3... | collective-permute-start | bytes 414728 | tf_op jit(solution)/shard_map/ppermute | solution.py:111
  16.8 5.9 %collective-permute-start.3 = (bf16[3,30,768]{2,1,0:T(8,128)(2,1)S(1)}, bf16[3,30,768]{2,1,0:T(8,128)(2,1)S(1)}, u32[]{:S(2)}, u32[]{:S(2)}) collective-permute-start(bf16[3,30,768]{2,1,0:T(8,128)(2,1)S(1)} %get-tuple-element.66), channel_id=1, source_target_pairs={{32,0},{64,32},{96,64},{128,96},{160,128},{192,160},{224,192},{33,... | collective-permute-start | bytes 414728 | tf_op jit(solution)/shard_map/ppermute | solution.py:111
  19.3 19.4 %copy-start.4 = (bf16[384,768]{1,0:T(8,128)(2,1)}, bf16[384,768]{1,0:T(8,128)(2,1)S(1)}, u32[]{:S(2)}) copy-start(bf16[384,768]{1,0:T(8,128)(2,1)S(1)} %fusion.8.db_ref) | copy-start | bytes 1769476
  35.0 16.5 %copy-start.1 = (bf16[384,3072]{1,0:T(8,128)(2,1)}, bf16[384,3072]{1,0:T(8,128)(2,1)S(1)}, u32[]{:S(2)}) copy-start(bf16[384,3072]{1,0:T(8,128)(2,1)S(1)} %get-tuple-element.86.hid_ref) | copy-start | bytes 7077892
  43.3 8.3 %collective-permute-start.4 = (bf16[3072,768]{1,0:T(8,128)(2,1)}, bf16[3072,768]{1,0:T(8,128)(2,1)}, u32[]{:S(2)}, u32[]{:S(2)}) collective-permute-start(bf16[3072,768]{1,0:T(8,128)(2,1)} %convolution_convert_fusion), channel_id=1, source_target_pairs={{0,1},{1,0},{2,3},{3,2},{4,5},{5,4},{6,7},{7,6},{8,9},{9,8},{10,11... | collective-permute-start | bytes 14155784 | tf_op jit(solution)/shard_map/ppermute | solution.py:106
  61.9 37.2 %collective-permute-start.5 = (bf16[768,768]{1,0:T(8,128)(2,1)}, bf16[768,768]{1,0:T(8,128)(2,1)}, u32[]{:S(2)}, u32[]{:S(2)}) collective-permute-start(bf16[768,768]{1,0:T(8,128)(2,1)} %get-tuple-element.33), channel_id=1, source_target_pairs={{0,2},{1,33},{2,4},{3,35},{4,6},{5,37},{6,0},{7,39},{8,10},{9,41},... | collective-permute-start | bytes 3538952 | tf_op jit(solution)/shard_map/ppermute | solution.py:58
  63.2 35.9 %collective-permute-start.6 = (bf16[768,768]{1,0:T(8,128)(2,1)}, bf16[768,768]{1,0:T(8,128)(2,1)}, u32[]{:S(2)}, u32[]{:S(2)}) collective-permute-start(bf16[768,768]{1,0:T(8,128)(2,1)} %get-tuple-element.34), channel_id=1, source_target_pairs={{0,4},{1,65},{2,6},{3,67},{4,0},{5,69},{6,2},{7,71},{8,12},{9,73},... | collective-permute-start | bytes 3538952 | tf_op jit(solution)/shard_map/ppermute | solution.py:58
  68.0 31.2 %collective-permute-start.7 = (bf16[768,768]{1,0:T(8,128)(2,1)}, bf16[768,768]{1,0:T(8,128)(2,1)}, u32[]{:S(2)}, u32[]{:S(2)}) collective-permute-start(bf16[768,768]{1,0:T(8,128)(2,1)} %get-tuple-element.35), channel_id=1, source_target_pairs={{0,6},{1,97},{2,0},{3,99},{4,2},{5,101},{6,4},{7,103},{8,14},{9,10... | collective-permute-start | bytes 3538952 | tf_op jit(solution)/shard_map/ppermute | solution.py:58
  85.8 13.3 %copy-start.15 = (bf16[768,768]{1,0:T(8,128)(2,1)S(1)}, bf16[768,768]{1,0:T(8,128)(2,1)}, u32[]{:S(2)}) copy-start(bf16[768,768]{1,0:T(8,128)(2,1)} %get-tuple-element.32) | copy-start | bytes 3538948
  85.9 6.9 %collective-permute-start.8 = (f32[32,768]{1,0:T(8,128)S(1)}, f32[32,768]{1,0:T(8,128)S(1)}, u32[]{:S(2)}, u32[]{:S(2)}) collective-permute-start(f32[32,768]{1,0:T(8,128)S(1)} %slice_select_fusion.2), channel_id=1, source_target_pairs={{0,1},{1,0},{2,3},{3,2},{4,5},{5,4},{6,7},{7,6},{8,9},{9,8},{10,11... | collective-permute-start | bytes 294920 | tf_op jit(solution)/shard_map/ppermute | solution.py:106
  89.2 5.5 %collective-permute-start.10 = (bf16[16,3,768]{2,1,0:T(4,128)(2,1)S(1)}, bf16[16,3,768]{2,1,0:T(4,128)(2,1)S(1)}, u32[]{:S(2)}, u32[]{:S(2)}) collective-permute-start(bf16[16,3,768]{2,1,0:T(4,128)(2,1)S(1)} %get-tuple-element.67), channel_id=1, source_target_pairs={{0,1},{1,2},{2,3},{3,4},{4,5},{5,6},{6,7},{7,8},{8,9},{9,10},{10,1... | collective-permute-start | bytes 221192 | tf_op jit(solution)/shard_map/ppermute | solution.py:111
  92.8 5.9 %collective-permute-start.11 = (bf16[16,3,768]{2,1,0:T(4,128)(2,1)S(1)}, bf16[16,3,768]{2,1,0:T(4,128)(2,1)S(1)}, u32[]{:S(2)}, u32[]{:S(2)}) collective-permute-start(bf16[16,3,768]{2,1,0:T(4,128)(2,1)S(1)} %get-tuple-element.68), channel_id=1, source_target_pairs={{1,0},{2,1},{3,2},{4,3},{5,4},{6,5},{7,6},{8,7},{9,8},{10,9},{11,1... | collective-permute-start | bytes 221192 | tf_op jit(solution)/shard_map/ppermute | solution.py:111
  94.8 4.3 %collective-permute-start.9 = (bf16[32,768]{1,0:T(8,128)(2,1)S(1)}, bf16[32,768]{1,0:T(8,128)(2,1)S(1)}, u32[]{:S(2)}, u32[]{:S(2)}) collective-permute-start(bf16[32,768]{1,0:T(8,128)(2,1)S(1)} %add_convert_fusion.4), channel_id=1, source_target_pairs={{0,128},{128,0},{1,129},{129,1},{2,130},{130,2},{3,131},{131,3},{4... | collective-permute-start | bytes 147464 | tf_op jit(solution)/shard_map/ppermute | solution.py:102
  103.2 16.9 %collective-permute-start.12 = (bf16[224,768]{1,0:T(8,128)(2,1)}, bf16[224,768]{1,0:T(8,128)(2,1)S(1)}, u32[]{:S(2)}, u32[]{:S(2)}) collective-permute-start(bf16[224,768]{1,0:T(8,128)(2,1)} %get-tuple-element.83), channel_id=1, source_target_pairs={{0,32},{1,3},{2,34},{3,5},{4,36},{5,7},{6,38},{7,1},{8,40},{9,11},... | collective-permute-start | bytes 1032200 | tf_op jit(solution)/shard_map/ppermute | solution.py:58
  103.2 21.1 %collective-permute-start.13 = (bf16[224,768]{1,0:T(8,128)(2,1)}, bf16[224,768]{1,0:T(8,128)(2,1)}, u32[]{:S(2)}, u32[]{:S(2)}) collective-permute-start(bf16[224,768]{1,0:T(8,128)(2,1)} %get-tuple-element.85), channel_id=1, source_target_pairs={{0,64},{1,5},{2,66},{3,7},{4,68},{5,1},{6,70},{7,3},{8,72},{9,13},... | collective-permute-start | bytes 1032200 | tf_op jit(solution)/shard_map/ppermute | solution.py:58
  115.7 8.6 %collective-permute-start.14 = (bf16[224,768]{1,0:T(8,128)(2,1)}, bf16[224,768]{1,0:T(8,128)(2,1)}, u32[]{:S(2)}, u32[]{:S(2)}) collective-permute-start(bf16[224,768]{1,0:T(8,128)(2,1)} %get-tuple-element.84), channel_id=1, source_target_pairs={{0,96},{1,7},{2,98},{3,1},{4,100},{5,3},{6,102},{7,5},{8,104},{9,1... | collective-permute-start | bytes 1032200 | tf_op jit(solution)/shard_map/ppermute | solution.py:58
  115.7 14.7 %collective-permute-start.19 = (bf16[3,30,768]{2,1,0:T(8,128)(2,1)S(1)}, bf16[3,30,768]{2,1,0:T(8,128)(2,1)S(1)}, u32[]{:S(2)}, u32[]{:S(2)}) collective-permute-start(bf16[3,30,768]{2,1,0:T(8,128)(2,1)S(1)} %get-tuple-element.63), channel_id=1, source_target_pairs={{0,32},{32,64},{64,96},{96,128},{128,160},{160,192},{192,224},{1,3... | collective-permute-start | bytes 414728 | tf_op jit(solution)/shard_map/ppermute | solution.py:111
  118.9 12.4 %collective-permute-start.20 = (bf16[3,30,768]{2,1,0:T(8,128)(2,1)S(1)}, bf16[3,30,768]{2,1,0:T(8,128)(2,1)S(1)}, u32[]{:S(2)}, u32[]{:S(2)}) collective-permute-start(bf16[3,30,768]{2,1,0:T(8,128)(2,1)S(1)} %get-tuple-element.64), channel_id=1, source_target_pairs={{32,0},{64,32},{96,64},{128,96},{160,128},{192,160},{224,192},{33,... | collective-permute-start | bytes 414728 | tf_op jit(solution)/shard_map/ppermute | solution.py:111
  125.7 12.4 %collective-permute-start.15 = (bf16[96,768]{1,0:T(8,128)(2,1)S(1)}, bf16[96,768]{1,0:T(8,128)(2,1)S(1)}, u32[]{:S(2)}, u32[]{:S(2)}) collective-permute-start(bf16[96,768]{1,0:T(8,128)(2,1)S(1)} %bitcast.79), channel_id=1, source_target_pairs={{0,128},{128,0},{1,129},{129,1},{2,130},{130,2},{3,131},{131,3},{4... | collective-permute-start | bytes 442376 | tf_op jit(solution)/shard_map/ppermute | solution.py:102
  126.6 11.4 %collective-permute-start.16 = (bf16[32,768]{1,0:T(8,128)(2,1)S(1)}, bf16[32,768]{1,0:T(8,128)(2,1)S(1)}, u32[]{:S(2)}, u32[]{:S(2)}) collective-permute-start(bf16[32,768]{1,0:T(8,128)(2,1)S(1)} %add_convert_fusion.3), channel_id=1, source_target_pairs={{0,2},{1,33},{2,4},{3,35},{4,6},{5,37},{6,0},{7,39},{8,10},{9,41},... | collective-permute-start | bytes 147464 | tf_op jit(solution)/shard_map/ppermute | solution.py:58
  127.9 10.1 %collective-permute-start.17 = (bf16[32,768]{1,0:T(8,128)(2,1)S(1)}, bf16[32,768]{1,0:T(8,128)(2,1)S(1)}, u32[]{:S(2)}, u32[]{:S(2)}) collective-permute-start(bf16[32,768]{1,0:T(8,128)(2,1)S(1)} %add_convert_fusion.3), channel_id=1, source_target_pairs={{0,4},{1,65},{2,6},{3,67},{4,0},{5,69},{6,2},{7,71},{8,12},{9,73},... | collective-permute-start | bytes 147464 | tf_op jit(solution)/shard_map/ppermute | solution.py:58
  130.4 7.6 %collective-permute-start.18 = (bf16[32,768]{1,0:T(8,128)(2,1)S(1)}, bf16[32,768]{1,0:T(8,128)(2,1)S(1)}, u32[]{:S(2)}, u32[]{:S(2)}) collective-permute-start(bf16[32,768]{1,0:T(8,128)(2,1)S(1)} %add_convert_fusion.3), channel_id=1, source_target_pairs={{0,6},{1,97},{2,0},{3,99},{4,2},{5,101},{6,4},{7,103},{8,14},{9,10... | collective-permute-start | bytes 147464 | tf_op jit(solution)/shard_map/ppermute | solution.py:58
  138.2 6.3 %collective-permute-start.21 = (bf16[56,768]{1,0:T(8,128)(2,1)S(1)}, bf16[56,768]{1,0:T(8,128)(2,1)S(1)}, u32[]{:S(2)}, u32[]{:S(2)}) collective-permute-start(bf16[56,768]{1,0:T(8,128)(2,1)S(1)} %get-tuple-element.80), channel_id=1, source_target_pairs={{0,8},{8,16},{16,24},{24,0},{1,9},{9,17},{17,25},{25,1},{2,10},{10... | collective-permute-start | bytes 258056 | tf_op jit(solution)/shard_map/ppermute | solution.py:95
  140.6 7.8 %collective-permute-start.22 = (bf16[56,768]{1,0:T(8,128)(2,1)S(1)}, bf16[56,768]{1,0:T(8,128)(2,1)S(1)}, u32[]{:S(2)}, u32[]{:S(2)}) collective-permute-start(bf16[56,768]{1,0:T(8,128)(2,1)S(1)} %get-tuple-element.81), channel_id=1, source_target_pairs={{0,16},{8,24},{16,0},{24,8},{1,17},{9,25},{17,1},{25,9},{2,18},{10... | collective-permute-start | bytes 258056 | tf_op jit(solution)/shard_map/ppermute | solution.py:95
  140.6 7.8 %collective-permute-start.23 = (bf16[56,768]{1,0:T(8,128)(2,1)S(1)}, bf16[56,768]{1,0:T(8,128)(2,1)S(1)}, u32[]{:S(2)}, u32[]{:S(2)}) collective-permute-start(bf16[56,768]{1,0:T(8,128)(2,1)S(1)} %get-tuple-element.82), channel_id=1, source_target_pairs={{0,24},{8,0},{16,8},{24,16},{1,25},{9,1},{17,9},{25,17},{2,26},{10... | collective-permute-start | bytes 258056 | tf_op jit(solution)/shard_map/ppermute | solution.py:95
  148.4 7.5 %collective-permute-start.24 = (f32[44,768]{1,0:T(8,128)S(1)}, f32[44,768]{1,0:T(8,128)S(1)}, u32[]{:S(2)}, u32[]{:S(2)}) collective-permute-start(f32[44,768]{1,0:T(8,128)S(1)} %pad_maximum_fusion.10), channel_id=1, source_target_pairs={{0,1},{1,0},{2,3},{3,2},{4,5},{5,4},{6,7},{7,6},{8,9},{9,8},{10,11... | collective-permute-start | bytes 405512 | tf_op jit(solution)/shard_map/ppermute | solution.py:106
  (15 other events, 82.3 us)

commit v5 on v4

--- a/solution.py
+++ b/solution.py
@@ -75,7 +75,7 @@
     return out
 
 
-def z_sum(v, small, beside):
+def z_sum(v, small, work):
     count, chans = small.shape
     zl = lax.axis_index("zl")
     zh = lax.axis_index("zh")
@@ -84,17 +84,17 @@
     low = small.astype(BF)
     got = zl_swap(away)
     others = split_move([low] * 4, ("x", "y"))
-    got, others, beside = lax.optimization_barrier((got, others, beside))
     low = add_all([low] + others).astype(BF)
     v = (near.astype(F32) + got.astype(F32)).astype(BF).reshape(v.shape[1:])
-    acc = lax.dynamic_index_in_dim(v, zh, 0, False).astype(F32)
-    sums = low.astype(F32)
+    kept = jnp.concatenate([low, lax.dynamic_index_in_dim(v, zh, 0, False)], axis=0)
+    back = []
     for k in range(1, 4):
         part = lax.dynamic_index_in_dim(v, lax.rem(zh + k, 4), 0, False)
         sent = jnp.concatenate([low, part], axis=0)
-        got = lax.ppermute(sent, "zh", [(i, (i + k) % 4) for i in range(4)])
-        sums = sums + got[:count].astype(F32)
-        acc = acc + got[count:].astype(F32)
+        back.append(lax.ppermute(sent, "zh", [(i, (i + k) % 4) for i in range(4)]))
+    beside = work(v)
+    back, beside = lax.optimization_barrier((back, beside))
+    acc, sums = split_add([kept], back, count)
     return acc, sums, beside
 
 
@@ -310,7 +310,8 @@
     )(padded, weights, extra)
 
 
-def chunk_kernel(at_ref, pre_ref, hid_ref, normed_ref, db_ref, come_ref, *outs):
+def chunk_kernel(at_ref, pre_ref, hid_ref, normed_ref, db_ref, come_ref, *rest):
+    outs, held, sems = rest[:4], rest[4], rest[5]
     unit = hid_ref.shape[1] // 16
     core = at_ref[0]
     me = (at_ref[1], at_ref[2])
@@ -322,13 +323,7 @@
     v = v + come_ref[...].astype(F32)
 
     def store(k, row, value):
-        value = value.astype(BF)
-        rows = pl.ds(pl.multiple_of(row, 16), 2 * unit)
-        for n in range(4):
-
-            @pl.when(k == n)
-            def _(n=n):
-                outs[n][rows, :] = value
+        held[k, pl.ds(pl.multiple_of(row, 16), 2 * unit), :] = value.astype(BF)
 
     def part(zh, x):
         t = zh * 4 + x
@@ -349,6 +344,14 @@
             for x in (0, 2):
                 t = zh * 4 + x
                 store(k, ((group // 4) * 16 + t) * unit, v[t * unit : (t + 2) * unit])
+
+    @pl.when(group == pl.num_programs(0) - 1)
+    def _():
+        copies = [pltpu.make_async_copy(held.at[n], outs[n], sems.at[n]) for n in range(4)]
+        for copy in copies:
+            copy.start()
+        for copy in copies:
+            copy.wait()
 
 
 def chunks(d_pre, hidden, normed, d_branch, come):
@@ -372,8 +375,9 @@
             whole,
             pl.BlockSpec((wide, chans), lambda g: (g, 0)),
         ],
-        out_specs=[pl.BlockSpec((rows, chans), lambda g: (0, 0))] * 4,
+        out_specs=[pl.BlockSpec(memory_space=pl.ANY)] * 4,
         out_shape=[pltpu.HBM((rows, chans), BF)] * 4,
+        scratch_shapes=[pltpu.VMEM((4, rows, chans), BF), pltpu.SemaphoreType.DMA((4,))],
         compiler_params=pltpu.CompilerParams(vmem_limit_bytes=22 * 1024 * 1024),
         cost_estimate=pl.CostEstimate(
             flops=2 * pixels * hid * chans, bytes_accessed=18 * 1024 * 1024, transcendentals=0
@@ -457,9 +461,11 @@
     got = split_move(moved, ("y", "x"))
     term, small = split_add(moved, got, small.shape[0])
     term = term.astype(BF).reshape(2, 4, 2 * per, chans)
-    d_pad, _ = lax.optimization_barrier((d_pad, term))
-    grad_image = conv(False, d_pad, kernel, cotangent)
-    term, small, grad_image = z_sum(term, small, grad_image)
+
+    def image_part(after):
+        return conv(False, lax.optimization_barrier((d_pad, after))[0], kernel, cotangent)
+
+    term, small, grad_image = z_sum(term, small, image_part)
     term = term * scale
     top, low = term[:per], term[per:]
     got = core_swap(jnp.concatenate([small, jnp.where(first, low, top)], axis=0))

time: 159 us -> 165 us (1.038)
  the two profiles are of different devices: /device:TPU:1 before, /device:TPU:25 now
where the time goes in v5:
time: 165 us
  starting transfers between devices  63.4 us (38%)
  Pallas kernels  35.8 us (22%)
  matrix products  22.5 us (14%)
  waiting for transfers between devices  19.6 us (12%)
  local copies, waits for them, and re-layouts  11.5 us (7%)
  other arithmetic  10.5 us (6%)
    ppermute x8, starting transfers between devices, shift(): lax.ppermute(v, axes, [(i, i + d) for i in range(n) if 0 <= i + d < n])  21.8 us
    ppermute x3, starting transfers between devices, core_swap(): return lax.ppermute(v, 'c', [(0, 1), (1, 0)])  21.3 us
    pallas_call x2, Pallas kernels, conv(): pl.pallas_call(functools.partial(conv_kernel, ahead), out_shape=(out, jax...  16.4 us
    ppermute x9, starting transfers between devices, split_move(): lax.ppermute(moved[k], AXES, core_pairs(k, lead))  13.8 us
    pallas_call x1, Pallas kernels, chunks(): pl.pallas_call(chunk_kernel, grid=(8,), in_specs=[pl.BlockSpec(memory_spa...  9.93 us
    ppermute x8, waiting for transfers between devices, shift(): lax.ppermute(v, axes, [(i, i + d) for i in range(n) if 0 <= i + d < n])  9.54 us
    pallas_call x1, Pallas kernels, backward(): pl.pallas_call(functools.partial(backward_kernel, scale), out_shape=(jax....  9.48 us
    ppermute x3, starting transfers between devices, z_sum(): back.append(lax.ppermute(sent, 'zh', [(i, (i + k) % 4) for i in range(4)]))  6.27 us
  transfers between devices with their start and end apart: 25, of which 9 were waited for; matrix products, arithmetic and copies ran while one was open for 12% of the time, Pallas kernels for 10%

profile of v5, /device:TPU:25, one launch (start us, length us, event | category | flops | bytes accessed | tf_op | source)
XLA Modules:
  0.0 164.5 jit_solution(9572038672286703102)
XLA Ops:
  1.8 3.7 %collective-permute-start = (bf16[16,3,768]{2,1,0:T(4,128)(2,1)S(1)}, bf16[16,3,768]{2,1,0:T(4,128)(2,1)S(1)}, u32[]{:S(2)}, u32[]{:S(2)}) collective-permute-start(bf16[16,3,768]{2,1,0:T(4,128)(2,1)S(1)} %get-tuple-element.67), channel_id=1, source_target_pairs={{0,1},{1,2},{2,3},{3,4},{4,5},{5,6},{6,7},{7,8},{8,9},{9,10},{10,1... | collective-permute-start | bytes 221192 | tf_op jit(solution)/shard_map/ppermute | solution.py:111
  5.5 1.9 %collective-permute-start.1 = (bf16[16,3,768]{2,1,0:T(4,128)(2,1)S(1)}, bf16[16,3,768]{2,1,0:T(4,128)(2,1)S(1)}, u32[]{:S(2)}, u32[]{:S(2)}) collective-permute-start(bf16[16,3,768]{2,1,0:T(4,128)(2,1)S(1)} %get-tuple-element.68), channel_id=1, source_target_pairs={{1,0},{2,1},{3,2},{4,3},{5,4},{6,5},{7,6},{8,7},{9,8},{10,9},{11,1... | collective-permute-start | bytes 221192 | tf_op jit(solution)/shard_map/ppermute | solution.py:111
  12.7 3.3 %collective-permute-start.2 = (bf16[3,30,768]{2,1,0:T(8,128)(2,1)S(1)}, bf16[3,30,768]{2,1,0:T(8,128)(2,1)S(1)}, u32[]{:S(2)}, u32[]{:S(2)}) collective-permute-start(bf16[3,30,768]{2,1,0:T(8,128)(2,1)S(1)} %get-tuple-element.63), channel_id=1, source_target_pairs={{0,32},{32,64},{64,96},{96,128},{128,160},{160,192},{192,224},{1,3... | collective-permute-start | bytes 414728 | tf_op jit(solution)/shard_map/ppermute | solution.py:111
  16.0 2.1 %collective-permute-start.3 = (bf16[3,30,768]{2,1,0:T(8,128)(2,1)S(1)}, bf16[3,30,768]{2,1,0:T(8,128)(2,1)S(1)}, u32[]{:S(2)}, u32[]{:S(2)}) collective-permute-start(bf16[3,30,768]{2,1,0:T(8,128)(2,1)S(1)} %get-tuple-element.64), channel_id=1, source_target_pairs={{32,0},{64,32},{96,64},{128,96},{160,128},{192,160},{224,192},{33,... | collective-permute-start | bytes 414728 | tf_op jit(solution)/shard_map/ppermute | solution.py:111
  19.3 4.7 %collective-permute-done.3 = bf16[3,30,768]{2,1,0:T(8,128)(2,1)S(1)} collective-permute-done((bf16[3,30,768]{2,1,0:T(8,128)(2,1)S(1)}, bf16[3,30,768]{2,1,0:T(8,128)(2,1)S(1)}, u32[]{:S(2)}, u32[]{:S(2)}) %collective-permute-start.3) | collective-permute-done | bytes 138272 | tf_op jit(solution)/shard_map/ppermute | solution.py:111
  24.4 9.5 %conv_norm.1 = (f32[16,24,768]{2,1,0:T(8,128)S(1)}, bf16[16,24,768]{2,1,0:T(8,128)(2,1)S(1)}) custom-call(bf16[22,30,768]{2,1,0:T(8,128)(2,1)S(1)} %pad_maximum_fusion.pad_ref, f32[49,768]{1,0:T(8,128)S(1)} %reshape.97.w_ref, f32[8,768]{1,0:T(8,128)S(1)} %stack.49.refs_0_), custom_call_target="tpu_custom_call" | custom-call | flops 28901376 | bytes 16777216 | tf_op jit(solution)/shard_map/conv_norm/pallas_call | solution.py:301
  34.9 2.8 %multiply_convert_fusion = (bf16[384,3072]{1,0:T(8,128)(2,1)S(1)}, f32[384,3072]{1,0:T(8,128)S(1)}) fusion(f32[3072]{0:T(1024)S(1)} %copy-done.14, bf16[384,768]{1,0:T(8,128)(2,1)S(1)} %bitcast.71, bf16[3072,768]{1,0:T(8,128)(2,1)S(1)} %copy-done.13), kind=kOutput, calls=%fused_computation.9 | convolution fusion | flops 1819017216 | bytes 12398592 | tf_op jit(solution)/shard_map/dot_general | solution.py:417
  37.7 3.6 %convert_reduce_fusion = (f32[3072]{0:T(1024)S(1)}, bf16[384,3072]{1,0:T(8,128)(2,1)S(1)}) fusion(f32[384,3072]{1,0:T(8,128)S(1)} %get-tuple-element.85, bf16[384,768]{1,0:T(8,128)(2,1)S(1)} %fusion.8.db_ref, bf16[768,3072]{1,0:T(8,128)(2,1)S(1)} %bitcast.81), kind=kOutput, calls=%fused_computation.8 | convolution fusion | flops 1826092032 | bytes 12398592 | tf_op jit(solution)/shard_map/dot_general | solution.py:424
  41.4 4.5 %convolution_convert_fusion = bf16[3072,768]{1,0:T(8,128)(2,1)} fusion(bf16[384,3072]{1,0:T(8,128)(2,1)S(1)} %get-tuple-element.84.hid_ref, bf16[384,3072]{1,0:T(8,128)(2,1)S(1)} %get-tuple-element.87.pre_ref, pred[]{:T(512)S(6)} %eq.2, bf16[384,768]{1,0:T(8,128)(2,1)S(1)} %fusion.8.db_ref, bf16[384,768]{1,0:T(8,128)(2,1)S(1)} %bitcast.72), kind=kOutput, calls=%fused_computation.1 | convolution fusion | flops 1815773184 | bytes 10616833 | tf_op jit(solution)/shard_map/dot_general | solution.py:133
  46.1 6.2 %fusion.18 = f32[384,768]{1,0:T(8,128)} fusion(bf16[384,3072]{1,0:T(8,128)(2,1)} %copy-done.3, bf16[3072,768]{1,0:T(8,128)(2,1)} %param.16), kind=kOutput, calls=%fused_computation.78 | convolution fusion | flops 1811939328 | bytes 8257536 | tf_op jit(solution)/shard_map/dot_general | solution.py:432
  52.4 1.8 %collective-permute-done.4.come_ref = bf16[3072,768]{1,0:T(8,128)(2,1)} collective-permute-done((bf16[3072,768]{1,0:T(8,128)(2,1)}, bf16[3072,768]{1,0:T(8,128)(2,1)}, u32[]{:S(2)}, u32[]{:S(2)}) %collective-permute-start.4) | collective-permute-done | bytes 4718624 | tf_op jit(solution)/shard_map/ppermute | solution.py:106
  54.1 9.9 %chunks.1 = (bf16[768,768]{1,0:T(8,128)(2,1)}, bf16[768,768]{1,0:T(8,128)(2,1)}, bf16[768,768]{1,0:T(8,128)(2,1)}, bf16[768,768]{1,0:T(8,128)(2,1)}) custom-call(s32[3]{0:T(128)S(1)} %pad_add_fusion.at_ref, bf16[384,3072]{1,0:T(8,128)(2,1)S(1)} %copy-done.4, bf16[384,3072]{1,0:T(8,128)(2,1)S(1)} %copy-done.2, bf16[384,768]{1,0:T(8,128)(2,1)S(1)} %bitcast.73, ...), custom_call_target="tpu_custom_call" | custom-call | flops 1811939328 | bytes 18874368 | tf_op jit(solution)/shard_map/chunks/pallas_call | solution.py:367
  64.3 1.3 collective-permute-start.7
  65.6 5.4 %fusion.19 = f32[384,768]{1,0:T(8,128)} fusion(bf16[384,3072]{1,0:T(8,128)(2,1)S(1)} %copy-done.2, bf16[768,3072]{1,0:T(8,128)(2,1)} %param.18), kind=kOutput, calls=%fused_computation.79 | convolution fusion | flops 1811939328 | bytes 8257536 | tf_op jit(solution)/shard_map/dot_general | solution.py:429
  74.8 9.5 %backward.1 = (f32[64,768]{1,0:T(8,128)S(1)}, bf16[16,24,768]{2,1,0:T(8,128)(2,1)S(1)}) custom-call(bf16[22,30,768]{2,1,0:T(8,128)(2,1)S(1)} %pad_maximum_fusion.pad_ref, f32[16,24,768]{2,1,0:T(8,128)S(1)} %copy-done.6, f32[16,24,768]{2,1,0:T(8,128)S(1)} %bitcast.69, f32[16,24,768]{2,1,0:T(8,128)S(1)} %bitcast.70, bf16[16,24,768]{2,1,0:T(8,128)(2,1)S(1)} %copy-done, ...), custom_call_target="tpu_custom_call" | custom-call | flops 28901376 | bytes 8388608 | tf_op jit(solution)/shard_map/backward/pallas_call | solution.py:222
  84.3 7.7 %collective-permute-start.8 = (f32[32,768]{1,0:T(8,128)S(1)}, f32[32,768]{1,0:T(8,128)S(1)}, u32[]{:S(2)}, u32[]{:S(2)}) collective-permute-start(f32[32,768]{1,0:T(8,128)S(1)} %slice_select_fusion.2), channel_id=1, source_target_pairs={{0,1},{1,0},{2,3},{3,2},{4,5},{5,4},{6,7},{7,6},{8,9},{9,8},{10,11... | collective-permute-start | bytes 294920 | tf_op jit(solution)/shard_map/ppermute | solution.py:106
  92.1 3.6 %collective-permute-start.10 = (bf16[16,3,768]{2,1,0:T(4,128)(2,1)S(1)}, bf16[16,3,768]{2,1,0:T(4,128)(2,1)S(1)}, u32[]{:S(2)}, u32[]{:S(2)}) collective-permute-start(bf16[16,3,768]{2,1,0:T(4,128)(2,1)S(1)} %get-tuple-element.65), channel_id=1, source_target_pairs={{0,1},{1,2},{2,3},{3,4},{4,5},{5,6},{6,7},{7,8},{8,9},{9,10},{10,1... | collective-permute-start | bytes 221192 | tf_op jit(solution)/shard_map/ppermute | solution.py:111
  95.8 1.9 %collective-permute-start.11 = (bf16[16,3,768]{2,1,0:T(4,128)(2,1)S(1)}, bf16[16,3,768]{2,1,0:T(4,128)(2,1)S(1)}, u32[]{:S(2)}, u32[]{:S(2)}) collective-permute-start(bf16[16,3,768]{2,1,0:T(4,128)(2,1)S(1)} %get-tuple-element.66), channel_id=1, source_target_pairs={{1,0},{2,1},{3,2},{4,3},{5,4},{6,5},{7,6},{8,7},{9,8},{10,9},{11,1... | collective-permute-start | bytes 221192 | tf_op jit(solution)/shard_map/ppermute | solution.py:111
  97.8 3.9 %collective-permute-done.11 = bf16[16,3,768]{2,1,0:T(4,128)(2,1)S(1)} collective-permute-done((bf16[16,3,768]{2,1,0:T(4,128)(2,1)S(1)}, bf16[16,3,768]{2,1,0:T(4,128)(2,1)S(1)}, u32[]{:S(2)}, u32[]{:S(2)}) %collective-permute-start.11) | collective-permute-done | bytes 73760 | tf_op jit(solution)/shard_map/ppermute | solution.py:111
  102.2 2.6 %add_convert_fusion = bf16[768,768]{1,0:T(8,128)(2,1)S(1)} fusion(bf16[768,768]{1,0:T(8,128)(2,1)} %collective-permute-done.7, bf16[768,768]{1,0:T(8,128)(2,1)} %collective-permute-done.6, bf16[768,768]{1,0:T(8,128)(2,1)} %collective-permute-done.5, bf16[768,768]{1,0:T(8,128)(2,1)S(1)} %copy-done.10), kind=kLoop, calls=%fused_computation.12 | loop fusion | flops 4718592 | bytes 5898240 | tf_op jit(solution)/shard_map/convert_element_type | solution.py:458
  106.2 10.1 %collective-permute-start.13 = (bf16[224,768]{1,0:T(8,128)(2,1)}, bf16[224,768]{1,0:T(8,128)(2,1)}, u32[]{:S(2)}, u32[]{:S(2)}) collective-permute-start(bf16[224,768]{1,0:T(8,128)(2,1)} %get-tuple-element.83), channel_id=1, source_target_pairs={{0,64},{1,5},{2,66},{3,7},{4,68},{5,1},{6,70},{7,3},{8,72},{9,13},... | collective-permute-start | bytes 1032200 | tf_op jit(solution)/shard_map/ppermute | solution.py:58
  116.3 1.9 %collective-permute-start.22 = (bf16[3,30,768]{2,1,0:T(8,128)(2,1)S(1)}, bf16[3,30,768]{2,1,0:T(8,128)(2,1)S(1)}, u32[]{:S(2)}, u32[]{:S(2)}) collective-permute-start(bf16[3,30,768]{2,1,0:T(8,128)(2,1)S(1)} %get-tuple-element.61), channel_id=1, source_target_pairs={{0,32},{32,64},{64,96},{96,128},{128,160},{160,192},{192,224},{1,3... | collective-permute-start | bytes 414728 | tf_op jit(solution)/shard_map/ppermute | solution.py:111
  118.2 3.4 %collective-permute-start.23 = (bf16[3,30,768]{2,1,0:T(8,128)(2,1)S(1)}, bf16[3,30,768]{2,1,0:T(8,128)(2,1)S(1)}, u32[]{:S(2)}, u32[]{:S(2)}) collective-permute-start(bf16[3,30,768]{2,1,0:T(8,128)(2,1)S(1)} %get-tuple-element.62), channel_id=1, source_target_pairs={{32,0},{64,32},{96,64},{128,96},{160,128},{192,160},{224,192},{33,... | collective-permute-start | bytes 414728 | tf_op jit(solution)/shard_map/ppermute | solution.py:111
  121.6 3.4 %collective-permute-done.13 = bf16[224,768]{1,0:T(8,128)(2,1)} collective-permute-done((bf16[224,768]{1,0:T(8,128)(2,1)}, bf16[224,768]{1,0:T(8,128)(2,1)}, u32[]{:S(2)}, u32[]{:S(2)}) %collective-permute-start.13) | collective-permute-done | bytes 344096 | tf_op jit(solution)/shard_map/ppermute | solution.py:58
  126.1 2.0 %collective-permute-start.16 = (bf16[32,768]{1,0:T(8,128)(2,1)S(1)}, bf16[32,768]{1,0:T(8,128)(2,1)S(1)}, u32[]{:S(2)}, u32[]{:S(2)}) collective-permute-start(bf16[32,768]{1,0:T(8,128)(2,1)S(1)} %add_convert_fusion.3), channel_id=1, source_target_pairs={{0,4},{1,65},{2,6},{3,67},{4,0},{5,69},{6,2},{7,71},{8,12},{9,73},... | collective-permute-start | bytes 147464 | tf_op jit(solution)/shard_map/ppermute | solution.py:58
  128.1 1.3 add_convert_fusion.1
  130.5 1.7 %collective-permute-done.17 = bf16[32,768]{1,0:T(8,128)(2,1)S(1)} collective-permute-done((bf16[32,768]{1,0:T(8,128)(2,1)S(1)}, bf16[32,768]{1,0:T(8,128)(2,1)S(1)}, u32[]{:S(2)}, u32[]{:S(2)}) %collective-permute-start.17) | collective-permute-done | bytes 49184 | tf_op jit(solution)/shard_map/ppermute | solution.py:58
  132.3 1.3 collective-permute-done.18
  133.6 2.9 %collective-permute-start.19 = (bf16[56,768]{1,0:T(8,128)(2,1)S(1)}, bf16[56,768]{1,0:T(8,128)(2,1)S(1)}, u32[]{:S(2)}, u32[]{:S(2)}) collective-permute-start(bf16[56,768]{1,0:T(8,128)(2,1)S(1)} %get-tuple-element.80), channel_id=1, source_target_pairs={{0,8},{8,16},{16,24},{24,0},{1,9},{9,17},{17,25},{25,1},{2,10},{10... | collective-permute-start | bytes 258056 | tf_op jit(solution)/shard_map/ppermute | solution.py:94
  136.5 3.4 %collective-permute-start.21 = (bf16[56,768]{1,0:T(8,128)(2,1)S(1)}, bf16[56,768]{1,0:T(8,128)(2,1)S(1)}, u32[]{:S(2)}, u32[]{:S(2)}) collective-permute-start(bf16[56,768]{1,0:T(8,128)(2,1)S(1)} %get-tuple-element.78), channel_id=1, source_target_pairs={{0,24},{8,0},{16,8},{24,16},{1,25},{9,1},{17,9},{25,17},{2,26},{10... | collective-permute-start | bytes 258056 | tf_op jit(solution)/shard_map/ppermute | solution.py:94
  140.3 6.9 %conv_image.1 = f32[16,24,768]{2,1,0:T(8,128)} custom-call(bf16[22,30,768]{2,1,0:T(8,128)(2,1)S(1)} %pad_maximum_fusion.1.pad_ref, f32[49,768]{1,0:T(8,128)S(1)} %reshape.97.w_ref, bf16[16,24,768]{2,1,0:T(8,128)(2,1)S(1)} %copy-done), custom_call_target="tpu_custom_call" | custom-call | flops 28901376 | bytes 16777216 | tf_op jit(solution)/shard_map/conv_image/pallas_call | solution.py:301
  147.3 13.6 %collective-permute-start.24 = (f32[44,768]{1,0:T(8,128)S(1)}, f32[44,768]{1,0:T(8,128)S(1)}, u32[]{:S(2)}, u32[]{:S(2)}) collective-permute-start(f32[44,768]{1,0:T(8,128)S(1)} %pad_maximum_fusion.10), channel_id=1, source_target_pairs={{0,1},{1,0},{2,3},{3,2},{4,5},{5,4},{6,7},{7,6},{8,9},{9,8},{10,11... | collective-permute-start | bytes 405512 | tf_op jit(solution)/shard_map/ppermute | solution.py:106
  (107 shorter events, 21.5 us)
Async XLA Ops:
  0.6 23.4 %copy-start.9 = (bf16[16,24,768]{2,1,0:T(8,128)(2,1)S(1)}, bf16[16,24,768]{2,1,0:T(8,128)(2,1)}, u32[]{:S(2)}) copy-start(bf16[16,24,768]{2,1,0:T(8,128)(2,1)} %param.11) | copy-start | bytes 1769476
  1.8 8.7 %collective-permute-start = (bf16[16,3,768]{2,1,0:T(4,128)(2,1)S(1)}, bf16[16,3,768]{2,1,0:T(4,128)(2,1)S(1)}, u32[]{:S(2)}, u32[]{:S(2)}) collective-permute-start(bf16[16,3,768]{2,1,0:T(4,128)(2,1)S(1)} %get-tuple-element.67), channel_id=1, source_target_pairs={{0,1},{1,2},{2,3},{3,4},{4,5},{5,6},{6,7},{7,8},{8,9},{9,10},{10,1... | collective-permute-start | bytes 221192 | tf_op jit(solution)/shard_map/ppermute | solution.py:111
  5.5 5.9 %collective-permute-start.1 = (bf16[16,3,768]{2,1,0:T(4,128)(2,1)S(1)}, bf16[16,3,768]{2,1,0:T(4,128)(2,1)S(1)}, u32[]{:S(2)}, u32[]{:S(2)}) collective-permute-start(bf16[16,3,768]{2,1,0:T(4,128)(2,1)S(1)} %get-tuple-element.68), channel_id=1, source_target_pairs={{1,0},{2,1},{3,2},{4,3},{5,4},{6,5},{7,6},{8,7},{9,8},{10,9},{11,1... | collective-permute-start | bytes 221192 | tf_op jit(solution)/shard_map/ppermute | solution.py:111
  11.4 23.5 %copy-start.13 = (bf16[3072,768]{1,0:T(8,128)(2,1)S(1)}, bf16[3072,768]{1,0:T(8,128)(2,1)}, u32[]{:S(2)}) copy-start(bf16[3072,768]{1,0:T(8,128)(2,1)} %param.16) | copy-start | bytes 14155780
  12.7 22.3 %copy-start.14 = (f32[3072]{0:T(1024)S(1)}, f32[3072]{0:T(1024)}, u32[]{:S(2)}) copy-start(f32[3072]{0:T(1024)} %param.17) | copy-start | bytes 36868
  12.7 6.6 %collective-permute-start.2 = (bf16[3,30,768]{2,1,0:T(8,128)(2,1)S(1)}, bf16[3,30,768]{2,1,0:T(8,128)(2,1)S(1)}, u32[]{:S(2)}, u32[]{:S(2)}) collective-permute-start(bf16[3,30,768]{2,1,0:T(8,128)(2,1)S(1)} %get-tuple-element.63), channel_id=1, source_target_pairs={{0,32},{32,64},{64,96},{96,128},{128,160},{160,192},{192,224},{1,3... | collective-permute-start | bytes 414728 | tf_op jit(solution)/shard_map/ppermute | solution.py:111
  16.0 8.0 %collective-permute-start.3 = (bf16[3,30,768]{2,1,0:T(8,128)(2,1)S(1)}, bf16[3,30,768]{2,1,0:T(8,128)(2,1)S(1)}, u32[]{:S(2)}, u32[]{:S(2)}) collective-permute-start(bf16[3,30,768]{2,1,0:T(8,128)(2,1)S(1)} %get-tuple-element.64), channel_id=1, source_target_pairs={{32,0},{64,32},{96,64},{128,96},{160,128},{192,160},{224,192},{33,... | collective-permute-start | bytes 414728 | tf_op jit(solution)/shard_map/ppermute | solution.py:111
  24.4 13.3 %slice-start = ((s8[4718592]{0:T(1024)(128)(4,1)}), s8[4194304]{0:T(1024)(128)(4,1)S(1)}, s32[]{:S(2)}) async-start(s8[4718592]{0:T(1024)(128)(4,1)} %bitcast.80), calls=%async_computation | async-start | bytes 8388608
  45.9 8.3 %collective-permute-start.4 = (bf16[3072,768]{1,0:T(8,128)(2,1)}, bf16[3072,768]{1,0:T(8,128)(2,1)}, u32[]{:S(2)}, u32[]{:S(2)}) collective-permute-start(bf16[3072,768]{1,0:T(8,128)(2,1)} %convolution_convert_fusion), channel_id=1, source_target_pairs={{0,1},{1,0},{2,3},{3,2},{4,5},{5,4},{6,7},{7,6},{8,9},{9,8},{10,11... | collective-permute-start | bytes 14155784 | tf_op jit(solution)/shard_map/ppermute | solution.py:106
  46.1 8.0 %copy-start.2 = (bf16[384,3072]{1,0:T(8,128)(2,1)S(1)}, bf16[384,3072]{1,0:T(8,128)(2,1)}, u32[]{:S(2)}) copy-start(bf16[384,3072]{1,0:T(8,128)(2,1)} %copy-done.1) | copy-start | bytes 7077892
  46.1 8.0 %copy-start.4 = (bf16[384,3072]{1,0:T(8,128)(2,1)S(1)}, bf16[384,3072]{1,0:T(8,128)(2,1)}, u32[]{:S(2)}) copy-start(bf16[384,3072]{1,0:T(8,128)(2,1)} %copy-done.3) | copy-start | bytes 7077892
  64.1 38.0 %collective-permute-start.5 = (bf16[768,768]{1,0:T(8,128)(2,1)}, bf16[768,768]{1,0:T(8,128)(2,1)}, u32[]{:S(2)}, u32[]{:S(2)}) collective-permute-start(bf16[768,768]{1,0:T(8,128)(2,1)} %get-tuple-element.30), channel_id=1, source_target_pairs={{0,2},{1,33},{2,4},{3,35},{4,6},{5,37},{6,0},{7,39},{8,10},{9,41},... | collective-permute-start | bytes 3538952 | tf_op jit(solution)/shard_map/ppermute | solution.py:58
  64.2 38.0 %collective-permute-start.6 = (bf16[768,768]{1,0:T(8,128)(2,1)}, bf16[768,768]{1,0:T(8,128)(2,1)}, u32[]{:S(2)}, u32[]{:S(2)}) collective-permute-start(bf16[768,768]{1,0:T(8,128)(2,1)} %get-tuple-element.31), channel_id=1, source_target_pairs={{0,4},{1,65},{2,6},{3,67},{4,0},{5,69},{6,2},{7,71},{8,12},{9,73},... | collective-permute-start | bytes 3538952 | tf_op jit(solution)/shard_map/ppermute | solution.py:58
  64.3 37.9 %collective-permute-start.7 = (bf16[768,768]{1,0:T(8,128)(2,1)}, bf16[768,768]{1,0:T(8,128)(2,1)}, u32[]{:S(2)}, u32[]{:S(2)}) collective-permute-start(bf16[768,768]{1,0:T(8,128)(2,1)} %get-tuple-element.32), channel_id=1, source_target_pairs={{0,6},{1,97},{2,0},{3,99},{4,2},{5,101},{6,4},{7,103},{8,14},{9,10... | collective-permute-start | bytes 3538952 | tf_op jit(solution)/shard_map/ppermute | solution.py:58
  84.3 17.8 %copy-start.10 = (bf16[768,768]{1,0:T(8,128)(2,1)S(1)}, bf16[768,768]{1,0:T(8,128)(2,1)}, u32[]{:S(2)}) copy-start(bf16[768,768]{1,0:T(8,128)(2,1)} %get-tuple-element.39) | copy-start | bytes 3538948
  84.3 11.4 %collective-permute-start.8 = (f32[32,768]{1,0:T(8,128)S(1)}, f32[32,768]{1,0:T(8,128)S(1)}, u32[]{:S(2)}, u32[]{:S(2)}) collective-permute-start(f32[32,768]{1,0:T(8,128)S(1)} %slice_select_fusion.2), channel_id=1, source_target_pairs={{0,1},{1,0},{2,3},{3,2},{4,5},{5,4},{6,7},{7,6},{8,9},{9,8},{10,11... | collective-permute-start | bytes 294920 | tf_op jit(solution)/shard_map/ppermute | solution.py:106
  92.1 5.6 %collective-permute-start.10 = (bf16[16,3,768]{2,1,0:T(4,128)(2,1)S(1)}, bf16[16,3,768]{2,1,0:T(4,128)(2,1)S(1)}, u32[]{:S(2)}, u32[]{:S(2)}) collective-permute-start(bf16[16,3,768]{2,1,0:T(4,128)(2,1)S(1)} %get-tuple-element.65), channel_id=1, source_target_pairs={{0,1},{1,2},{2,3},{3,4},{4,5},{5,6},{6,7},{7,8},{8,9},{9,10},{10,1... | collective-permute-start | bytes 221192 | tf_op jit(solution)/shard_map/ppermute | solution.py:111
  95.8 5.9 %collective-permute-start.11 = (bf16[16,3,768]{2,1,0:T(4,128)(2,1)S(1)}, bf16[16,3,768]{2,1,0:T(4,128)(2,1)S(1)}, u32[]{:S(2)}, u32[]{:S(2)}) collective-permute-start(bf16[16,3,768]{2,1,0:T(4,128)(2,1)S(1)} %get-tuple-element.66), channel_id=1, source_target_pairs={{1,0},{2,1},{3,2},{4,3},{5,4},{6,5},{7,6},{8,7},{9,8},{10,9},{11,1... | collective-permute-start | bytes 221192 | tf_op jit(solution)/shard_map/ppermute | solution.py:111
  97.7 4.3 %collective-permute-start.9 = (bf16[32,768]{1,0:T(8,128)(2,1)S(1)}, bf16[32,768]{1,0:T(8,128)(2,1)S(1)}, u32[]{:S(2)}, u32[]{:S(2)}) collective-permute-start(bf16[32,768]{1,0:T(8,128)(2,1)S(1)} %add_convert_fusion.4), channel_id=1, source_target_pairs={{0,128},{128,0},{1,129},{129,1},{2,130},{130,2},{3,131},{131,3},{4... | collective-permute-start | bytes 147464 | tf_op jit(solution)/shard_map/ppermute | solution.py:102
  106.2 15.4 %collective-permute-start.12 = (bf16[224,768]{1,0:T(8,128)(2,1)}, bf16[224,768]{1,0:T(8,128)(2,1)}, u32[]{:S(2)}, u32[]{:S(2)}) collective-permute-start(bf16[224,768]{1,0:T(8,128)(2,1)} %get-tuple-element.81), channel_id=1, source_target_pairs={{0,32},{1,3},{2,34},{3,5},{4,36},{5,7},{6,38},{7,1},{8,40},{9,11},... | collective-permute-start | bytes 1032200 | tf_op jit(solution)/shard_map/ppermute | solution.py:58
  106.2 18.8 %collective-permute-start.13 = (bf16[224,768]{1,0:T(8,128)(2,1)}, bf16[224,768]{1,0:T(8,128)(2,1)}, u32[]{:S(2)}, u32[]{:S(2)}) collective-permute-start(bf16[224,768]{1,0:T(8,128)(2,1)} %get-tuple-element.83), channel_id=1, source_target_pairs={{0,64},{1,5},{2,66},{3,7},{4,68},{5,1},{6,70},{7,3},{8,72},{9,13},... | collective-permute-start | bytes 1032200 | tf_op jit(solution)/shard_map/ppermute | solution.py:58
  116.3 8.7 %collective-permute-start.14 = (bf16[224,768]{1,0:T(8,128)(2,1)}, bf16[224,768]{1,0:T(8,128)(2,1)}, u32[]{:S(2)}, u32[]{:S(2)}) collective-permute-start(bf16[224,768]{1,0:T(8,128)(2,1)} %get-tuple-element.82), channel_id=1, source_target_pairs={{0,96},{1,7},{2,98},{3,1},{4,100},{5,3},{6,102},{7,5},{8,104},{9,1... | collective-permute-start | bytes 1032200 | tf_op jit(solution)/shard_map/ppermute | solution.py:58
  116.3 23.6 %collective-permute-start.22 = (bf16[3,30,768]{2,1,0:T(8,128)(2,1)S(1)}, bf16[3,30,768]{2,1,0:T(8,128)(2,1)S(1)}, u32[]{:S(2)}, u32[]{:S(2)}) collective-permute-start(bf16[3,30,768]{2,1,0:T(8,128)(2,1)S(1)} %get-tuple-element.61), channel_id=1, source_target_pairs={{0,32},{32,64},{64,96},{96,128},{128,160},{160,192},{192,224},{1,3... | collective-permute-start | bytes 414728 | tf_op jit(solution)/shard_map/ppermute | solution.py:111
  118.2 21.7 %collective-permute-start.23 = (bf16[3,30,768]{2,1,0:T(8,128)(2,1)S(1)}, bf16[3,30,768]{2,1,0:T(8,128)(2,1)S(1)}, u32[]{:S(2)}, u32[]{:S(2)}) collective-permute-start(bf16[3,30,768]{2,1,0:T(8,128)(2,1)S(1)} %get-tuple-element.62), channel_id=1, source_target_pairs={{32,0},{64,32},{96,64},{128,96},{160,128},{192,160},{224,192},{33,... | collective-permute-start | bytes 414728 | tf_op jit(solution)/shard_map/ppermute | solution.py:111
  125.9 3.6 %collective-permute-start.15 = (bf16[32,768]{1,0:T(8,128)(2,1)S(1)}, bf16[32,768]{1,0:T(8,128)(2,1)S(1)}, u32[]{:S(2)}, u32[]{:S(2)}) collective-permute-start(bf16[32,768]{1,0:T(8,128)(2,1)S(1)} %add_convert_fusion.3), channel_id=1, source_target_pairs={{0,2},{1,33},{2,4},{3,35},{4,6},{5,37},{6,0},{7,39},{8,10},{9,41},... | collective-permute-start | bytes 147464 | tf_op jit(solution)/shard_map/ppermute | solution.py:58
  126.1 4.4 %collective-permute-start.16 = (bf16[32,768]{1,0:T(8,128)(2,1)S(1)}, bf16[32,768]{1,0:T(8,128)(2,1)S(1)}, u32[]{:S(2)}, u32[]{:S(2)}) collective-permute-start(bf16[32,768]{1,0:T(8,128)(2,1)S(1)} %add_convert_fusion.3), channel_id=1, source_target_pairs={{0,4},{1,65},{2,6},{3,67},{4,0},{5,69},{6,2},{7,71},{8,12},{9,73},... | collective-permute-start | bytes 147464 | tf_op jit(solution)/shard_map/ppermute | solution.py:58
  128.1 4.2 %collective-permute-start.17 = (bf16[32,768]{1,0:T(8,128)(2,1)S(1)}, bf16[32,768]{1,0:T(8,128)(2,1)S(1)}, u32[]{:S(2)}, u32[]{:S(2)}) collective-permute-start(bf16[32,768]{1,0:T(8,128)(2,1)S(1)} %add_convert_fusion.3), channel_id=1, source_target_pairs={{0,6},{1,97},{2,0},{3,99},{4,2},{5,101},{6,4},{7,103},{8,14},{9,10... | collective-permute-start | bytes 147464 | tf_op jit(solution)/shard_map/ppermute | solution.py:58
  129.5 4.1 %collective-permute-start.18 = (bf16[96,768]{1,0:T(8,128)(2,1)S(1)}, bf16[96,768]{1,0:T(8,128)(2,1)S(1)}, u32[]{:S(2)}, u32[]{:S(2)}) collective-permute-start(bf16[96,768]{1,0:T(8,128)(2,1)S(1)} %bitcast.79), channel_id=1, source_target_pairs={{0,128},{128,0},{1,129},{129,1},{2,130},{130,2},{3,131},{131,3},{4... | collective-permute-start | bytes 442376 | tf_op jit(solution)/shard_map/ppermute | solution.py:102
  133.6 13.6 %collective-permute-start.19 = (bf16[56,768]{1,0:T(8,128)(2,1)S(1)}, bf16[56,768]{1,0:T(8,128)(2,1)S(1)}, u32[]{:S(2)}, u32[]{:S(2)}) collective-permute-start(bf16[56,768]{1,0:T(8,128)(2,1)S(1)} %get-tuple-element.80), channel_id=1, source_target_pairs={{0,8},{8,16},{16,24},{24,0},{1,9},{9,17},{17,25},{25,1},{2,10},{10... | collective-permute-start | bytes 258056 | tf_op jit(solution)/shard_map/ppermute | solution.py:94
  136.5 10.7 %collective-permute-start.20 = (bf16[56,768]{1,0:T(8,128)(2,1)S(1)}, bf16[56,768]{1,0:T(8,128)(2,1)S(1)}, u32[]{:S(2)}, u32[]{:S(2)}) collective-permute-start(bf16[56,768]{1,0:T(8,128)(2,1)S(1)} %get-tuple-element.79), channel_id=1, source_target_pairs={{0,16},{8,24},{16,0},{24,8},{1,17},{9,25},{17,1},{25,9},{2,18},{10... | collective-permute-start | bytes 258056 | tf_op jit(solution)/shard_map/ppermute | solution.py:94
  136.5 10.7 %collective-permute-start.21 = (bf16[56,768]{1,0:T(8,128)(2,1)S(1)}, bf16[56,768]{1,0:T(8,128)(2,1)S(1)}, u32[]{:S(2)}, u32[]{:S(2)}) collective-permute-start(bf16[56,768]{1,0:T(8,128)(2,1)S(1)} %get-tuple-element.78), channel_id=1, source_target_pairs={{0,24},{8,0},{16,8},{24,16},{1,25},{9,1},{17,9},{25,17},{2,26},{10... | collective-permute-start | bytes 258056 | tf_op jit(solution)/shard_map/ppermute | solution.py:94
  147.3 14.6 %collective-permute-start.24 = (f32[44,768]{1,0:T(8,128)S(1)}, f32[44,768]{1,0:T(8,128)S(1)}, u32[]{:S(2)}, u32[]{:S(2)}) collective-permute-start(f32[44,768]{1,0:T(8,128)S(1)} %pad_maximum_fusion.10), channel_id=1, source_target_pairs={{0,1},{1,0},{2,3},{3,2},{4,5},{5,4},{6,7},{7,6},{8,9},{9,8},{10,11... | collective-permute-start | bytes 405512 | tf_op jit(solution)/shard_map/ppermute | solution.py:106
  (10 other events, 31.7 us)

commit v6 on v5

--- a/solution.py
+++ b/solution.py
@@ -77,6 +77,7 @@
 
 def z_sum(v, small, work):
     count, chans = small.shape
+    v, small = lax.optimization_barrier((v, small))
     zl = lax.axis_index("zl")
     zh = lax.axis_index("zh")
     away = lax.dynamic_index_in_dim(v, 1 - zl, 0, False).reshape(-1, chans)
@@ -459,6 +460,7 @@
 
     moved = split_send(term, small, ("y", "x"), (1, 2))
     got = split_move(moved, ("y", "x"))
+    got, d_pad = lax.optimization_barrier((got, d_pad))
     term, small = split_add(moved, got, small.shape[0])
     term = term.astype(BF).reshape(2, 4, 2 * per, chans)
 

time: 165 us -> 160 us (0.970)
  the two profiles are of different devices: /device:TPU:25 before, /device:TPU:1 now
where the time goes in v6:
time: 160 us; the launch traced here: 159 us
  starting transfers between devices  61.7 us (39%)
  Pallas kernels  33.3 us (21%)
  matrix products  22.5 us (14%)
  waiting for transfers between devices  17.6 us (11%)
  local copies, waits for them, and re-layouts  11.4 us (7%)
  other arithmetic  11.4 us (7%)
    ppermute x9, starting transfers between devices, split_move(): lax.ppermute(moved[k], AXES, core_pairs(k, lead))  23.2 us
    ppermute x8, starting transfers between devices, shift(): lax.ppermute(v, axes, [(i, i + d) for i in range(n) if 0 <= i + d < n])  21 us
    pallas_call x2, Pallas kernels, conv(): pl.pallas_call(functools.partial(conv_kernel, ahead), out_shape=(out, jax...  14.3 us
    ppermute x8, waiting for transfers between devices, shift(): lax.ppermute(v, axes, [(i, i + d) for i in range(n) if 0 <= i + d < n])  10.9 us
    pallas_call x1, Pallas kernels, chunks(): pl.pallas_call(chunk_kernel, grid=(8,), in_specs=[pl.BlockSpec(memory_spa...  9.89 us
    pallas_call x1, Pallas kernels, backward(): pl.pallas_call(functools.partial(backward_kernel, scale), out_shape=(jax....  9.07 us
    ppermute x3, starting transfers between devices, core_swap(): return lax.ppermute(v, 'c', [(0, 1), (1, 0)])  7.72 us
    ppermute x3, starting transfers between devices, z_sum(): back.append(lax.ppermute(sent, 'zh', [(i, (i + k) % 4) for i in range(4)]))  7.56 us
  transfers between devices with their start and end apart: 25, of which 11 were waited for; matrix products, arithmetic and copies ran while one was open for 11% of the time, Pallas kernels for 10%

profile of v6, /device:TPU:1, one launch (start us, length us, event | category | flops | bytes accessed | tf_op | source)
XLA Modules:
  0.0 159.3 jit_solution(13839146592078218926)
XLA Ops:
  1.8 4.5 %collective-permute-start = (bf16[16,3,768]{2,1,0:T(4,128)(2,1)S(1)}, bf16[16,3,768]{2,1,0:T(4,128)(2,1)S(1)}, u32[]{:S(2)}, u32[]{:S(2)}) collective-permute-start(bf16[16,3,768]{2,1,0:T(4,128)(2,1)S(1)} %get-tuple-element.79), channel_id=1, source_target_pairs={{0,1},{1,2},{2,3},{3,4},{4,5},{5,6},{6,7},{7,8},{8,9},{9,10},{10,1... | collective-permute-start | bytes 221192 | tf_op jit(solution)/shard_map/ppermute | solution.py:112
  6.3 1.9 %collective-permute-start.1 = (bf16[16,3,768]{2,1,0:T(4,128)(2,1)S(1)}, bf16[16,3,768]{2,1,0:T(4,128)(2,1)S(1)}, u32[]{:S(2)}, u32[]{:S(2)}) collective-permute-start(bf16[16,3,768]{2,1,0:T(4,128)(2,1)S(1)} %get-tuple-element.80), channel_id=1, source_target_pairs={{1,0},{2,1},{3,2},{4,3},{5,4},{6,5},{7,6},{8,7},{9,8},{10,9},{11,1... | collective-permute-start | bytes 221192 | tf_op jit(solution)/shard_map/ppermute | solution.py:112
  13.5 3.3 %collective-permute-start.2 = (bf16[3,30,768]{2,1,0:T(8,128)(2,1)S(1)}, bf16[3,30,768]{2,1,0:T(8,128)(2,1)S(1)}, u32[]{:S(2)}, u32[]{:S(2)}) collective-permute-start(bf16[3,30,768]{2,1,0:T(8,128)(2,1)S(1)} %get-tuple-element.75), channel_id=1, source_target_pairs={{0,32},{32,64},{64,96},{96,128},{128,160},{160,192},{192,224},{1,3... | collective-permute-start | bytes 414728 | tf_op jit(solution)/shard_map/ppermute | solution.py:112
  19.3 3.4 %collective-permute-done.3 = bf16[3,30,768]{2,1,0:T(8,128)(2,1)S(1)} collective-permute-done((bf16[3,30,768]{2,1,0:T(8,128)(2,1)S(1)}, bf16[3,30,768]{2,1,0:T(8,128)(2,1)S(1)}, u32[]{:S(2)}, u32[]{:S(2)}) %collective-permute-start.3) | collective-permute-done | bytes 138272 | tf_op jit(solution)/shard_map/ppermute | solution.py:112
  23.1 8.0 %conv_norm.1 = (f32[16,24,768]{2,1,0:T(8,128)S(1)}, bf16[16,24,768]{2,1,0:T(8,128)(2,1)S(1)}) custom-call(bf16[22,30,768]{2,1,0:T(8,128)(2,1)S(1)} %pad_maximum_fusion.pad_ref, f32[49,768]{1,0:T(8,128)S(1)} %reshape.97.w_ref, f32[8,768]{1,0:T(8,128)S(1)} %stack.45.refs_0_), custom_call_target="tpu_custom_call" | custom-call | flops 28901376 | bytes 16777216 | tf_op jit(solution)/shard_map/conv_norm/pallas_call | solution.py:302
  32.2 2.7 %multiply_convert_fusion = (bf16[384,3072]{1,0:T(8,128)(2,1)S(1)}, f32[384,3072]{1,0:T(8,128)S(1)}) fusion(f32[3072]{0:T(1024)S(1)} %copy-done.14, bf16[384,768]{1,0:T(8,128)(2,1)S(1)} %bitcast.71, bf16[3072,768]{1,0:T(8,128)(2,1)S(1)} %copy-done.13), kind=kOutput, calls=%fused_computation.9 | convolution fusion | flops 1819017216 | bytes 12398592 | tf_op jit(solution)/shard_map/dot_general | solution.py:418
  35.0 3.6 %convert_reduce_fusion = (f32[3072]{0:T(1024)S(1)}, bf16[384,3072]{1,0:T(8,128)(2,1)S(1)}) fusion(f32[384,3072]{1,0:T(8,128)S(1)} %get-tuple-element.97, bf16[384,768]{1,0:T(8,128)(2,1)S(1)} %fusion.8.db_ref, bf16[768,3072]{1,0:T(8,128)(2,1)S(1)} %bitcast.81), kind=kOutput, calls=%fused_computation.8 | convolution fusion | flops 1826092032 | bytes 12398592 | tf_op jit(solution)/shard_map/dot_general | solution.py:425
  38.6 4.5 %convolution_convert_fusion = bf16[3072,768]{1,0:T(8,128)(2,1)} fusion(bf16[384,3072]{1,0:T(8,128)(2,1)S(1)} %get-tuple-element.96.hid_ref, bf16[384,3072]{1,0:T(8,128)(2,1)S(1)} %get-tuple-element.99.pre_ref, pred[]{:T(512)S(6)} %eq.2, bf16[384,768]{1,0:T(8,128)(2,1)S(1)} %fusion.8.db_ref, bf16[384,768]{1,0:T(8,128)(2,1)S(1)} %bitcast.72), kind=kOutput, calls=%fused_computation.1 | convolution fusion | flops 1815773184 | bytes 10616833 | tf_op jit(solution)/shard_map/dot_general | solution.py:134
  43.4 6.2 %fusion.18 = f32[384,768]{1,0:T(8,128)} fusion(bf16[384,3072]{1,0:T(8,128)(2,1)} %copy-done.3, bf16[3072,768]{1,0:T(8,128)(2,1)} %param.16), kind=kOutput, calls=%fused_computation.78 | convolution fusion | flops 1811939328 | bytes 8257536 | tf_op jit(solution)/shard_map/dot_general | solution.py:433
  49.6 1.8 %collective-permute-done.4.come_ref = bf16[3072,768]{1,0:T(8,128)(2,1)} collective-permute-done((bf16[3072,768]{1,0:T(8,128)(2,1)}, bf16[3072,768]{1,0:T(8,128)(2,1)}, u32[]{:S(2)}, u32[]{:S(2)}) %collective-permute-start.4) | collective-permute-done | bytes 4718624 | tf_op jit(solution)/shard_map/ppermute | solution.py:107
  51.4 9.9 %chunks.1 = (bf16[768,768]{1,0:T(8,128)(2,1)}, bf16[768,768]{1,0:T(8,128)(2,1)}, bf16[768,768]{1,0:T(8,128)(2,1)}, bf16[768,768]{1,0:T(8,128)(2,1)}) custom-call(s32[3]{0:T(128)S(1)} %pad_add_fusion.at_ref, bf16[384,3072]{1,0:T(8,128)(2,1)S(1)} %copy-done.4, bf16[384,3072]{1,0:T(8,128)(2,1)S(1)} %copy-done.2, bf16[384,768]{1,0:T(8,128)(2,1)S(1)} %bitcast.73, ...), custom_call_target="tpu_custom_call" | custom-call | flops 1811939328 | bytes 18874368 | tf_op jit(solution)/shard_map/chunks/pallas_call | solution.py:368
  61.3 1.4 collective-permute-start.5
  62.6 4.7 %collective-permute-start.6 = (bf16[768,768]{1,0:T(8,128)(2,1)}, bf16[768,768]{1,0:T(8,128)(2,1)}, u32[]{:S(2)}, u32[]{:S(2)}) collective-permute-start(bf16[768,768]{1,0:T(8,128)(2,1)} %get-tuple-element.39), channel_id=1, source_target_pairs={{0,4},{1,65},{2,6},{3,67},{4,0},{5,69},{6,2},{7,71},{8,12},{9,73},... | collective-permute-start | bytes 3538952 | tf_op jit(solution)/shard_map/ppermute | solution.py:58
  67.4 5.4 %fusion.19 = f32[384,768]{1,0:T(8,128)} fusion(bf16[384,3072]{1,0:T(8,128)(2,1)S(1)} %copy-done.2, bf16[768,3072]{1,0:T(8,128)(2,1)} %param.18), kind=kOutput, calls=%fused_computation.79 | convolution fusion | flops 1811939328 | bytes 8257536 | tf_op jit(solution)/shard_map/dot_general | solution.py:430
  76.7 9.1 %backward.1 = (f32[64,768]{1,0:T(8,128)S(1)}, bf16[16,24,768]{2,1,0:T(8,128)(2,1)S(1)}) custom-call(bf16[22,30,768]{2,1,0:T(8,128)(2,1)S(1)} %pad_maximum_fusion.pad_ref, f32[16,24,768]{2,1,0:T(8,128)S(1)} %copy-done.6, f32[16,24,768]{2,1,0:T(8,128)S(1)} %bitcast.69, f32[16,24,768]{2,1,0:T(8,128)S(1)} %bitcast.70, bf16[16,24,768]{2,1,0:T(8,128)(2,1)S(1)} %copy-done, ...), custom_call_target="tpu_custom_call" | custom-call | flops 28901376 | bytes 8388608 | tf_op jit(solution)/shard_map/backward/pallas_call | solution.py:223
  85.8 3.1 %collective-permute-start.8 = (f32[32,768]{1,0:T(8,128)S(1)}, f32[32,768]{1,0:T(8,128)S(1)}, u32[]{:S(2)}, u32[]{:S(2)}) collective-permute-start(f32[32,768]{1,0:T(8,128)S(1)} %slice_select_fusion.2), channel_id=1, source_target_pairs={{0,1},{1,0},{2,3},{3,2},{4,5},{5,4},{6,7},{7,6},{8,9},{9,8},{10,11... | collective-permute-start | bytes 294920 | tf_op jit(solution)/shard_map/ppermute | solution.py:107
  88.9 3.6 %collective-permute-start.10 = (bf16[16,3,768]{2,1,0:T(4,128)(2,1)S(1)}, bf16[16,3,768]{2,1,0:T(4,128)(2,1)S(1)}, u32[]{:S(2)}, u32[]{:S(2)}) collective-permute-start(bf16[16,3,768]{2,1,0:T(4,128)(2,1)S(1)} %get-tuple-element.77), channel_id=1, source_target_pairs={{0,1},{1,2},{2,3},{3,4},{4,5},{5,6},{6,7},{7,8},{8,9},{9,10},{10,1... | collective-permute-start | bytes 221192 | tf_op jit(solution)/shard_map/ppermute | solution.py:112
  92.6 1.9 %collective-permute-start.11 = (bf16[16,3,768]{2,1,0:T(4,128)(2,1)S(1)}, bf16[16,3,768]{2,1,0:T(4,128)(2,1)S(1)}, u32[]{:S(2)}, u32[]{:S(2)}) collective-permute-start(bf16[16,3,768]{2,1,0:T(4,128)(2,1)S(1)} %get-tuple-element.78), channel_id=1, source_target_pairs={{1,0},{2,1},{3,2},{4,3},{5,4},{6,5},{7,6},{8,7},{9,8},{10,9},{11,1... | collective-permute-start | bytes 221192 | tf_op jit(solution)/shard_map/ppermute | solution.py:112
  94.5 2.1 %collective-permute-start.9 = (bf16[32,768]{1,0:T(8,128)(2,1)S(1)}, bf16[32,768]{1,0:T(8,128)(2,1)S(1)}, u32[]{:S(2)}, u32[]{:S(2)}) collective-permute-start(bf16[32,768]{1,0:T(8,128)(2,1)S(1)} %add_convert_fusion.3), channel_id=1, source_target_pairs={{0,128},{128,0},{1,129},{129,1},{2,130},{130,2},{3,131},{131,3},{4... | collective-permute-start | bytes 147464 | tf_op jit(solution)/shard_map/ppermute | solution.py:103
  96.6 1.9 %collective-permute-done.11 = bf16[16,3,768]{2,1,0:T(4,128)(2,1)S(1)} collective-permute-done((bf16[16,3,768]{2,1,0:T(4,128)(2,1)S(1)}, bf16[16,3,768]{2,1,0:T(4,128)(2,1)S(1)}, u32[]{:S(2)}, u32[]{:S(2)}) %collective-permute-start.11) | collective-permute-done | bytes 73760 | tf_op jit(solution)/shard_map/ppermute | solution.py:112
  98.9 2.6 %add_convert_fusion = bf16[768,768]{1,0:T(8,128)(2,1)S(1)} fusion(bf16[768,768]{1,0:T(8,128)(2,1)} %collective-permute-done.7, bf16[768,768]{1,0:T(8,128)(2,1)} %collective-permute-done.6, bf16[768,768]{1,0:T(8,128)(2,1)} %collective-permute-done.5, bf16[768,768]{1,0:T(8,128)(2,1)S(1)} %copy-done.10), kind=kLoop, calls=%fused_computation.12 | loop fusion | flops 4718592 | bytes 5898240 | tf_op jit(solution)/shard_map/convert_element_type | solution.py:459
  103.0 12.4 %collective-permute-start.13 = (bf16[224,768]{1,0:T(8,128)(2,1)}, bf16[224,768]{1,0:T(8,128)(2,1)}, u32[]{:S(2)}, u32[]{:S(2)}) collective-permute-start(bf16[224,768]{1,0:T(8,128)(2,1)} %get-tuple-element.95), channel_id=1, source_target_pairs={{0,64},{1,5},{2,66},{3,7},{4,68},{5,1},{6,70},{7,3},{8,72},{9,13},... | collective-permute-start | bytes 1032200 | tf_op jit(solution)/shard_map/ppermute | solution.py:58
  115.5 3.1 %collective-permute-start.15 = (bf16[3,30,768]{2,1,0:T(8,128)(2,1)S(1)}, bf16[3,30,768]{2,1,0:T(8,128)(2,1)S(1)}, u32[]{:S(2)}, u32[]{:S(2)}) collective-permute-start(bf16[3,30,768]{2,1,0:T(8,128)(2,1)S(1)} %get-tuple-element.73), channel_id=1, source_target_pairs={{0,32},{32,64},{64,96},{96,128},{128,160},{160,192},{192,224},{1,3... | collective-permute-start | bytes 414728 | tf_op jit(solution)/shard_map/ppermute | solution.py:112
  120.6 3.9 %collective-permute-done.16 = bf16[3,30,768]{2,1,0:T(8,128)(2,1)} collective-permute-done((bf16[3,30,768]{2,1,0:T(8,128)(2,1)S(1)}, bf16[3,30,768]{2,1,0:T(8,128)(2,1)}, u32[]{:S(2)}, u32[]{:S(2)}) %collective-permute-start.16) | collective-permute-done | bytes 138272 | tf_op jit(solution)/shard_map/ppermute | solution.py:112
  124.5 1.3 pad_maximum_fusion.1.pad_ref
  126.8 1.3 add_convert_fusion.1
  129.2 3.6 %collective-permute-start.18 = (bf16[32,768]{1,0:T(8,128)(2,1)S(1)}, bf16[32,768]{1,0:T(8,128)(2,1)S(1)}, u32[]{:S(2)}, u32[]{:S(2)}) collective-permute-start(bf16[32,768]{1,0:T(8,128)(2,1)S(1)} %convert_add_fusion.2), channel_id=1, source_target_pairs={{0,4},{1,65},{2,6},{3,67},{4,0},{5,69},{6,2},{7,71},{8,12},{9,73},... | collective-permute-start | bytes 147464 | tf_op jit(solution)/shard_map/ppermute | solution.py:58
  133.1 1.7 %collective-permute-done.18 = bf16[32,768]{1,0:T(8,128)(2,1)S(1)} collective-permute-done((bf16[32,768]{1,0:T(8,128)(2,1)S(1)}, bf16[32,768]{1,0:T(8,128)(2,1)S(1)}, u32[]{:S(2)}, u32[]{:S(2)}) %collective-permute-start.18) | collective-permute-done | bytes 49184 | tf_op jit(solution)/shard_map/ppermute | solution.py:58
  137.0 3.9 %collective-permute-start.21 = (bf16[56,768]{1,0:T(8,128)(2,1)S(1)}, bf16[56,768]{1,0:T(8,128)(2,1)S(1)}, u32[]{:S(2)}, u32[]{:S(2)}) collective-permute-start(bf16[56,768]{1,0:T(8,128)(2,1)S(1)} %get-tuple-element.92), channel_id=1, source_target_pairs={{0,8},{8,16},{16,24},{24,0},{1,9},{9,17},{17,25},{25,1},{2,10},{10... | collective-permute-start | bytes 258056 | tf_op jit(solution)/shard_map/ppermute | solution.py:95
  141.0 3.6 %collective-permute-start.23 = (bf16[56,768]{1,0:T(8,128)(2,1)S(1)}, bf16[56,768]{1,0:T(8,128)(2,1)S(1)}, u32[]{:S(2)}, u32[]{:S(2)}) collective-permute-start(bf16[56,768]{1,0:T(8,128)(2,1)S(1)} %get-tuple-element.90), channel_id=1, source_target_pairs={{0,24},{8,0},{16,8},{24,16},{1,25},{9,1},{17,9},{25,17},{2,26},{10... | collective-permute-start | bytes 258056 | tf_op jit(solution)/shard_map/ppermute | solution.py:95
  144.6 6.3 %conv_image.1 = f32[16,24,768]{2,1,0:T(8,128)} custom-call(bf16[22,30,768]{2,1,0:T(8,128)(2,1)S(1)} %pad_maximum_fusion.1.pad_ref, f32[49,768]{1,0:T(8,128)S(1)} %reshape.97.w_ref, bf16[16,24,768]{2,1,0:T(8,128)(2,1)S(1)} %copy-done), custom_call_target="tpu_custom_call" | custom-call | flops 28901376 | bytes 16777216 | tf_op jit(solution)/shard_map/conv_image/pallas_call | solution.py:302
  151.0 4.6 %collective-permute-start.24 = (f32[44,768]{1,0:T(8,128)S(1)}, f32[44,768]{1,0:T(8,128)S(1)}, u32[]{:S(2)}, u32[]{:S(2)}) collective-permute-start(f32[44,768]{1,0:T(8,128)S(1)} %pad_maximum_fusion.10), channel_id=1, source_target_pairs={{0,1},{1,0},{2,3},{3,2},{4,5},{5,4},{6,7},{7,6},{8,9},{9,8},{10,11... | collective-permute-start | bytes 405512 | tf_op jit(solution)/shard_map/ppermute | solution.py:107
  (107 shorter events, 26.4 us)
Async XLA Ops:
  0.6 22.1 %copy-start.9 = (bf16[16,24,768]{2,1,0:T(8,128)(2,1)S(1)}, bf16[16,24,768]{2,1,0:T(8,128)(2,1)}, u32[]{:S(2)}) copy-start(bf16[16,24,768]{2,1,0:T(8,128)(2,1)} %param.11) | copy-start | bytes 1769476
  1.8 9.5 %collective-permute-start = (bf16[16,3,768]{2,1,0:T(4,128)(2,1)S(1)}, bf16[16,3,768]{2,1,0:T(4,128)(2,1)S(1)}, u32[]{:S(2)}, u32[]{:S(2)}) collective-permute-start(bf16[16,3,768]{2,1,0:T(4,128)(2,1)S(1)} %get-tuple-element.79), channel_id=1, source_target_pairs={{0,1},{1,2},{2,3},{3,4},{4,5},{5,6},{6,7},{7,8},{8,9},{9,10},{10,1... | collective-permute-start | bytes 221192 | tf_op jit(solution)/shard_map/ppermute | solution.py:112
  6.3 5.9 %collective-permute-start.1 = (bf16[16,3,768]{2,1,0:T(4,128)(2,1)S(1)}, bf16[16,3,768]{2,1,0:T(4,128)(2,1)S(1)}, u32[]{:S(2)}, u32[]{:S(2)}) collective-permute-start(bf16[16,3,768]{2,1,0:T(4,128)(2,1)S(1)} %get-tuple-element.80), channel_id=1, source_target_pairs={{1,0},{2,1},{3,2},{4,3},{5,4},{6,5},{7,6},{8,7},{9,8},{10,9},{11,1... | collective-permute-start | bytes 221192 | tf_op jit(solution)/shard_map/ppermute | solution.py:112
  12.3 19.9 %copy-start.13 = (bf16[3072,768]{1,0:T(8,128)(2,1)S(1)}, bf16[3072,768]{1,0:T(8,128)(2,1)}, u32[]{:S(2)}) copy-start(bf16[3072,768]{1,0:T(8,128)(2,1)} %param.16) | copy-start | bytes 14155780
  13.5 18.7 %copy-start.14 = (f32[3072]{0:T(1024)S(1)}, f32[3072]{0:T(1024)}, u32[]{:S(2)}) copy-start(f32[3072]{0:T(1024)} %param.17) | copy-start | bytes 36868
  13.5 5.8 %collective-permute-start.2 = (bf16[3,30,768]{2,1,0:T(8,128)(2,1)S(1)}, bf16[3,30,768]{2,1,0:T(8,128)(2,1)S(1)}, u32[]{:S(2)}, u32[]{:S(2)}) collective-permute-start(bf16[3,30,768]{2,1,0:T(8,128)(2,1)S(1)} %get-tuple-element.75), channel_id=1, source_target_pairs={{0,32},{32,64},{64,96},{96,128},{128,160},{160,192},{192,224},{1,3... | collective-permute-start | bytes 414728 | tf_op jit(solution)/shard_map/ppermute | solution.py:112
  16.8 5.9 %collective-permute-start.3 = (bf16[3,30,768]{2,1,0:T(8,128)(2,1)S(1)}, bf16[3,30,768]{2,1,0:T(8,128)(2,1)S(1)}, u32[]{:S(2)}, u32[]{:S(2)}) collective-permute-start(bf16[3,30,768]{2,1,0:T(8,128)(2,1)S(1)} %get-tuple-element.76), channel_id=1, source_target_pairs={{32,0},{64,32},{96,64},{128,96},{160,128},{192,160},{224,192},{33,... | collective-permute-start | bytes 414728 | tf_op jit(solution)/shard_map/ppermute | solution.py:112
  23.1 11.8 %slice-start = ((s8[4718592]{0:T(1024)(128)(4,1)}), s8[4194304]{0:T(1024)(128)(4,1)S(1)}, s32[]{:S(2)}) async-start(s8[4718592]{0:T(1024)(128)(4,1)} %bitcast.80), calls=%async_computation | async-start | bytes 8388608
  43.1 8.3 %collective-permute-start.4 = (bf16[3072,768]{1,0:T(8,128)(2,1)}, bf16[3072,768]{1,0:T(8,128)(2,1)}, u32[]{:S(2)}, u32[]{:S(2)}) collective-permute-start(bf16[3072,768]{1,0:T(8,128)(2,1)} %convolution_convert_fusion), channel_id=1, source_target_pairs={{0,1},{1,0},{2,3},{3,2},{4,5},{5,4},{6,7},{7,6},{8,9},{9,8},{10,11... | collective-permute-start | bytes 14155784 | tf_op jit(solution)/shard_map/ppermute | solution.py:107
  43.4 8.0 %copy-start.2 = (bf16[384,3072]{1,0:T(8,128)(2,1)S(1)}, bf16[384,3072]{1,0:T(8,128)(2,1)}, u32[]{:S(2)}) copy-start(bf16[384,3072]{1,0:T(8,128)(2,1)} %copy-done.1) | copy-start | bytes 7077892
  43.4 8.0 %copy-start.4 = (bf16[384,3072]{1,0:T(8,128)(2,1)S(1)}, bf16[384,3072]{1,0:T(8,128)(2,1)}, u32[]{:S(2)}) copy-start(bf16[384,3072]{1,0:T(8,128)(2,1)} %copy-done.3) | copy-start | bytes 7077892
  61.3 37.6 %collective-permute-start.5 = (bf16[768,768]{1,0:T(8,128)(2,1)}, bf16[768,768]{1,0:T(8,128)(2,1)}, u32[]{:S(2)}, u32[]{:S(2)}) collective-permute-start(bf16[768,768]{1,0:T(8,128)(2,1)} %get-tuple-element.38), channel_id=1, source_target_pairs={{0,2},{1,33},{2,4},{3,35},{4,6},{5,37},{6,0},{7,39},{8,10},{9,41},... | collective-permute-start | bytes 3538952 | tf_op jit(solution)/shard_map/ppermute | solution.py:58
  62.6 36.3 %collective-permute-start.6 = (bf16[768,768]{1,0:T(8,128)(2,1)}, bf16[768,768]{1,0:T(8,128)(2,1)}, u32[]{:S(2)}, u32[]{:S(2)}) collective-permute-start(bf16[768,768]{1,0:T(8,128)(2,1)} %get-tuple-element.39), channel_id=1, source_target_pairs={{0,4},{1,65},{2,6},{3,67},{4,0},{5,69},{6,2},{7,71},{8,12},{9,73},... | collective-permute-start | bytes 3538952 | tf_op jit(solution)/shard_map/ppermute | solution.py:58
  67.4 31.5 %collective-permute-start.7 = (bf16[768,768]{1,0:T(8,128)(2,1)}, bf16[768,768]{1,0:T(8,128)(2,1)}, u32[]{:S(2)}, u32[]{:S(2)}) collective-permute-start(bf16[768,768]{1,0:T(8,128)(2,1)} %get-tuple-element.40), channel_id=1, source_target_pairs={{0,6},{1,97},{2,0},{3,99},{4,2},{5,101},{6,4},{7,103},{8,14},{9,10... | collective-permute-start | bytes 3538952 | tf_op jit(solution)/shard_map/ppermute | solution.py:58
  85.7 13.2 %copy-start.10 = (bf16[768,768]{1,0:T(8,128)(2,1)S(1)}, bf16[768,768]{1,0:T(8,128)(2,1)}, u32[]{:S(2)}) copy-start(bf16[768,768]{1,0:T(8,128)(2,1)} %get-tuple-element.37) | copy-start | bytes 3538948
  85.8 6.8 %collective-permute-start.8 = (f32[32,768]{1,0:T(8,128)S(1)}, f32[32,768]{1,0:T(8,128)S(1)}, u32[]{:S(2)}, u32[]{:S(2)}) collective-permute-start(f32[32,768]{1,0:T(8,128)S(1)} %slice_select_fusion.2), channel_id=1, source_target_pairs={{0,1},{1,0},{2,3},{3,2},{4,5},{5,4},{6,7},{7,6},{8,9},{9,8},{10,11... | collective-permute-start | bytes 294920 | tf_op jit(solution)/shard_map/ppermute | solution.py:107
  88.9 5.6 %collective-permute-start.10 = (bf16[16,3,768]{2,1,0:T(4,128)(2,1)S(1)}, bf16[16,3,768]{2,1,0:T(4,128)(2,1)S(1)}, u32[]{:S(2)}, u32[]{:S(2)}) collective-permute-start(bf16[16,3,768]{2,1,0:T(4,128)(2,1)S(1)} %get-tuple-element.77), channel_id=1, source_target_pairs={{0,1},{1,2},{2,3},{3,4},{4,5},{5,6},{6,7},{7,8},{8,9},{9,10},{10,1... | collective-permute-start | bytes 221192 | tf_op jit(solution)/shard_map/ppermute | solution.py:112
  92.6 5.9 %collective-permute-start.11 = (bf16[16,3,768]{2,1,0:T(4,128)(2,1)S(1)}, bf16[16,3,768]{2,1,0:T(4,128)(2,1)S(1)}, u32[]{:S(2)}, u32[]{:S(2)}) collective-permute-start(bf16[16,3,768]{2,1,0:T(4,128)(2,1)S(1)} %get-tuple-element.78), channel_id=1, source_target_pairs={{1,0},{2,1},{3,2},{4,3},{5,4},{6,5},{7,6},{8,7},{9,8},{10,9},{11,1... | collective-permute-start | bytes 221192 | tf_op jit(solution)/shard_map/ppermute | solution.py:112
  94.5 4.3 %collective-permute-start.9 = (bf16[32,768]{1,0:T(8,128)(2,1)S(1)}, bf16[32,768]{1,0:T(8,128)(2,1)S(1)}, u32[]{:S(2)}, u32[]{:S(2)}) collective-permute-start(bf16[32,768]{1,0:T(8,128)(2,1)S(1)} %add_convert_fusion.3), channel_id=1, source_target_pairs={{0,128},{128,0},{1,129},{129,1},{2,130},{130,2},{3,131},{131,3},{4... | collective-permute-start | bytes 147464 | tf_op jit(solution)/shard_map/ppermute | solution.py:103
  103.0 22.9 %collective-permute-start.12 = (bf16[224,768]{1,0:T(8,128)(2,1)}, bf16[224,768]{1,0:T(8,128)(2,1)}, u32[]{:S(2)}, u32[]{:S(2)}) collective-permute-start(bf16[224,768]{1,0:T(8,128)(2,1)} %get-tuple-element.94), channel_id=1, source_target_pairs={{0,32},{1,3},{2,34},{3,5},{4,36},{5,7},{6,38},{7,1},{8,40},{9,11},... | collective-permute-start | bytes 1032200 | tf_op jit(solution)/shard_map/ppermute | solution.py:58
  103.0 22.9 %collective-permute-start.13 = (bf16[224,768]{1,0:T(8,128)(2,1)}, bf16[224,768]{1,0:T(8,128)(2,1)}, u32[]{:S(2)}, u32[]{:S(2)}) collective-permute-start(bf16[224,768]{1,0:T(8,128)(2,1)} %get-tuple-element.95), channel_id=1, source_target_pairs={{0,64},{1,5},{2,66},{3,7},{4,68},{5,1},{6,70},{7,3},{8,72},{9,13},... | collective-permute-start | bytes 1032200 | tf_op jit(solution)/shard_map/ppermute | solution.py:58
  115.4 10.4 %collective-permute-start.14 = (bf16[224,768]{1,0:T(8,128)(2,1)}, bf16[224,768]{1,0:T(8,128)(2,1)}, u32[]{:S(2)}, u32[]{:S(2)}) collective-permute-start(bf16[224,768]{1,0:T(8,128)(2,1)} %get-tuple-element.93), channel_id=1, source_target_pairs={{0,96},{1,7},{2,98},{3,1},{4,100},{5,3},{6,102},{7,5},{8,104},{9,1... | collective-permute-start | bytes 1032200 | tf_op jit(solution)/shard_map/ppermute | solution.py:58
  115.5 5.2 %collective-permute-start.15 = (bf16[3,30,768]{2,1,0:T(8,128)(2,1)S(1)}, bf16[3,30,768]{2,1,0:T(8,128)(2,1)S(1)}, u32[]{:S(2)}, u32[]{:S(2)}) collective-permute-start(bf16[3,30,768]{2,1,0:T(8,128)(2,1)S(1)} %get-tuple-element.73), channel_id=1, source_target_pairs={{0,32},{32,64},{64,96},{96,128},{128,160},{160,192},{192,224},{1,3... | collective-permute-start | bytes 414728 | tf_op jit(solution)/shard_map/ppermute | solution.py:112
  118.6 6.0 %collective-permute-start.16 = (bf16[3,30,768]{2,1,0:T(8,128)(2,1)S(1)}, bf16[3,30,768]{2,1,0:T(8,128)(2,1)}, u32[]{:S(2)}, u32[]{:S(2)}) collective-permute-start(bf16[3,30,768]{2,1,0:T(8,128)(2,1)S(1)} %get-tuple-element.74), channel_id=1, source_target_pairs={{32,0},{64,32},{96,64},{128,96},{160,128},{192,160},{224,192},{33,... | collective-permute-start | bytes 414728 | tf_op jit(solution)/shard_map/ppermute | solution.py:112
  128.1 5.0 %collective-permute-start.17 = (bf16[32,768]{1,0:T(8,128)(2,1)S(1)}, bf16[32,768]{1,0:T(8,128)(2,1)S(1)}, u32[]{:S(2)}, u32[]{:S(2)}) collective-permute-start(bf16[32,768]{1,0:T(8,128)(2,1)S(1)} %convert_add_fusion.2), channel_id=1, source_target_pairs={{0,2},{1,33},{2,4},{3,35},{4,6},{5,37},{6,0},{7,39},{8,10},{9,41},... | collective-permute-start | bytes 147464 | tf_op jit(solution)/shard_map/ppermute | solution.py:58
  129.2 5.6 %collective-permute-start.18 = (bf16[32,768]{1,0:T(8,128)(2,1)S(1)}, bf16[32,768]{1,0:T(8,128)(2,1)S(1)}, u32[]{:S(2)}, u32[]{:S(2)}) collective-permute-start(bf16[32,768]{1,0:T(8,128)(2,1)S(1)} %convert_add_fusion.2), channel_id=1, source_target_pairs={{0,4},{1,65},{2,6},{3,67},{4,0},{5,69},{6,2},{7,71},{8,12},{9,73},... | collective-permute-start | bytes 147464 | tf_op jit(solution)/shard_map/ppermute | solution.py:58
  132.8 2.9 %collective-permute-start.19 = (bf16[32,768]{1,0:T(8,128)(2,1)S(1)}, bf16[32,768]{1,0:T(8,128)(2,1)S(1)}, u32[]{:S(2)}, u32[]{:S(2)}) collective-permute-start(bf16[32,768]{1,0:T(8,128)(2,1)S(1)} %convert_add_fusion.2), channel_id=1, source_target_pairs={{0,6},{1,97},{2,0},{3,99},{4,2},{5,101},{6,4},{7,103},{8,14},{9,10... | collective-permute-start | bytes 147464 | tf_op jit(solution)/shard_map/ppermute | solution.py:58
  132.8 4.1 %collective-permute-start.20 = (bf16[96,768]{1,0:T(8,128)(2,1)S(1)}, bf16[96,768]{1,0:T(8,128)(2,1)S(1)}, u32[]{:S(2)}, u32[]{:S(2)}) collective-permute-start(bf16[96,768]{1,0:T(8,128)(2,1)S(1)} %bitcast.79), channel_id=1, source_target_pairs={{0,128},{128,0},{1,129},{129,1},{2,130},{130,2},{3,131},{131,3},{4... | collective-permute-start | bytes 442376 | tf_op jit(solution)/shard_map/ppermute | solution.py:103
  137.0 13.9 %collective-permute-start.21 = (bf16[56,768]{1,0:T(8,128)(2,1)S(1)}, bf16[56,768]{1,0:T(8,128)(2,1)S(1)}, u32[]{:S(2)}, u32[]{:S(2)}) collective-permute-start(bf16[56,768]{1,0:T(8,128)(2,1)S(1)} %get-tuple-element.92), channel_id=1, source_target_pairs={{0,8},{8,16},{16,24},{24,0},{1,9},{9,17},{17,25},{25,1},{2,10},{10... | collective-permute-start | bytes 258056 | tf_op jit(solution)/shard_map/ppermute | solution.py:95
  141.0 9.9 %collective-permute-start.22 = (bf16[56,768]{1,0:T(8,128)(2,1)S(1)}, bf16[56,768]{1,0:T(8,128)(2,1)S(1)}, u32[]{:S(2)}, u32[]{:S(2)}) collective-permute-start(bf16[56,768]{1,0:T(8,128)(2,1)S(1)} %get-tuple-element.91), channel_id=1, source_target_pairs={{0,16},{8,24},{16,0},{24,8},{1,17},{9,25},{17,1},{25,9},{2,18},{10... | collective-permute-start | bytes 258056 | tf_op jit(solution)/shard_map/ppermute | solution.py:95
  141.0 9.9 %collective-permute-start.23 = (bf16[56,768]{1,0:T(8,128)(2,1)S(1)}, bf16[56,768]{1,0:T(8,128)(2,1)S(1)}, u32[]{:S(2)}, u32[]{:S(2)}) collective-permute-start(bf16[56,768]{1,0:T(8,128)(2,1)S(1)} %get-tuple-element.90), channel_id=1, source_target_pairs={{0,24},{8,0},{16,8},{24,16},{1,25},{9,1},{17,9},{25,17},{2,26},{10... | collective-permute-start | bytes 258056 | tf_op jit(solution)/shard_map/ppermute | solution.py:95
  151.0 5.6 %collective-permute-start.24 = (f32[44,768]{1,0:T(8,128)S(1)}, f32[44,768]{1,0:T(8,128)S(1)}, u32[]{:S(2)}, u32[]{:S(2)}) collective-permute-start(f32[44,768]{1,0:T(8,128)S(1)} %pad_maximum_fusion.10), channel_id=1, source_target_pairs={{0,1},{1,0},{2,3},{3,2},{4,5},{5,4},{6,7},{7,6},{8,9},{9,8},{10,11... | collective-permute-start | bytes 405512 | tf_op jit(solution)/shard_map/ppermute | solution.py:107
  (10 other events, 30.3 us)
